TPU v7x, 256 devices: a whole 4x4x8 slice. The times are simulated.
256 devices in a mesh: pool: 16 (over z_hi, y), mp: 16 (over z_lo, x, core).
Axes of the slice: x: 4, y: 4, z: 8 (z_hi: 4, z_lo: 2; z = z_hi * 2 + z_lo), core: 2. Of those that a mesh axis runs over, the one named last changes fastest.
Arguments:
- stored_hidden: bfloat16 [8192, 8192], P('pool', 'mp')
- block_owner: int32 [128], P('pool'), may hold values from 0 to 15, as said below
- block_valid: int32 [128], P('pool'), may hold values from 1 to 64, as said below
- block_start: int32 [128], P('pool'), may hold values from 0 to 16320
- turn_hidden: bfloat16 [8192, 8192], P('pool', 'mp')
- turn_position: int32 [8192], P('pool'), may hold values from 0 to 16895
- kv_weight: bfloat16 [8192, 2048], P(None, 'mp'), may hold values from -0.0625 to 0.0625
- kv_bias: float32 [2048], P('mp'), may hold values from -3 to 3
Outputs:
- restored_cache: bfloat16 [16384, 2048], P('pool', 'mp')
- turn_kv: bfloat16 [8192, 2048], P('pool', 'mp')
Inputs may be any that keep to these rules, and one draw needn't show every extreme that they name: `block_owner`: the 8 blocks of one storage shard (blocks s * 8 to s * 8 + 7) have distinct owners; in every draw one owner has a block from every storage shard. `block_valid`: every storage shard has a full block.
All inputs are finite; a program needn't handle non-finite values.
Results may differ from a plain program's by a relative error of at most 0.0012.
Values may be sent and summed in bfloat16 or wider, within the bound.
No kernel may reach another device: no remote copies, remote signals or barrier semaphores. Data moves between devices by JAX's collectives and lax.ppermute only.
A program may use at most 128 MiB of HBM per device.

v0:
```python
import jax
import jax.numpy as jnp
from jax import lax
from jax.sharding import PartitionSpec as P

D = 8192
HD = 128
BLK = 64
KVD = 1024


def fold_with(weight, piece):
    total = jnp.dot(piece, weight, preferred_element_type=jnp.float32)
    squares = jnp.sum(jnp.square(piece.astype(jnp.float32)), axis=1)
    return (total, squares)


def finish(total, squares, kv_bias):
    scale = lax.rsqrt(squares / D + 1e-06)
    return total * scale[:, None] + kv_bias[None, :]


def project_stored(rows, kv_weight, kv_bias):
    total, squares = fold_with(kv_weight, lax.all_gather(rows, "mp", axis=1, tiled=True))
    return finish(total, squares, kv_bias)


def project_turn(rows, kv_weight, kv_bias):
    total, squares = fold_with(kv_weight, lax.all_gather(rows, "mp", axis=1, tiled=True))
    return finish(total, squares, kv_bias)


def rotate(values, positions, offset):
    count = values.shape[0]
    heads = values.shape[1] // HD
    shaped = values.reshape(count, heads, HD)
    half = HD // 2
    freq = jnp.exp(
        -jnp.log(jnp.float32(1000000.0)) * (jnp.arange(half).astype(jnp.float32) * 2.0 / HD)
    )
    angle = positions.astype(jnp.float32)[:, None] * freq[None, :]
    cosine = jnp.cos(angle)[:, None, :]
    sine = jnp.sin(angle)[:, None, :]
    first = shaped[:, :, :half]
    second = shaped[:, :, half:]
    turned = jnp.concatenate(
        [first * cosine - second * sine, second * cosine + first * sine], axis=2
    )
    is_key = offset + jnp.arange(heads) * HD < KVD
    return jnp.where(is_key[None, :, None], turned, shaped).reshape(count, heads * HD)


def shards(
    stored_hidden,
    block_owner,
    block_valid,
    block_start,
    turn_hidden,
    turn_position,
    kv_weight,
    kv_bias,
):
    groups = lax.axis_size("pool")
    columns = kv_weight.shape[1]
    offset = lax.axis_index("mp") * columns
    local_feat = stored_hidden.shape[1]
    blocks_here = block_owner.shape[0]
    offsets = jnp.arange(BLK)
    picks = (block_owner[:, None] == jnp.arange(groups)[None, :]).astype(jnp.int32)
    blocks = stored_hidden.reshape(blocks_here, BLK, local_feat)
    outgoing = jnp.einsum(
        "bg,brd->grd", picks.astype(jnp.bfloat16), blocks, preferred_element_type=jnp.float32
    ).astype(jnp.bfloat16)
    facts = jnp.stack([block_valid, block_start], axis=1)
    out_facts = jnp.sum(picks[:, :, None] * facts[:, None, :], axis=0)
    arrived, arrived_facts = (
        lax.all_to_all(outgoing, "pool", split_axis=0, concat_axis=0, tiled=True),
        lax.all_to_all(out_facts, "pool", split_axis=0, concat_axis=0, tiled=True),
    )
    rows = arrived.reshape(groups * BLK, local_feat)
    pre = project_stored(rows, kv_weight, kv_bias)
    positions = (arrived_facts[:, 1][:, None] + offsets[None, :]).reshape(groups * BLK)
    roped = rotate(pre, positions, offset)
    keep = (offsets[None, :] < arrived_facts[:, 0][:, None]).reshape(groups * BLK, 1)
    restored_cache = jnp.where(keep, roped, 0.0).astype(jnp.bfloat16)
    turn_pre = project_turn(turn_hidden, kv_weight, kv_bias)
    turn_kv = rotate(turn_pre, turn_position, offset).astype(jnp.bfloat16)
    return (restored_cache, turn_kv)


def solution(mesh):
    placed = (
        P("pool", "mp"),
        P("pool"),
        P("pool"),
        P("pool"),
        P("pool", "mp"),
        P("pool"),
        P(None, "mp"),
        P("mp"),
    )
    return jax.shard_map(
        shards,
        mesh=mesh,
        in_specs=placed,
        out_specs=(P("pool", "mp"), P("pool", "mp")),
        check_vma=False,
    )
```

profile of v0, /device:TPU:1, one launch (start us, length us, event | category | flops | bytes accessed | tf_op | source)
XLA Modules:
  0.0 211.7 jit_solution(3641940313410480881)
XLA Ops:
  7.2 0.0 copy-start
  7.2 0.0 copy-start.2
  7.2 0.0 all-gather.5.cloned.1.call-start
  7.2 0.7 all-gather.5.cloned.1.call-update
  7.9 0.0 all-gather.3.cloned.1.call-start
  8.0 1.6 convolution_convert_fusion
  9.6 0.6 copy.29
  10.2 46.5 %all_to_all.17 = bf16[16,64,512]{2,1,0:T(8,128)(2,1)} all-to-all(bf16[16,64,512]{2,1,0:T(8,128)(2,1)S(1)} %copy.29), channel_id=1, replica_groups=mesh['pool'=16,'mp'=16] {'pool'}, dimensions={0} | all-to-all | bytes 2097152 | tf_op jit(solution)/shard_map/all_to_all | solution.py:77
  56.7 0.0 all-gather.3.cloned.1.call-update
  56.7 0.7 pad_add_fusion
  57.4 0.7 fusion.22
  58.1 0.1 multiply_reduce_fusion.2
  58.2 0.7 copy.26
  58.9 5.8 %all-to-all-start = ((s32[16,1,2]{2,1,0:T(1,128)}), s32[16,1,2]{2,1,0:T(1,128)S(1)}, u32[]{:S(2)}, u32[]{:S(2)}) async-start(s32[16,1,2]{2,1,0:T(1,128)} %copy.26), calls=%async_computation | async-start | bytes 16384 | tf_op jit(solution)/shard_map/all_to_all | solution.py:78
  64.7 0.7 convert_element_type.57
  65.3 8.0 %all-to-all-done = s32[16,1,2]{2,1,0:T(1,128)S(1)} async-done(((s32[16,1,2]{2,1,0:T(1,128)}), s32[16,1,2]{2,1,0:T(1,128)S(1)}, u32[]{:S(2)}, u32[]{:S(2)}) %all-to-all-start) | async-done | bytes 160 | tf_op jit(solution)/shard_map/all_to_all | solution.py:78
  73.4 0.1 copy.27
  73.5 0.1 add_convert_fusion
  73.6 0.1 convert_element_type.53
  73.6 0.1 iota_compare_fusion
  73.7 0.1 lt.33
  73.8 13.9 %all-gather.5.cloned.1.call-done = bf16[512,8192]{1,0:T(8,128)(2,1)} async-done(((bf16[512,512]{1,0:T(8,128)(2,1)}), bf16[512,8192]{1,0:T(8,128)(2,1)}) %all-gather.5.cloned.1.call-update) | async-done | bytes 8388624 | tf_op jit(solution)/shard_map/all_gather | solution.py:29
  87.7 0.0 copy-start.1
  87.7 5.3 %multiply_reduce_fusion.1 = f32[512]{0:T(512)S(1)} fusion(bf16[512,8192]{1,0:T(8,128)(2,1)} %all-gather.5.cloned.1.call-done), kind=kLoop, calls=%fused_computation.1 | loop fusion | flops 12582400 | bytes 8390656 | tf_op jit(solution)/shard_map/reduce_sum | solution.py:14
  93.0 0.0 copy-done
  93.0 0.0 copy-done.2
  93.0 0.5 copy-done.1
  93.5 2.9 %fusion.1 = f32[512,128]{0,1:T(8,128)S(1)} fusion(bf16[512,8192]{1,0:T(8,128)(2,1)S(1)} %copy-done.1, bf16[8192,128]{1,0:T(8,128)(2,1)S(1)} %copy-done, f32[128]{0:T(128)S(1)} %copy-done.2, f32[512]{0:T(512)S(1)} %add_rsqrt_fusion.1), kind=kOutput, calls=%fused_computation.6 | convolution fusion | flops 1073872896 | bytes 10750464 | tf_op jit(solution)/shard_map/dot_general | solution.py:13
  96.4 0.6 fusion.19
  97.0 0.8 copy.31
  97.8 86.3 %all-gather.3.cloned.1.call-done = bf16[1024,8192]{1,0:T(8,128)(2,1)} async-done(((bf16[1024,512]{1,0:T(8,128)(2,1)}), bf16[1024,8192]{1,0:T(8,128)(2,1)}) %all-gather.3.cloned.1.call-update) | async-done | bytes 16777232 | tf_op jit(solution)/shard_map/all_gather | solution.py:24
  184.1 7.2 %multiply_reduce_fusion = f32[1024]{0:T(1024)S(1)} fusion(bf16[1024,8192]{1,0:T(8,128)(2,1)} %all-gather.3.cloned.1.call-done), kind=kLoop, calls=%fused_computation | loop fusion | flops 25164800 | bytes 16781312 | tf_op jit(solution)/shard_map/reduce_sum | solution.py:14
  191.3 11.4 %fusion = f32[1024,128]{0,1:T(8,128)S(1)} fusion(bf16[1024,8192]{1,0:T(8,128)(2,1)} %all-gather.3.cloned.1.call-done, bf16[8192,128]{1,0:T(8,128)(2,1)S(1)} %copy-done, f32[128]{0:T(128)S(1)} %copy-done.2, f32[1024]{0:T(1024)S(1)} %add_rsqrt_fusion), kind=kOutput, calls=%fused_computation.4 | convolution fusion | flops 2147745792 | bytes 19403264 | tf_op jit(solution)/shard_map/dot_general | solution.py:13
  202.7 1.2 fusion.10
  203.9 0.1 fusion.3
  204.0 0.8 copy.30
  (5 shorter events, 0.1 us)
Async XLA Ops:
  7.2 85.8 %copy-start = (bf16[8192,128]{1,0:T(8,128)(2,1)S(1)}, bf16[8192,128]{1,0:T(8,128)(2,1)}, u32[]{:S(2)}) copy-start(bf16[8192,128]{1,0:T(8,128)(2,1)} %param.14) | copy-start | bytes 6291460
  7.2 85.8 %copy-start.2 = (f32[128]{0:T(128)S(1)}, f32[128]{0:T(128)}, u32[]{:S(2)}) copy-start(f32[128]{0:T(128)} %param.15) | copy-start | bytes 1540
  7.2 80.5 %all-gather.5.cloned.1.call-start = ((), (), s32[]{:S(2)}) async-start(), calls=%async_computation.3 | async-start | bytes 8912896 | tf_op jit(solution)/shard_map/all_gather | solution.py:29
  7.9 176.2 %all-gather.3.cloned.1.call-start = ((), (), s32[]{:S(2)}) async-start(), calls=%async_computation.2 | async-start | bytes 17825792 | tf_op jit(solution)/shard_map/all_gather | solution.py:24
  58.9 14.5 %all-to-all-start = ((s32[16,1,2]{2,1,0:T(1,128)}), s32[16,1,2]{2,1,0:T(1,128)S(1)}, u32[]{:S(2)}, u32[]{:S(2)}) async-start(s32[16,1,2]{2,1,0:T(1,128)} %copy.26), calls=%async_computation | async-start | bytes 16384 | tf_op jit(solution)/shard_map/all_to_all | solution.py:78
  87.7 5.8 %copy-start.1 = (bf16[512,8192]{1,0:T(8,128)(2,1)S(1)}, bf16[512,8192]{1,0:T(8,128)(2,1)}, u32[]{:S(2)}) copy-start(bf16[512,8192]{1,0:T(8,128)(2,1)} %all-gather.5.cloned.1.call-done) | copy-start | bytes 25165828
Sparse Core Ops, SparseCore 0:
  9.8 77.8 all-gather.4
  89.5 94.5 all-gather.2
where the time goes:
time: 212 us
  waiting for transfers between devices  109 us (51%)
  blocking collectives  46.5 us (22%)
  other arithmetic  16.6 us (8%)
  matrix products  16 us (8%)
  between operations  14.2 us (7%)
  starting transfers between devices  5.84 us (3%)
  local copies, waits for them, and re-layouts  3.62 us (2%)
    all_gather x1, waiting for transfers between devices, project_stored(): lax.all_gather(rows, 'mp', axis=1, tiled=True)  86.3 us
    all_to_all x1, blocking collectives, shards(): lax.all_to_all(outgoing, 'pool', split_axis=0, concat_axis=0, tiled=True)  46.5 us
    dot_general x2, matrix products, fold_with(): total = jnp.dot(piece, weight, preferred_element_type=jnp.float32)  14.4 us
    all_gather x1, waiting for transfers between devices, project_turn(): lax.all_gather(rows, 'mp', axis=1, tiled=True)  13.9 us
    reduce_sum x2, other arithmetic, fold_with(): squares = jnp.sum(jnp.square(piece.astype(jnp.float32)), axis=1)  12.4 us
    all_to_all x1, waiting for transfers between devices, shards(): lax.all_to_all(out_facts, 'pool', split_axis=0, concat_axis=0, tiled=True)  8.05 us
    all_to_all x1, starting transfers between devices, shards(): lax.all_to_all(out_facts, 'pool', split_axis=0, concat_axis=0, tiled=True)  5.76 us
  transfers between devices with their start and end apart: 3, of which 3 were waited for; matrix products, arithmetic and copies ran while one was open for 7% of the time, Pallas kernels for 0%

commit v1 on v0

v1 whole, which is shorter than its diff:
```python
import jax
import jax.numpy as jnp
from jax import lax
from jax.sharding import PartitionSpec as P

D = 8192
HD = 128
BLK = 64
KVD = 1024
NZ = 2
NX = 4
NC = 2
LIFT = 16384.0


def spot(z, x, c):
    return (z * NX + x) * NC + c


def pairs(move):
    return [
        (spot(z, x, c), spot(*move(z, x, c)))
        for z in range(NZ)
        for x in range(NX)
        for c in range(NC)
    ]


def to_z(v):
    return lax.ppermute(v, "mp", pairs(lambda z, x, c: (1 - z, x, c)))


def to_core(v):
    return lax.ppermute(v, "mp", pairs(lambda z, x, c: (z, x, 1 - c)))


def along_x(v, d):
    return lax.ppermute(v, "mp", pairs(lambda z, x, c: (z, (x + d) % NX, c)))


def angles(positions):
    half = HD // 2
    freq = jnp.exp(
        -jnp.log(jnp.float32(1000000.0)) * (jnp.arange(half).astype(jnp.float32) * 2.0 / HD)
    )
    angle = positions.astype(jnp.float32)[:, None] * freq[None, :]
    return jnp.cos(angle), jnp.sin(angle)


def rotate(values, cosine, sine, is_key):
    half = HD // 2
    first = values[:, :half]
    second = values[:, half:]
    turned = jnp.concatenate(
        [first * cosine - second * sine, second * cosine + first * sine], axis=1
    )
    return jnp.where(is_key, turned, values)


def squares_of(rows):
    return jnp.sum(jnp.square(rows.astype(jnp.float32)), axis=1)


def partials(rows, weights):
    outs = []
    for w in weights:
        outs.append(jnp.dot(rows, w, preferred_element_type=jnp.float32))
    return outs


def collect(rows, weights):
    norm = squares_of(rows)
    held = jnp.clip(norm, 1e-36, 1e37)
    down = (LIFT * lax.rsqrt(held))[:, None]
    parts = partials(rows, weights)
    total = norm
    terms = []
    for d in range(1, NX):
        sent = (parts[d] * down).astype(jnp.float16)
        got = along_x(sent, NX - d)
        other = along_x(norm, NX - d)
        total = total + other
        up = jnp.sqrt(jnp.clip(other, 1e-36, 1e37)) * (1.0 / LIFT)
        terms.append((got, up))
    return parts[0], terms, total


def finish(own, terms, total, kv_bias):
    scale = lax.rsqrt(total / D + 1e-06)
    value = own * scale[:, None]
    for got, up in terms:
        value = value + got.astype(jnp.float32) * (up * scale)[:, None]
    return value + kv_bias[None, :]


def shards(
    stored_hidden,
    block_owner,
    block_valid,
    block_start,
    turn_hidden,
    turn_position,
    kv_weight,
    kv_bias,
):
    groups = lax.axis_size("pool")
    me = lax.axis_index("mp")
    x = (me // NC) % NX
    core = me % NC
    z = me // (NC * NX)
    is_key = me * HD < KVD
    local = stored_hidden.shape[1]
    blocks_here = block_owner.shape[0]
    offsets = jnp.arange(BLK)

    by_slab = kv_weight.reshape(NZ, NX, NC * local, HD)

    def slab(d):
        return lax.dynamic_index_in_dim(by_slab, (x + d) % NX, axis=1, keepdims=False)

    def whole(rows):
        near = to_core(rows)
        far = to_z(rows)
        far_near = to_core(far)
        mine = jnp.where(core == 0, jnp.concatenate([rows, near], 1), jnp.concatenate([near, rows], 1))
        others = jnp.where(core == 0, jnp.concatenate([far, far_near], 1), jnp.concatenate([far_near, far], 1))
        return jnp.where(z == 0, jnp.concatenate([mine, others], 1), jnp.concatenate([others, mine], 1))

    stored = whole(stored_hidden)
    weights = [slab(0).reshape(NZ * NC * local, HD)] + [
        along_x(slab(d), d).reshape(NZ * NC * local, HD) for d in range(1, NX)
    ]
    turn = whole(turn_hidden)

    s_own, s_terms, s_total = collect(stored, weights)
    t_own, t_terms, t_total = collect(turn, weights)

    positions = (block_start[:, None] + offsets[None, :]).reshape(-1)
    cosine, sine = angles(positions)
    pre = finish(s_own, s_terms, s_total, kv_bias)
    roped = rotate(pre, cosine, sine, is_key)
    keep = (offsets[None, :] < block_valid[:, None]).reshape(-1, 1)
    restored = jnp.where(keep, roped, 0.0).astype(jnp.bfloat16).reshape(blocks_here, BLK, HD)
    picks = (block_owner[:, None] == jnp.arange(groups)[None, :]).astype(jnp.bfloat16)
    outgoing = jnp.einsum(
        "bg,brd->grd", picks, restored, preferred_element_type=jnp.float32
    ).astype(jnp.bfloat16)
    arrived = lax.all_to_all(outgoing, "pool", split_axis=0, concat_axis=0, tiled=True)
    restored_cache = arrived.reshape(groups * BLK, HD)

    cosine, sine = angles(turn_position)
    pre = finish(t_own, t_terms, t_total, kv_bias)
    turn_kv = rotate(pre, cosine, sine, is_key).astype(jnp.bfloat16)
    return (restored_cache, turn_kv)


def solution(mesh):
    placed = (
        P("pool", "mp"),
        P("pool"),
        P("pool"),
        P("pool"),
        P("pool", "mp"),
        P("pool"),
        P(None, "mp"),
        P("mp"),
    )
    return jax.shard_map(
        shards,
        mesh=mesh,
        in_specs=placed,
        out_specs=(P("pool", "mp"), P("pool", "mp")),
        check_vma=False,
    )
```

time: 212 us -> 98.7 us (0.47)
  the two profiles are of different devices: /device:TPU:1 before, /device:TPU:32 now
where the time goes in v1:
time: 98.7 us; the launch traced here: 98.4 us
  waiting for transfers between devices  40.1 us (41%)
  starting transfers between devices  36.6 us (37%)
  other arithmetic  8.37 us (8%)
  matrix products  7.09 us (7%)
  local copies, waits for them, and re-layouts  5.31 us (5%)
    ppermute x15, starting transfers between devices, along_x(): return lax.ppermute(v, 'mp', pairs(lambda z, x, c: (z, (x + d) % NX, c)))  23.9 us
    ppermute x2, waiting for transfers between devices, to_z(): return lax.ppermute(v, 'mp', pairs(lambda z, x, c: (1 - z, x, c)))  15.1 us
    ppermute x15, waiting for transfers between devices, along_x(): return lax.ppermute(v, 'mp', pairs(lambda z, x, c: (z, (x + d) % NX, c)))  14.7 us
    all_to_all x1, starting transfers between devices, shards(): lax.all_to_all(outgoing, 'pool', split_axis=0, concat_axis=0, tiled=True)  10.3 us
    all_to_all x1, waiting for transfers between devices, shards(): lax.all_to_all(outgoing, 'pool', split_axis=0, concat_axis=0, tiled=True)  10.2 us
    dot_general x8, matrix products, partials(): outs.append(jnp.dot(rows, w, preferred_element_type=jnp.float32))  6.75 us
    select_n x2, other arithmetic, whole(): jnp.where(core == 0, jnp.concatenate([rows, near], 1), jnp.concatenate([n...  3.06 us
    dynamic_slice x1, local copies, waits for them, and re-layouts, slab(): lax.dynamic_index_in_dim(by_slab, (x + d) % NX, axis=1, keepdims=False)  2.76 us
  transfers between devices with their start and end apart: 22, of which 9 were waited for; matrix products, arithmetic and copies ran while one was open for 15% of the time, Pallas kernels for 0%

profile of v1, /device:TPU:32, one launch (start us, length us, event | category | flops | bytes accessed | tf_op | source)
XLA Modules:
  0.0 98.4 jit_solution(18298904945014263754)
XLA Ops:
  0.6 1.9 %collective-permute-start.1 = (bf16[512,512]{1,0:T(8,128)(2,1)}, bf16[512,512]{1,0:T(8,128)(2,1)S(1)}, u32[]{:S(2)}, u32[]{:S(2)}) collective-permute-start(bf16[512,512]{1,0:T(8,128)(2,1)} %param.8), channel_id=1, source_target_pairs={{0,8},{1,9},{2,10},{3,11},{4,12},{5,13},{6,14},{7,15},{8,0},{9,1},... | collective-permute-start | bytes 1572872 | tf_op jit(solution)/shard_map/ppermute | solution.py:30
  2.6 0.2 collective-permute-start.13
  2.8 0.3 collective-permute-start.12
  3.1 2.8 %constant_dynamic-slice_fusion = (bf16[2,1,1024,128]{3,2,1,0:T(8,128)(2,1)S(1)}, bf16[2,1024,128]{2,1,0:T(8,128)(2,1)}, bf16[2,1024,128]{2,1,0:T(8,128)(2,1)}, bf16[2,1024,128]{2,1,0:T(8,128)(2,1)}) fusion(bf16[2,4,1024,128]{3,2,1,0:T(8,128)(2,1)} %bitcast.34, s32[]{:T(128)S(6)} %select_n.106, s32[]{:T(128)S(6)} %select_n.112, s32[]{:T(128)S(6)} %select_n.110, ...), kind=kLoop, calls=%fused_computation.63 | loop fusion | bytes 4194320 | tf_op jit(solution)/shard_map/jit(dynamic_index_in_dim)/dynamic_slice | solution.py:119
  5.8 1.4 %collective-permute-start.6 = (bf16[2,1024,128]{2,1,0:T(8,128)(2,1)}, bf16[2,1024,128]{2,1,0:T(8,128)(2,1)S(1)}, u32[]{:S(2)}, u32[]{:S(2)}) collective-permute-start(bf16[2,1024,128]{2,1,0:T(8,128)(2,1)} %get-tuple-element.19), channel_id=1, source_target_pairs={{0,2},{1,3},{2,4},{3,5},{4,6},{5,7},{6,0},{7,1},{8,10},{9,11},{10,... | collective-permute-start | bytes 1572872 | tf_op jit(solution)/shard_map/ppermute | solution.py:38
  7.4 8.3 %collective-permute-done.1 = bf16[512,512]{1,0:T(8,128)(2,1)S(1)} collective-permute-done((bf16[512,512]{1,0:T(8,128)(2,1)}, bf16[512,512]{1,0:T(8,128)(2,1)S(1)}, u32[]{:S(2)}, u32[]{:S(2)}) %collective-permute-start.1) | collective-permute-done | bytes 524320 | tf_op jit(solution)/shard_map/ppermute | solution.py:30
  15.9 3.1 %collective-permute-start.8 = (bf16[2,1024,128]{2,1,0:T(8,128)(2,1)}, bf16[2,1024,128]{2,1,0:T(8,128)(2,1)S(1)}, u32[]{:S(2)}, u32[]{:S(2)}) collective-permute-start(bf16[2,1024,128]{2,1,0:T(8,128)(2,1)} %get-tuple-element.18), channel_id=1, source_target_pairs={{0,4},{1,5},{2,6},{3,7},{4,0},{5,1},{6,2},{7,3},{8,12},{9,13},{10,... | collective-permute-start | bytes 1572872 | tf_op jit(solution)/shard_map/ppermute | solution.py:38
  19.0 6.8 %collective-permute-done.13 = bf16[512,512]{1,0:T(8,128)(2,1)S(1)} collective-permute-done((bf16[512,512]{1,0:T(8,128)(2,1)}, bf16[512,512]{1,0:T(8,128)(2,1)S(1)}, u32[]{:S(2)}, u32[]{:S(2)}) %collective-permute-start.13) | collective-permute-done | bytes 524320 | tf_op jit(solution)/shard_map/ppermute | solution.py:30
  25.8 1.5 %maximum_select_fusion.2 = bf16[512,1024]{1,0:T(8,128)(2,1)S(1)} fusion(bf16[512,512]{1,0:T(8,128)(2,1)} %collective-permute-done, bf16[512,512]{1,0:T(8,128)(2,1)S(1)} %copy-done, pred[]{:T(512)S(6)} %eq.34), kind=kLoop, calls=%fused_computation.17 | loop fusion | flops 4718592 | bytes 2097153 | tf_op jit(solution)/shard_map/jit(_where)/select_n | solution.py:125
  27.4 1.5 %maximum_select_fusion.4 = bf16[512,1024]{1,0:T(8,128)(2,1)S(1)} fusion(bf16[512,512]{1,0:T(8,128)(2,1)} %collective-permute-done.12, bf16[512,512]{1,0:T(8,128)(2,1)S(1)} %copy-done.1, pred[]{:T(512)S(6)} %eq.34), kind=kLoop, calls=%fused_computation.19 | loop fusion | flops 4718592 | bytes 2097153 | tf_op jit(solution)/shard_map/jit(_where)/select_n | solution.py:125
  28.9 1.5 %maximum_select_fusion.3 = bf16[512,1024]{1,0:T(8,128)(2,1)S(1)} fusion(bf16[512,512]{1,0:T(8,128)(2,1)} %collective-permute-done.2, bf16[512,512]{1,0:T(8,128)(2,1)S(1)} %collective-permute-done.1, pred[]{:T(512)S(6)} %eq.34), kind=kLoop, calls=%fused_computation.18 | loop fusion | flops 4718592 | bytes 2097153 | tf_op jit(solution)/shard_map/jit(_where)/select_n | solution.py:126
  30.5 1.0 %multiply_reduce_fusion.1 = (f32[512]{0:T(512)S(1)}, bf16[512,2048]{1,0:T(8,128)(2,1)S(1)}) fusion(bf16[512,1024]{1,0:T(8,128)(2,1)S(1)} %maximum_select_fusion.2, bf16[512,1024]{1,0:T(8,128)(2,1)S(1)} %maximum_select_fusion.3, pred[]{:T(512)S(6)} %eq.33), kind=kLoop, calls=%fused_computation.1 | loop fusion | flops 12582400 | bytes 4196353 | tf_op jit(solution)/shard_map/reduce_sum | solution.py:61
  31.5 2.8 %collective-permute-start.3 = (f32[512]{0:T(512)S(1)}, f32[512]{0:T(512)S(1)}, u32[]{:S(2)}, u32[]{:S(2)}) collective-permute-start(f32[512]{0:T(512)S(1)} %get-tuple-element.14), channel_id=1, source_target_pairs={{0,6},{1,7},{2,0},{3,1},{4,2},{5,3},{6,4},{7,5},{8,14},{9,15},{10,... | collective-permute-start | bytes 6152 | tf_op jit(solution)/shard_map/ppermute | solution.py:38
  34.3 0.8 collective-permute-start.4
  35.1 0.8 fusion.25
  36.0 1.0 collective-permute-start.5
  37.0 0.3 maximum_select_fusion.5
  37.3 1.0 %multiply_reduce_fusion = (f32[512]{0:T(512)S(1)}, bf16[512,2048]{1,0:T(8,128)(2,1)S(1)}) fusion(bf16[512,1024]{1,0:T(8,128)(2,1)S(1)} %maximum_select_fusion.4, bf16[512,1024]{1,0:T(8,128)(2,1)S(1)} %maximum_select_fusion.5, pred[]{:T(512)S(6)} %eq.33), kind=kLoop, calls=%fused_computation | loop fusion | flops 12582400 | bytes 4196353 | tf_op jit(solution)/shard_map/reduce_sum | solution.py:61
  38.3 2.4 %collective-permute-start.10 = (bf16[2,1024,128]{2,1,0:T(8,128)(2,1)S(1)}, bf16[2,1024,128]{2,1,0:T(8,128)(2,1)S(1)}, u32[]{:S(2)}, u32[]{:S(2)}) collective-permute-start(bf16[2,1024,128]{2,1,0:T(8,128)(2,1)S(1)} %copy-done.2), channel_id=1, source_target_pairs={{0,6},{1,7},{2,0},{3,1},{4,2},{5,3},{6,4},{7,5},{8,14},{9,15},{10,... | collective-permute-start | bytes 1572872 | tf_op jit(solution)/shard_map/ppermute | solution.py:38
  40.8 0.1 collective-permute-start.15
  40.9 1.7 %collective-permute-start.16 = (f32[512]{0:T(512)S(1)}, f32[512]{0:T(512)S(1)}, u32[]{:S(2)}, u32[]{:S(2)}) collective-permute-start(f32[512]{0:T(512)S(1)} %get-tuple-element.10), channel_id=1, source_target_pairs={{0,4},{1,5},{2,6},{3,7},{4,0},{5,1},{6,2},{7,3},{8,12},{9,13},{10,... | collective-permute-start | bytes 6152 | tf_op jit(solution)/shard_map/ppermute | solution.py:38
  42.5 1.5 %collective-permute-start.17 = (f32[512]{0:T(512)S(1)}, f32[512]{0:T(512)S(1)}, u32[]{:S(2)}, u32[]{:S(2)}) collective-permute-start(f32[512]{0:T(512)S(1)} %get-tuple-element.10), channel_id=1, source_target_pairs={{0,2},{1,3},{2,4},{3,5},{4,6},{5,7},{6,0},{7,1},{8,10},{9,11},{10,... | collective-permute-start | bytes 6152 | tf_op jit(solution)/shard_map/ppermute | solution.py:38
  44.0 0.8 fusion
  44.8 0.8 fusion.1
  45.7 6.4 %collective-permute-done.15 = f32[512]{0:T(512)S(1)} collective-permute-done((f32[512]{0:T(512)S(1)}, f32[512]{0:T(512)S(1)}, u32[]{:S(2)}, u32[]{:S(2)}) %collective-permute-start.15) | collective-permute-done | bytes 2080 | tf_op jit(solution)/shard_map/ppermute | solution.py:38
  52.1 0.8 fusion.3
  52.9 0.8 fusion.4
  53.8 0.8 fusion.2
  54.6 0.8 fusion.5
  55.4 3.6 %collective-permute-start.7 = (f16[512,128]{0,1:T(8,128)(2,1)S(1)}, f16[512,128]{0,1:T(8,128)(2,1)S(1)}, u32[]{:S(2)}, u32[]{:S(2)}) collective-permute-start(f16[512,128]{0,1:T(8,128)(2,1)S(1)} %fusion), channel_id=1, source_target_pairs={{0,6},{1,7},{2,0},{3,1},{4,2},{5,3},{6,4},{7,5},{8,14},{9,15},{10,... | collective-permute-start | bytes 393224 | tf_op jit(solution)/shard_map/ppermute | solution.py:38
  59.0 0.3 collective-permute-start.9
  59.3 0.7 collective-permute-start.11
  60.0 2.6 %collective-permute-start.18 = (f16[512,128]{0,1:T(8,128)(2,1)S(1)}, f16[512,128]{0,1:T(8,128)(2,1)S(1)}, u32[]{:S(2)}, u32[]{:S(2)}) collective-permute-start(f16[512,128]{0,1:T(8,128)(2,1)S(1)} %fusion.3), channel_id=1, source_target_pairs={{0,6},{1,7},{2,0},{3,1},{4,2},{5,3},{6,4},{7,5},{8,14},{9,15},{10,... | collective-permute-start | bytes 393224 | tf_op jit(solution)/shard_map/ppermute | solution.py:38
  62.6 2.0 %collective-permute-start.19 = (f16[512,128]{0,1:T(8,128)(2,1)S(1)}, f16[512,128]{0,1:T(8,128)(2,1)S(1)}, u32[]{:S(2)}, u32[]{:S(2)}) collective-permute-start(f16[512,128]{0,1:T(8,128)(2,1)S(1)} %fusion.4), channel_id=1, source_target_pairs={{0,4},{1,5},{2,6},{3,7},{4,0},{5,1},{6,2},{7,3},{8,12},{9,13},{10,... | collective-permute-start | bytes 393224 | tf_op jit(solution)/shard_map/ppermute | solution.py:38
  64.6 0.6 collective-permute-done.7
  65.2 1.9 %collective-permute-done.9 = f16[512,128]{0,1:T(8,128)(2,1)S(1)} collective-permute-done((f16[512,128]{0,1:T(8,128)(2,1)S(1)}, f16[512,128]{0,1:T(8,128)(2,1)S(1)}, u32[]{:S(2)}, u32[]{:S(2)}) %collective-permute-start.9) | collective-permute-done | bytes 131104 | tf_op jit(solution)/shard_map/ppermute | solution.py:38
  67.1 2.2 %collective-permute-done.11 = f16[512,128]{0,1:T(8,128)(2,1)S(1)} collective-permute-done((f16[512,128]{0,1:T(8,128)(2,1)S(1)}, f16[512,128]{0,1:T(8,128)(2,1)S(1)}, u32[]{:S(2)}, u32[]{:S(2)}) %collective-permute-start.11) | collective-permute-done | bytes 131104 | tf_op jit(solution)/shard_map/ppermute | solution.py:38
  69.3 2.3 %collective-permute-done.19 = f16[512,128]{0,1:T(8,128)(2,1)S(1)} collective-permute-done((f16[512,128]{0,1:T(8,128)(2,1)S(1)}, f16[512,128]{0,1:T(8,128)(2,1)S(1)}, u32[]{:S(2)}, u32[]{:S(2)}) %collective-permute-start.19) | collective-permute-done | bytes 131104 | tf_op jit(solution)/shard_map/ppermute | solution.py:38
  71.6 1.3 %collective-permute-done.20 = f16[512,128]{0,1:T(8,128)(2,1)S(1)} collective-permute-done((f16[512,128]{0,1:T(8,128)(2,1)S(1)}, f16[512,128]{0,1:T(8,128)(2,1)S(1)}, u32[]{:S(2)}, u32[]{:S(2)}) %collective-permute-start.20) | collective-permute-done | bytes 131104 | tf_op jit(solution)/shard_map/ppermute | solution.py:38
  73.0 0.9 add_add_fusion
  73.9 1.2 %fusion.17 = (bf16[512,64]{0,1:T(8,128)(2,1)S(1)}, bf16[512,64]{0,1:T(8,128)(2,1)S(1)}, bf16[512,64]{0,1:T(8,128)(2,1)S(1)}, bf16[512,64]{0,1:T(8,128)(2,1)S(1)}) fusion(f32[512,128]{0,1:T(8,128)S(1)} %get-tuple-element.32, f32[512]{0:T(512)S(1)} %convert_element_type.94, f32[64]{0:T(128)S(1)} %multiply_exponential_fusion, ...), kind=kLoop, calls=%fused_computation.43 | loop fusion | flops 589824 | bytes 790784 | tf_op jit(solution)/shard_map/sub | solution.py:55
  75.1 0.1 copy.31
  75.2 0.3 convolution_convert_fusion
  75.6 0.8 copy.33
  76.4 10.3 %all-to-all-start = ((bf16[16,64,128]{2,1,0:T(8,128)(2,1)}), bf16[16,64,128]{2,1,0:T(8,128)(2,1)S(1)}, u32[]{:S(2)}, u32[]{:S(2)}) async-start(bf16[16,64,128]{2,1,0:T(8,128)(2,1)} %copy.33), calls=%async_computation | async-start | bytes 524288 | tf_op jit(solution)/shard_map/all_to_all | solution.py:148
  86.7 0.8 copy.37
  87.5 10.2 %all-to-all-done = bf16[16,64,128]{2,1,0:T(8,128)(2,1)S(1)} async-done(((bf16[16,64,128]{2,1,0:T(8,128)(2,1)}), bf16[16,64,128]{2,1,0:T(8,128)(2,1)S(1)}, u32[]{:S(2)}, u32[]{:S(2)}) %all-to-all-start) | async-done | bytes 262176 | tf_op jit(solution)/shard_map/all_to_all | solution.py:148
  97.7 0.7 copy.47
  (45 shorter events, 0.5 us)
Async XLA Ops:
  0.6 15.1 %collective-permute-start.1 = (bf16[512,512]{1,0:T(8,128)(2,1)}, bf16[512,512]{1,0:T(8,128)(2,1)S(1)}, u32[]{:S(2)}, u32[]{:S(2)}) collective-permute-start(bf16[512,512]{1,0:T(8,128)(2,1)} %param.8), channel_id=1, source_target_pairs={{0,8},{1,9},{2,10},{3,11},{4,12},{5,13},{6,14},{7,15},{8,0},{9,1},... | collective-permute-start | bytes 1572872 | tf_op jit(solution)/shard_map/ppermute | solution.py:30
  2.6 13.4 %collective-permute-start = (bf16[512,512]{1,0:T(8,128)(2,1)}, bf16[512,512]{1,0:T(8,128)(2,1)}, u32[]{:S(2)}, u32[]{:S(2)}) collective-permute-start(bf16[512,512]{1,0:T(8,128)(2,1)} %param.8), channel_id=1, source_target_pairs={{0,1},{1,0},{2,3},{3,2},{4,5},{5,4},{6,7},{7,6},{8,9},{9,8},{10,11... | collective-permute-start | bytes 1572872 | tf_op jit(solution)/shard_map/ppermute | solution.py:34
  2.6 23.3 %collective-permute-start.13 = (bf16[512,512]{1,0:T(8,128)(2,1)}, bf16[512,512]{1,0:T(8,128)(2,1)S(1)}, u32[]{:S(2)}, u32[]{:S(2)}) collective-permute-start(bf16[512,512]{1,0:T(8,128)(2,1)} %param.12), channel_id=1, source_target_pairs={{0,8},{1,9},{2,10},{3,11},{4,12},{5,13},{6,14},{7,15},{8,0},{9,1},... | collective-permute-start | bytes 1572872 | tf_op jit(solution)/shard_map/ppermute | solution.py:30
  2.8 24.6 %collective-permute-start.12 = (bf16[512,512]{1,0:T(8,128)(2,1)}, bf16[512,512]{1,0:T(8,128)(2,1)}, u32[]{:S(2)}, u32[]{:S(2)}) collective-permute-start(bf16[512,512]{1,0:T(8,128)(2,1)} %param.12), channel_id=1, source_target_pairs={{0,1},{1,0},{2,3},{3,2},{4,5},{5,4},{6,7},{7,6},{8,9},{9,8},{10,11... | collective-permute-start | bytes 1572872 | tf_op jit(solution)/shard_map/ppermute | solution.py:34
  3.1 4.2 %copy-start.6 = (s32[8]{0:T(128)S(1)}, s32[8]{0:T(128)}, u32[]{:S(2)}) copy-start(s32[8]{0:T(128)} %param.11) | copy-start | bytes 100
  3.1 4.3 %copy-start.3 = (s32[512]{0:T(512)S(1)}, s32[512]{0:T(512)}, u32[]{:S(2)}) copy-start(s32[512]{0:T(512)} %param.13) | copy-start | bytes 6148
  3.1 12.7 %copy-start.7 = (s32[8]{0:T(128)S(1)}, s32[8]{0:T(128)}, u32[]{:S(2)}) copy-start(s32[8]{0:T(128)} %param.10) | copy-start | bytes 100
  3.1 22.7 %copy-start = (bf16[512,512]{1,0:T(8,128)(2,1)S(1)}, bf16[512,512]{1,0:T(8,128)(2,1)}, u32[]{:S(2)}) copy-start(bf16[512,512]{1,0:T(8,128)(2,1)} %param.8) | copy-start | bytes 1572868
  5.8 21.5 %copy-start.1 = (bf16[512,512]{1,0:T(8,128)(2,1)S(1)}, bf16[512,512]{1,0:T(8,128)(2,1)}, u32[]{:S(2)}) copy-start(bf16[512,512]{1,0:T(8,128)(2,1)} %param.12) | copy-start | bytes 1572868
  5.8 36.7 %collective-permute-start.6 = (bf16[2,1024,128]{2,1,0:T(8,128)(2,1)}, bf16[2,1024,128]{2,1,0:T(8,128)(2,1)S(1)}, u32[]{:S(2)}, u32[]{:S(2)}) collective-permute-start(bf16[2,1024,128]{2,1,0:T(8,128)(2,1)} %get-tuple-element.19), channel_id=1, source_target_pairs={{0,2},{1,3},{2,4},{3,5},{4,6},{5,7},{6,0},{7,1},{8,10},{9,11},{10,... | collective-permute-start | bytes 1572872 | tf_op jit(solution)/shard_map/ppermute | solution.py:38
  15.7 13.2 %collective-permute-start.2 = (bf16[512,512]{1,0:T(8,128)(2,1)S(1)}, bf16[512,512]{1,0:T(8,128)(2,1)}, u32[]{:S(2)}, u32[]{:S(2)}) collective-permute-start(bf16[512,512]{1,0:T(8,128)(2,1)S(1)} %collective-permute-done.1), channel_id=1, source_target_pairs={{0,1},{1,0},{2,3},{3,2},{4,5},{5,4},{6,7},{7,6},{8,9},{9,8},{10,11... | collective-permute-start | bytes 1572872 | tf_op jit(solution)/shard_map/ppermute | solution.py:34
  15.9 28.9 %collective-permute-start.8 = (bf16[2,1024,128]{2,1,0:T(8,128)(2,1)}, bf16[2,1024,128]{2,1,0:T(8,128)(2,1)S(1)}, u32[]{:S(2)}, u32[]{:S(2)}) collective-permute-start(bf16[2,1024,128]{2,1,0:T(8,128)(2,1)} %get-tuple-element.18), channel_id=1, source_target_pairs={{0,4},{1,5},{2,6},{3,7},{4,0},{5,1},{6,2},{7,3},{8,12},{9,13},{10,... | collective-permute-start | bytes 1572872 | tf_op jit(solution)/shard_map/ppermute | solution.py:38
  25.8 10.2 %collective-permute-start.14 = (bf16[512,512]{1,0:T(8,128)(2,1)S(1)}, bf16[512,512]{1,0:T(8,128)(2,1)S(1)}, u32[]{:S(2)}, u32[]{:S(2)}) collective-permute-start(bf16[512,512]{1,0:T(8,128)(2,1)S(1)} %collective-permute-done.13), channel_id=1, source_target_pairs={{0,1},{1,0},{2,3},{3,2},{4,5},{5,4},{6,7},{7,6},{8,9},{9,8},{10,11... | collective-permute-start | bytes 1572872 | tf_op jit(solution)/shard_map/ppermute | solution.py:34
  31.5 6.8 %collective-permute-start.3 = (f32[512]{0:T(512)S(1)}, f32[512]{0:T(512)S(1)}, u32[]{:S(2)}, u32[]{:S(2)}) collective-permute-start(f32[512]{0:T(512)S(1)} %get-tuple-element.14), channel_id=1, source_target_pairs={{0,6},{1,7},{2,0},{3,1},{4,2},{5,3},{6,4},{7,5},{8,14},{9,15},{10,... | collective-permute-start | bytes 6152 | tf_op jit(solution)/shard_map/ppermute | solution.py:38
  34.3 6.4 %collective-permute-start.4 = (f32[512]{0:T(512)S(1)}, f32[512]{0:T(512)S(1)}, u32[]{:S(2)}, u32[]{:S(2)}) collective-permute-start(f32[512]{0:T(512)S(1)} %get-tuple-element.14), channel_id=1, source_target_pairs={{0,4},{1,5},{2,6},{3,7},{4,0},{5,1},{6,2},{7,3},{8,12},{9,13},{10,... | collective-permute-start | bytes 6152 | tf_op jit(solution)/shard_map/ppermute | solution.py:38
  36.0 4.9 %collective-permute-start.5 = (f32[512]{0:T(512)S(1)}, f32[512]{0:T(512)S(1)}, u32[]{:S(2)}, u32[]{:S(2)}) collective-permute-start(f32[512]{0:T(512)S(1)} %get-tuple-element.14), channel_id=1, source_target_pairs={{0,2},{1,3},{2,4},{3,5},{4,6},{5,7},{6,0},{7,1},{8,10},{9,11},{10,... | collective-permute-start | bytes 6152 | tf_op jit(solution)/shard_map/ppermute | solution.py:38
  37.3 1.1 %copy-start.2 = (bf16[2,1024,128]{2,1,0:T(8,128)(2,1)S(1)}, bf16[2,1024,128]{2,1,0:T(8,128)(2,1)}, u32[]{:S(2)}) copy-start(bf16[2,1024,128]{2,1,0:T(8,128)(2,1)} %get-tuple-element.17) | copy-start | bytes 1572868
  38.3 15.4 %collective-permute-start.10 = (bf16[2,1024,128]{2,1,0:T(8,128)(2,1)S(1)}, bf16[2,1024,128]{2,1,0:T(8,128)(2,1)S(1)}, u32[]{:S(2)}, u32[]{:S(2)}) collective-permute-start(bf16[2,1024,128]{2,1,0:T(8,128)(2,1)S(1)} %copy-done.2), channel_id=1, source_target_pairs={{0,6},{1,7},{2,0},{3,1},{4,2},{5,3},{6,4},{7,5},{8,14},{9,15},{10,... | collective-permute-start | bytes 1572872 | tf_op jit(solution)/shard_map/ppermute | solution.py:38
  40.8 11.3 %collective-permute-start.15 = (f32[512]{0:T(512)S(1)}, f32[512]{0:T(512)S(1)}, u32[]{:S(2)}, u32[]{:S(2)}) collective-permute-start(f32[512]{0:T(512)S(1)} %get-tuple-element.10), channel_id=1, source_target_pairs={{0,6},{1,7},{2,0},{3,1},{4,2},{5,3},{6,4},{7,5},{8,14},{9,15},{10,... | collective-permute-start | bytes 6152 | tf_op jit(solution)/shard_map/ppermute | solution.py:38
  40.9 11.2 %collective-permute-start.16 = (f32[512]{0:T(512)S(1)}, f32[512]{0:T(512)S(1)}, u32[]{:S(2)}, u32[]{:S(2)}) collective-permute-start(f32[512]{0:T(512)S(1)} %get-tuple-element.10), channel_id=1, source_target_pairs={{0,4},{1,5},{2,6},{3,7},{4,0},{5,1},{6,2},{7,3},{8,12},{9,13},{10,... | collective-permute-start | bytes 6152 | tf_op jit(solution)/shard_map/ppermute | solution.py:38
  42.5 9.5 %collective-permute-start.17 = (f32[512]{0:T(512)S(1)}, f32[512]{0:T(512)S(1)}, u32[]{:S(2)}, u32[]{:S(2)}) collective-permute-start(f32[512]{0:T(512)S(1)} %get-tuple-element.10), channel_id=1, source_target_pairs={{0,2},{1,3},{2,4},{3,5},{4,6},{5,7},{6,0},{7,1},{8,10},{9,11},{10,... | collective-permute-start | bytes 6152 | tf_op jit(solution)/shard_map/ppermute | solution.py:38
  53.7 19.2 %copy-start.4 = (f32[128]{0:T(128)S(1)}, f32[128]{0:T(128)}, u32[]{:S(2)}) copy-start(f32[128]{0:T(128)} %param.15) | copy-start | bytes 1540
  55.4 9.7 %collective-permute-start.7 = (f16[512,128]{0,1:T(8,128)(2,1)S(1)}, f16[512,128]{0,1:T(8,128)(2,1)S(1)}, u32[]{:S(2)}, u32[]{:S(2)}) collective-permute-start(f16[512,128]{0,1:T(8,128)(2,1)S(1)} %fusion), channel_id=1, source_target_pairs={{0,6},{1,7},{2,0},{3,1},{4,2},{5,3},{6,4},{7,5},{8,14},{9,15},{10,... | collective-permute-start | bytes 393224 | tf_op jit(solution)/shard_map/ppermute | solution.py:38
  59.0 8.0 %collective-permute-start.9 = (f16[512,128]{0,1:T(8,128)(2,1)S(1)}, f16[512,128]{0,1:T(8,128)(2,1)S(1)}, u32[]{:S(2)}, u32[]{:S(2)}) collective-permute-start(f16[512,128]{0,1:T(8,128)(2,1)S(1)} %fusion.1), channel_id=1, source_target_pairs={{0,4},{1,5},{2,6},{3,7},{4,0},{5,1},{6,2},{7,3},{8,12},{9,13},{10,... | collective-permute-start | bytes 393224 | tf_op jit(solution)/shard_map/ppermute | solution.py:38
  59.3 9.9 %collective-permute-start.11 = (f16[512,128]{0,1:T(8,128)(2,1)S(1)}, f16[512,128]{0,1:T(8,128)(2,1)S(1)}, u32[]{:S(2)}, u32[]{:S(2)}) collective-permute-start(f16[512,128]{0,1:T(8,128)(2,1)S(1)} %fusion.2), channel_id=1, source_target_pairs={{0,2},{1,3},{2,4},{3,5},{4,6},{5,7},{6,0},{7,1},{8,10},{9,11},{10,... | collective-permute-start | bytes 393224 | tf_op jit(solution)/shard_map/ppermute | solution.py:38
  60.0 9.3 %collective-permute-start.18 = (f16[512,128]{0,1:T(8,128)(2,1)S(1)}, f16[512,128]{0,1:T(8,128)(2,1)S(1)}, u32[]{:S(2)}, u32[]{:S(2)}) collective-permute-start(f16[512,128]{0,1:T(8,128)(2,1)S(1)} %fusion.3), channel_id=1, source_target_pairs={{0,6},{1,7},{2,0},{3,1},{4,2},{5,3},{6,4},{7,5},{8,14},{9,15},{10,... | collective-permute-start | bytes 393224 | tf_op jit(solution)/shard_map/ppermute | solution.py:38
  62.6 9.0 %collective-permute-start.19 = (f16[512,128]{0,1:T(8,128)(2,1)S(1)}, f16[512,128]{0,1:T(8,128)(2,1)S(1)}, u32[]{:S(2)}, u32[]{:S(2)}) collective-permute-start(f16[512,128]{0,1:T(8,128)(2,1)S(1)} %fusion.4), channel_id=1, source_target_pairs={{0,4},{1,5},{2,6},{3,7},{4,0},{5,1},{6,2},{7,3},{8,12},{9,13},{10,... | collective-permute-start | bytes 393224 | tf_op jit(solution)/shard_map/ppermute | solution.py:38
  65.2 7.8 %collective-permute-start.20 = (f16[512,128]{0,1:T(8,128)(2,1)S(1)}, f16[512,128]{0,1:T(8,128)(2,1)S(1)}, u32[]{:S(2)}, u32[]{:S(2)}) collective-permute-start(f16[512,128]{0,1:T(8,128)(2,1)S(1)} %fusion.5), channel_id=1, source_target_pairs={{0,2},{1,3},{2,4},{3,5},{4,6},{5,7},{6,0},{7,1},{8,10},{9,11},{10,... | collective-permute-start | bytes 393224 | tf_op jit(solution)/shard_map/ppermute | solution.py:38
  72.9 2.3 %copy-start.5 = (s32[8]{0:T(128)S(1)}, s32[8]{0:T(128)}, u32[]{:S(2)}) copy-start(s32[8]{0:T(128)} %param.9) | copy-start | bytes 100
  76.4 21.3 %all-to-all-start = ((bf16[16,64,128]{2,1,0:T(8,128)(2,1)}), bf16[16,64,128]{2,1,0:T(8,128)(2,1)S(1)}, u32[]{:S(2)}, u32[]{:S(2)}) async-start(bf16[16,64,128]{2,1,0:T(8,128)(2,1)} %copy.33), calls=%async_computation | async-start | bytes 524288 | tf_op jit(solution)/shard_map/all_to_all | solution.py:148

commit v2 on v1

v2 whole, which is shorter than its diff:
```python
import jax
import jax.numpy as jnp
from jax import lax
from jax.experimental import pallas as pl
from jax.experimental.pallas import tpu as pltpu
from jax.sharding import PartitionSpec as P

D = 8192
HD = 128
BLK = 64
KVD = 1024
NZ = 2
NX = 4
NC = 2
SLAB = D // NX
LIFT = 16384.0
STEPS = 2048.0
TILE = 256
LN2 = 0.6931471805599453
LOW = 1e-36
HIGH = 1e37


def spot(z, x, c):
    return (z * NX + x) * NC + c


def pairs(move):
    return [
        (spot(z, x, c), spot(*move(z, x, c)))
        for z in range(NZ)
        for x in range(NX)
        for c in range(NC)
    ]


def to_z(v):
    return lax.ppermute(v, "mp", pairs(lambda z, x, c: (1 - z, x, c)))


def to_core(v):
    return lax.ppermute(v, "mp", pairs(lambda z, x, c: (z, x, 1 - c)))


def along_x(v, d):
    return lax.ppermute(v, "mp", pairs(lambda z, x, c: (z, (x + d) % NX, c)))


VMEM = pl.BlockSpec(memory_space=pltpu.VMEM)
SMEM = pl.BlockSpec(memory_space=pltpu.SMEM)
f32 = jnp.float32


def diagonal():
    shape = (HD, HD)
    return lax.broadcasted_iota(jnp.int32, shape, 0) == lax.broadcasted_iota(jnp.int32, shape, 1)


def anchor_kernel(x, out):
    out[...] = x[...]


def anchor(x):
    return pl.pallas_call(
        anchor_kernel,
        out_shape=jax.ShapeDtypeStruct(x.shape, x.dtype),
        in_specs=[VMEM],
        out_specs=VMEM,
        cost_estimate=pl.CostEstimate(flops=10**11, bytes_accessed=3 * 10**8, transcendentals=0),
    )(x)


def outer_kernel(home, r0, r1, r2, r3, w1, w3, f1, f3, code, norm):
    rows = norm.shape[0]
    mask = diagonal()

    def step(t, carry):
        at = pl.ds(pl.multiple_of(t * TILE, TILE), TILE)
        acc = jnp.zeros((TILE, 2 * HD), f32)
        sq = jnp.zeros((TILE, HD), f32)
        for j, r in enumerate((r0, r1, r2, r3)):
            piece = r[at, :]
            at_w = lax.bitwise_xor(home[0], j)
            acc += jnp.dot(
                piece, jnp.concatenate([w1[at_w], w3[at_w]], axis=1), preferred_element_type=f32
            )
            wide = piece.astype(f32)
            wide = wide * wide
            for k in range(wide.shape[1] // HD):
                sq += wide[:, k * HD : (k + 1) * HD]
        total = jnp.clip(jnp.sum(sq, axis=1, keepdims=True), LOW, HIGH)
        norm[at, :] = total
        down = LIFT * lax.rsqrt(total)
        f1[at, :] = acc[:, :HD] * down
        f3[at, :] = acc[:, HD:] * down
        return carry

    lax.fori_loop(0, rows // TILE, step, 0)
    lines = [
        jnp.sum(jnp.where(mask, norm[k * HD : (k + 1) * HD, :], 0.0), axis=0, keepdims=True)
        for k in range(rows // HD)
    ]
    u = jnp.log(jnp.concatenate(lines, axis=0)) * (1.0 / LN2)
    whole = jnp.floor(u)
    part = (u - whole) * STEPS
    middle = jnp.floor(part)
    told = jnp.concatenate([whole, middle, part - middle, jnp.zeros_like(u)], axis=0)
    code[...] = told
    f1[pl.ds(rows, 16), :] = told
    f3[pl.ds(rows, 16), :] = told


def inner_kernel(home, r0, r1, r2, r3, w0, w2, code, norm, own, f2):
    rows = norm.shape[0]

    def step(t, carry):
        at = pl.ds(pl.multiple_of(t * TILE, TILE), TILE)
        acc = jnp.zeros((TILE, 2 * HD), f32)
        for j, r in enumerate((r0, r1, r2, r3)):
            at_w = lax.bitwise_xor(home[0], j)
            acc += jnp.dot(
                r[at, :], jnp.concatenate([w0[at_w], w2[at_w]], axis=1), preferred_element_type=f32
            )
        own[at, :] = acc[:, :HD]
        f2[at, :] = acc[:, HD:] * (LIFT * lax.rsqrt(norm[at, :]))
        return carry

    lax.fori_loop(0, rows // TILE, step, 0)
    f2[pl.ds(rows, 16), :] = code[...]


def call(body, out, args, flops, scalars=0):
    return pl.pallas_call(
        body,
        out_shape=out,
        in_specs=[SMEM] * scalars + [VMEM] * (len(args) - scalars),
        out_specs=jax.tree.map(lambda _: VMEM, out),
        compiler_params=pltpu.CompilerParams(vmem_limit_bytes=24 * 2**20),
        cost_estimate=pl.CostEstimate(flops=flops, bytes_accessed=2**20, transcendentals=0),
    )(*args)


def outer(home, rows, w1, w3):
    count = rows[0].shape[0]
    sent = jax.ShapeDtypeStruct((count + 16, HD), f32)
    out = (
        sent,
        sent,
        jax.ShapeDtypeStruct((16, HD), f32),
        jax.ShapeDtypeStruct((count, 1), f32),
    )
    f1, f3, code, norm = call(outer_kernel, out, (home, *rows, w1, w3), 4 * count * HD * SLAB, 1)
    return f1.astype(jnp.float16), f3.astype(jnp.float16), code, norm


def inner(home, rows, w0, w2, code, norm):
    count = rows[0].shape[0]
    out = (
        jax.ShapeDtypeStruct((count, HD), f32),
        jax.ShapeDtypeStruct((count + 16, HD), f32),
    )
    own, f2 = call(inner_kernel, out, (home, *rows, w0, w2, code, norm), 4 * count * HD * SLAB, 1)
    return own, f2.astype(jnp.float16)


def finished(k, mask, own, code, got, bias, cosine, sine):
    at = slice(k * HD, (k + 1) * HD)
    lines = own.shape[0] // HD

    def norm_line(ref, first):
        u = ref[first + k : first + k + 1, :] + (
            ref[first + lines + k : first + lines + k + 1, :]
            + ref[first + 2 * lines + k : first + 2 * lines + k + 1, :]
        ) * (1.0 / STEPS)
        return jnp.exp(u * LN2)

    def column(line):
        return jnp.sum(jnp.where(mask, line, 0.0), axis=1, keepdims=True)

    norms = [norm_line(g, own.shape[0]) for g in got]
    total = norm_line(code, 0) + norms[0] + norms[1] + norms[2]
    scale = lax.rsqrt(total / D + 1e-06)
    value = own[at, :] * column(scale) + bias[...]
    for g, n in zip(got, norms):
        value += g[at, :] * column(jnp.sqrt(n) * scale * (1.0 / LIFT))
    return value * cosine[at, :] + pltpu.roll(value, HD // 2, 1) * sine[at, :]


def turn_kernel(own, code, g1, g2, g3, bias, cosine, sine, out):
    mask = diagonal()
    for k in range(own.shape[0] // HD):
        value = finished(k, mask, own, code, (g1, g2, g3), bias, cosine, sine)
        out[k * HD : (k + 1) * HD, :] = value.astype(out.dtype)


def stored_kernel(owner, valid, own, code, g1, g2, g3, bias, cosine, sine, out):
    mask = diagonal()
    row = lax.broadcasted_iota(jnp.int32, (BLK, HD), 0)
    out[...] = jnp.zeros(out.shape, out.dtype)
    for k in range(own.shape[0] // HD):
        value = finished(k, mask, own, code, (g1, g2, g3), bias, cosine, sine)
        for h in range(HD // BLK):
            b = k * (HD // BLK) + h
            kept = jnp.where(row < valid[b], value[h * BLK : (h + 1) * BLK], 0.0)
            out[owner[b]] = kept.astype(out.dtype)


def tables(positions, is_key):
    half = HD // 2
    freq = jnp.exp(
        -jnp.log(jnp.float32(1000000.0)) * (jnp.arange(half).astype(jnp.float32) * 2.0 / HD)
    )
    angle = positions.astype(jnp.float32)[:, None] * jnp.concatenate([freq, freq])[None, :]
    sign = jnp.where(jnp.arange(HD) < half, -1.0, 1.0)
    return (
        jnp.where(is_key, jnp.cos(angle), 1.0),
        jnp.where(is_key, jnp.sin(angle) * sign[None, :], 0.0),
    )


def shards(
    stored_hidden,
    block_owner,
    block_valid,
    block_start,
    turn_hidden,
    turn_position,
    kv_weight,
    kv_bias,
):
    groups = lax.axis_size("pool")
    me = lax.axis_index("mp")
    x = (me // NC) % NX
    z = me // (NC * NX)
    core = me % NC
    is_key = me * HD < KVD
    count, local = stored_hidden.shape
    bias = kv_bias[None, :]

    chunks = kv_weight.reshape(NZ, NX, NC, local, HD)

    home = (z * NC + core).astype(jnp.int32)[None]

    def slab(d):
        part = lax.dynamic_index_in_dim(chunks, (x + d) % NX, axis=1, keepdims=False)
        return part.reshape(NZ * NC, local, HD)

    held = anchor(bias)
    s_far = to_z(stored_hidden)
    w1 = along_x(slab(1), 1)
    w3 = along_x(slab(3), 3)
    w2 = along_x(slab(2), 2)
    near_in, bias = lax.optimization_barrier((stored_hidden, held))
    s_near = to_core(near_in)
    far_in, turn_in, _ = lax.optimization_barrier((s_far, turn_hidden, held))
    s_far_near = to_core(far_in)
    t_far = to_z(turn_in)
    t_near = to_core(turn_in)
    t_far_near = to_core(t_far)
    w0 = slab(0)

    s_rows = (stored_hidden, s_near, s_far, s_far_near)
    s1, s3, s_code, s_norm = outer(home, s_rows, w1, w3)
    s_g1, s_g3 = along_x(s1, NX - 1), along_x(s3, NX - 3)
    s_own, s2 = inner(home, s_rows, w0, w2, s_code, s_norm)
    s_g2 = along_x(s2, NX - 2)

    t_rows = (turn_hidden, t_near, t_far, t_far_near)
    t1, t3, t_code, t_norm = outer(home, t_rows, w1, w3)
    t_own, t2 = inner(home, t_rows, w0, w2, t_code, t_norm)
    s_own, t1, t2, t3 = lax.optimization_barrier((s_own, t1, t2, t3))

    positions = (block_start[:, None] + jnp.arange(BLK)[None, :]).reshape(-1)
    args = [v.astype(f32) for v in (s_g1, s_g2, s_g3)]
    outgoing = call(
        stored_kernel,
        jax.ShapeDtypeStruct((groups, BLK, HD), jnp.bfloat16),
        (block_owner, block_valid, s_own, s_code, *args, bias, *tables(positions, is_key)),
        2**20,
        2,
    )
    arrived = lax.all_to_all(outgoing, "pool", split_axis=0, concat_axis=0, tiled=True)
    restored_cache = arrived.reshape(groups * BLK, HD)

    t_got = along_x(t1, NX - 1), along_x(t2, NX - 2), along_x(t3, NX - 3)
    args = [v.astype(f32) for v in t_got]
    turn_kv = call(
        turn_kernel,
        jax.ShapeDtypeStruct((count, HD), jnp.bfloat16),
        (t_own, t_code, *args, bias, *tables(turn_position, is_key)),
        2**20,
    )
    return (restored_cache, turn_kv)


def solution(mesh):
    placed = (
        P("pool", "mp"),
        P("pool"),
        P("pool"),
        P("pool"),
        P("pool", "mp"),
        P("pool"),
        P(None, "mp"),
        P("mp"),
    )
    return jax.shard_map(
        shards,
        mesh=mesh,
        in_specs=placed,
        out_specs=(P("pool", "mp"), P("pool", "mp")),
        check_vma=False,
    )
```

time: 98.7 us -> 77.9 us (0.79)
  Pallas kernels: 0 us -> 12.5 us
  starting transfers between devices: 36.6 us -> 25.6 us
  waiting for transfers between devices: 40.1 us -> 31.9 us
  matrix products: 7.09 us -> 0 us
  other arithmetic: 8.37 us -> 3.08 us
  local copies, waits for them, and re-layouts: 5.31 us -> 3.63 us
    pallas_call x0 -> x7, Pallas kernels: none -> 12.5 us  [the longest x6 11.3 us: call(): pl.pallas_call(body, out_shape=out, in_specs=[SMEM] * scalars + [VMEM] *...]
    ppermute x15 -> x9, starting transfers between devices: 23.9 us -> 11.8 us  [along_x(): return lax.ppermute(v, 'mp', pairs(lambda z, x, c: (z, (x + d) % NX, c)))]
    all_to_all x1, waiting for transfers between devices: 10.2 us -> 1.1 us  [shards(): lax.all_to_all(outgoing, 'pool', split_axis=0, concat_axis=0, tiled=True)]
    dot_general x9 -> x0, matrix products: 7.09 us -> none  [the longest x8 6.75 us: partials(): outs.append(jnp.dot(rows, w, preferred_element_type=jnp.float32))]
    ppermute x2, waiting for transfers between devices: 15.1 us -> 19.4 us  [to_z(): return lax.ppermute(v, 'mp', pairs(lambda z, x, c: (1 - z, x, c)))]
    ppermute x15 -> x9, waiting for transfers between devices: 14.7 us -> 11.3 us  [along_x(): return lax.ppermute(v, 'mp', pairs(lambda z, x, c: (z, (x + d) % NX, c)))]
    select_n x4 -> x2, other arithmetic: 4.87 us -> 2.76 us  [the longest x1 2.68 us: tables(): jnp.where(is_key, jnp.sin(angle) * sign[None, :], 0.0)]
    reduce_sum x2 -> x0, other arithmetic: 2.07 us -> none  [squares_of(): return jnp.sum(jnp.square(rows.astype(jnp.float32)), axis=1)]
  transfers between devices with their start and end apart: 22 -> 16, of which waited for: 9 -> 9; matrix products, arithmetic and copies ran while one was open for 15% -> 4% of each run, Pallas kernels for 0% -> 10%
where the time goes in v2:
time: 77.9 us; the launch traced here: 77.6 us
  waiting for transfers between devices  31.9 us (41%)
  starting transfers between devices  25.6 us (33%)
  Pallas kernels  12.5 us (16%)
  local copies, waits for them, and re-layouts  3.63 us (5%)
  other arithmetic  3.08 us (4%)
  between operations  0.95 us (1%)
    ppermute x2, waiting for transfers between devices, to_z(): return lax.ppermute(v, 'mp', pairs(lambda z, x, c: (1 - z, x, c)))  19.4 us
    ppermute x9, starting transfers between devices, along_x(): return lax.ppermute(v, 'mp', pairs(lambda z, x, c: (z, (x + d) % NX, c)))  11.8 us
    ppermute x9, waiting for transfers between devices, along_x(): return lax.ppermute(v, 'mp', pairs(lambda z, x, c: (z, (x + d) % NX, c)))  11.3 us
    pallas_call x6, Pallas kernels, call(): pl.pallas_call(body, out_shape=out, in_specs=[SMEM] * scalars + [VMEM] *...  11.3 us
    all_to_all x1, starting transfers between devices, shards(): lax.all_to_all(outgoing, 'pool', split_axis=0, concat_axis=0, tiled=True)  11 us
    dynamic_slice x1, local copies, waits for them, and re-layouts, slab(): lax.dynamic_index_in_dim(chunks, (x + d) % NX, axis=1, keepdims=False)  2.81 us
    select_n x1, other arithmetic, tables(): jnp.where(is_key, jnp.sin(angle) * sign[None, :], 0.0)  2.68 us
    ppermute x2, starting transfers between devices, to_z(): return lax.ppermute(v, 'mp', pairs(lambda z, x, c: (1 - z, x, c)))  2.13 us
  transfers between devices with their start and end apart: 16, of which 9 were waited for; matrix products, arithmetic and copies ran while one was open for 4% of the time, Pallas kernels for 10%

profile of v2, /device:TPU:32, one launch (start us, length us, event | category | flops | bytes accessed | tf_op | source)
XLA Modules:
  0.0 77.6 jit_solution(5358874298302847787)
XLA Ops:
  0.7 2.8 %constant_dynamic-slice_fusion = (bf16[2,1,2,512,128]{4,3,2,1,0:T(8,128)(2,1)}, bf16[2,1,2,512,128]{4,3,2,1,0:T(8,128)(2,1)}, bf16[2,1,2,512,128]{4,3,2,1,0:T(8,128)(2,1)}, bf16[2,1,2,512,128]{4,3,2,1,0:T(8,128)(2,1)S(1)}) fusion(bf16[2,4,2,512,128]{4,3,2,1,0:T(8,128)(2,1)} %bitcast.18, s32[]{:T(128)S(6)} %select_n.89, s32[]{:T(128)S(6)} %select_n.87, ...), kind=kLoop, calls=%fused_computation.12 | loop fusion | bytes 4194320 | tf_op jit(solution)/shard_map/jit(dynamic_index_in_dim)/dynamic_slice | solution.py:245
  3.5 1.5 %collective-permute-start.4 = (bf16[4,512,128]{2,1,0:T(8,128)(2,1)}, bf16[4,512,128]{2,1,0:T(8,128)(2,1)S(1)}, u32[]{:S(2)}, u32[]{:S(2)}) collective-permute-start(bf16[4,512,128]{2,1,0:T(8,128)(2,1)} %bitcast.5), channel_id=1, source_target_pairs={{0,2},{1,3},{2,4},{3,5},{4,6},{5,7},{6,0},{7,1},{8,10},{9,11},{10,... | collective-permute-start | bytes 1572872 | tf_op jit(solution)/shard_map/ppermute | solution.py:46
  5.0 1.7 %collective-permute-start.5 = (bf16[4,512,128]{2,1,0:T(8,128)(2,1)}, bf16[4,512,128]{2,1,0:T(8,128)(2,1)S(1)}, u32[]{:S(2)}, u32[]{:S(2)}) collective-permute-start(bf16[4,512,128]{2,1,0:T(8,128)(2,1)} %bitcast.6), channel_id=1, source_target_pairs={{0,6},{1,7},{2,0},{3,1},{4,2},{5,3},{6,4},{7,5},{8,14},{9,15},{10,... | collective-permute-start | bytes 1572872 | tf_op jit(solution)/shard_map/ppermute | solution.py:46
  6.8 1.8 %collective-permute-start.1 = (bf16[512,512]{1,0:T(8,128)(2,1)S(1)}, bf16[512,512]{1,0:T(8,128)(2,1)}, u32[]{:S(2)}, u32[]{:S(2)}) collective-permute-start(bf16[512,512]{1,0:T(8,128)(2,1)S(1)} %copy-done), channel_id=1, source_target_pairs={{0,8},{1,9},{2,10},{3,11},{4,12},{5,13},{6,14},{7,15},{8,0},{9,1},... | collective-permute-start | bytes 1572872 | tf_op jit(solution)/shard_map/ppermute | solution.py:38
  8.6 1.2 %shard_map.95.bias = f32[1,128]{1,0:T(1,128)} custom-call(f32[1,128]{1,0:T(1,128)} %bitcast.21), custom_call_target="tpu_custom_call" | custom-call | flops 99999997952 | bytes 300000000 | tf_op jit(solution)/shard_map/pallas_call | solution.py:64
  9.9 10.1 %collective-permute-done.1.r2 = bf16[512,512]{1,0:T(8,128)(2,1)} collective-permute-done((bf16[512,512]{1,0:T(8,128)(2,1)S(1)}, bf16[512,512]{1,0:T(8,128)(2,1)}, u32[]{:S(2)}, u32[]{:S(2)}) %collective-permute-start.1) | collective-permute-done | bytes 524320 | tf_op jit(solution)/shard_map/ppermute | solution.py:38
  20.0 0.3 collective-permute-start.7
  20.3 0.0 collective-permute-start
  20.3 0.5 collective-permute-start.2
  20.8 0.0 collective-permute-done.4.w1
  20.8 1.8 %collective-permute-start.3 = (bf16[4,512,128]{2,1,0:T(8,128)(2,1)}, bf16[4,512,128]{2,1,0:T(8,128)(2,1)}, u32[]{:S(2)}, u32[]{:S(2)}) collective-permute-start(bf16[4,512,128]{2,1,0:T(8,128)(2,1)} %bitcast.20), channel_id=1, source_target_pairs={{0,4},{1,5},{2,6},{3,7},{4,0},{5,1},{6,2},{7,3},{8,12},{9,13},{10,... | collective-permute-start | bytes 1572872 | tf_op jit(solution)/shard_map/ppermute | solution.py:46
  22.6 0.1 add_convert_fusion
  22.7 0.1 convert_element_type.65
  22.8 0.0 collective-permute-done.5.w3
  22.8 0.1 collective-permute-start.6
  22.9 9.3 %collective-permute-done.7.r2 = bf16[512,512]{1,0:T(8,128)(2,1)S(1)} collective-permute-done((bf16[512,512]{1,0:T(8,128)(2,1)S(1)}, bf16[512,512]{1,0:T(8,128)(2,1)S(1)}, u32[]{:S(2)}, u32[]{:S(2)}) %collective-permute-start.7) | collective-permute-done | bytes 524320 | tf_op jit(solution)/shard_map/ppermute | solution.py:38
  32.2 0.0 collective-permute-start.8
  32.2 0.1 compare_select_fusion
  32.3 0.0 collective-permute-done.r1
  32.3 0.0 collective-permute-done.2.r3
  32.3 2.4 %shard_map.96 = (f32[528,128]{1,0:T(8,128)S(1)}, f32[528,128]{1,0:T(8,128)S(1)}, f32[16,128]{1,0:T(8,128)S(1)}, f32[512,1]{1,0:T(8,128)S(1)}) custom-call(s32[1]{0:T(128)} %bitcast.home, bf16[512,512]{1,0:T(8,128)(2,1)S(1)} %copy-done, bf16[512,512]{1,0:T(8,128)(2,1)} %collective-permute-done.r1, bf16[512,512]{1,0:T(8,128)(2,1)} %collective-permute-done.1.r2, ...), custom_call_target="tpu_custom_call" | custom-call | flops 536870912 | bytes 1048576 | tf_op jit(solution)/shard_map/pallas_call | solution.py:133
  34.7 1.8 %collective-permute-done.3.w2 = bf16[4,512,128]{2,1,0:T(8,128)(2,1)} collective-permute-done((bf16[4,512,128]{2,1,0:T(8,128)(2,1)}, bf16[4,512,128]{2,1,0:T(8,128)(2,1)}, u32[]{:S(2)}, u32[]{:S(2)}) %collective-permute-start.3) | collective-permute-done | bytes 524320 | tf_op jit(solution)/shard_map/ppermute | solution.py:46
  36.5 2.4 %shard_map.97 = (f32[512,128]{1,0:T(8,128)S(1)}, f32[528,128]{1,0:T(8,128)S(1)}) custom-call(s32[1]{0:T(128)} %bitcast.home, bf16[512,512]{1,0:T(8,128)(2,1)S(1)} %copy-done, bf16[512,512]{1,0:T(8,128)(2,1)} %collective-permute-done.r1, bf16[512,512]{1,0:T(8,128)(2,1)} %collective-permute-done.1.r2, bf16[512,512]{1,0:T(8,128)(2,1)} %collective-permute-done.2.r3, ...), custom_call_target="tpu_custom_call" | custom-call | flops 536870912 | bytes 1048576 | tf_op jit(solution)/shard_map/pallas_call | solution.py:133
  38.9 1.9 %collective-permute-start.10 = (f16[528,128]{1,0:T(8,128)(2,1)S(1)}, f16[528,128]{1,0:T(8,128)(2,1)S(1)}, u32[]{:S(2)}, u32[]{:S(2)}) collective-permute-start(f16[528,128]{1,0:T(8,128)(2,1)S(1)} %convert_element_type.60), channel_id=1, source_target_pairs={{0,4},{1,5},{2,6},{3,7},{4,0},{5,1},{6,2},{7,3},{8,12},{9,13},{10,... | collective-permute-start | bytes 405512 | tf_op jit(solution)/shard_map/ppermute | solution.py:46
  40.8 1.2 %collective-permute-start.9 = (f16[528,128]{1,0:T(8,128)(2,1)S(1)}, f16[528,128]{1,0:T(8,128)(2,1)S(1)}, u32[]{:S(2)}, u32[]{:S(2)}) collective-permute-start(f16[528,128]{1,0:T(8,128)(2,1)S(1)} %convert_element_type.58), channel_id=1, source_target_pairs={{0,6},{1,7},{2,0},{3,1},{4,2},{5,3},{6,4},{7,5},{8,14},{9,15},{10,... | collective-permute-start | bytes 405512 | tf_op jit(solution)/shard_map/ppermute | solution.py:46
  42.1 1.0 %collective-permute-start.11 = (f16[528,128]{1,0:T(8,128)(2,1)S(1)}, f16[528,128]{1,0:T(8,128)(2,1)S(1)}, u32[]{:S(2)}, u32[]{:S(2)}) collective-permute-start(f16[528,128]{1,0:T(8,128)(2,1)S(1)} %convert_element_type.62), channel_id=1, source_target_pairs={{0,2},{1,3},{2,4},{3,5},{4,6},{5,7},{6,0},{7,1},{8,10},{9,11},{10,... | collective-permute-start | bytes 405512 | tf_op jit(solution)/shard_map/ppermute | solution.py:46
  43.0 2.7 %fusion.5 = (f32[512,128]{1,0:T(8,128)S(1)}, f32[512,128]{1,0:T(8,128)}, f32[512,128]{1,0:T(8,128)S(1)}, f32[512,128]{1,0:T(8,128)S(1)}) fusion(f32[512]{0:T(512)S(1)} %convert_element_type.70, f32[128]{0:T(128)S(1)} %get-tuple-element.52, f32[128]{0:T(128)S(1)} %get-tuple-element.53, pred[]{:T(512)S(6)} %lt.62, f32[512]{0:T(512)S(1)} %convert_element_type.65), kind=kLoop, calls=%fused_computation.9 | loop fusion | flops 524288 | bytes 1053697 | tf_op jit(solution)/shard_map/jit(_where)/select_n | solution.py:217
  45.7 1.2 %collective-permute-done.10 = f16[528,128]{1,0:T(8,128)(2,1)S(1)} collective-permute-done((f16[528,128]{1,0:T(8,128)(2,1)S(1)}, f16[528,128]{1,0:T(8,128)(2,1)S(1)}, u32[]{:S(2)}, u32[]{:S(2)}) %collective-permute-start.10) | collective-permute-done | bytes 135200 | tf_op jit(solution)/shard_map/ppermute | solution.py:46
  46.9 0.0 collective-permute-done.9
  47.0 1.7 %collective-permute-done.11 = f16[528,128]{1,0:T(8,128)(2,1)S(1)} collective-permute-done((f16[528,128]{1,0:T(8,128)(2,1)S(1)}, f16[528,128]{1,0:T(8,128)(2,1)S(1)}, u32[]{:S(2)}, u32[]{:S(2)}) %collective-permute-start.11) | collective-permute-done | bytes 135200 | tf_op jit(solution)/shard_map/ppermute | solution.py:46
  48.7 0.0 collective-permute-done.6.r1
  48.7 0.0 collective-permute-done.8.r3
  48.7 1.1 %shard_map.98 = (f32[528,128]{1,0:T(8,128)S(1)}, f32[528,128]{1,0:T(8,128)S(1)}, f32[16,128]{1,0:T(8,128)S(1)}, f32[512,1]{1,0:T(8,128)S(1)}) custom-call(s32[1]{0:T(128)} %bitcast.home, bf16[512,512]{1,0:T(8,128)(2,1)S(1)} %copy-done.1, bf16[512,512]{1,0:T(8,128)(2,1)S(1)} %collective-permute-done.6.r1, bf16[512,512]{1,0:T(8,128)(2,1)S(1)} %collective-permute-done.7.r2, ...), custom_call_target="tpu_custom_call" | custom-call | flops 536870912 | bytes 1048576 | tf_op jit(solution)/shard_map/pallas_call | solution.py:133
  49.8 0.0 copy-start.4
  49.8 0.0 copy-start.5
  49.8 1.9 %shard_map.99 = (f32[512,128]{1,0:T(8,128)S(1)}, f32[528,128]{1,0:T(8,128)S(1)}) custom-call(s32[1]{0:T(128)} %bitcast.home, bf16[512,512]{1,0:T(8,128)(2,1)S(1)} %copy-done.1, bf16[512,512]{1,0:T(8,128)(2,1)S(1)} %collective-permute-done.6.r1, bf16[512,512]{1,0:T(8,128)(2,1)S(1)} %collective-permute-done.7.r2, ...), custom_call_target="tpu_custom_call" | custom-call | flops 536870912 | bytes 1048576 | tf_op jit(solution)/shard_map/pallas_call | solution.py:133
  51.8 0.0 copy-start.2
  51.9 2.0 %shard_map.100 = bf16[16,64,128]{2,1,0:T(8,128)(2,1)} custom-call(s32[8]{0:T(128)S(1)} %copy-done.4, s32[8]{0:T(128)S(1)} %copy-done.5, f32[512,128]{1,0:T(8,128)S(1)} %get-tuple-element.33.own, f32[16,128]{1,0:T(8,128)S(1)} %get-tuple-element.24.code, f32[528,128]{1,0:T(8,128)S(1)} %convert_element_type.59.g1, f32[528,128]{1,0:T(8,128)S(1)} %convert_element_type.61.g2, ...), custom_call_target="tpu_custom_call" | custom-call | flops 1048576 | bytes 1048576 | tf_op jit(solution)/shard_map/pallas_call | solution.py:133
  53.9 11.0 %all-to-all-start = ((bf16[16,64,128]{2,1,0:T(8,128)(2,1)}), bf16[16,64,128]{2,1,0:T(8,128)(2,1)S(1)}, u32[]{:S(2)}, u32[]{:S(2)}) async-start(bf16[16,64,128]{2,1,0:T(8,128)(2,1)} %shard_map.100), calls=%async_computation | async-start | bytes 524288 | tf_op jit(solution)/shard_map/all_to_all | solution.py:282
  64.9 1.1 %collective-permute-start.12 = (f16[528,128]{1,0:T(8,128)(2,1)S(1)}, f16[528,128]{1,0:T(8,128)(2,1)S(1)}, u32[]{:S(2)}, u32[]{:S(2)}) collective-permute-start(f16[528,128]{1,0:T(8,128)(2,1)S(1)} %convert_element_type.55), channel_id=1, source_target_pairs={{0,6},{1,7},{2,0},{3,1},{4,2},{5,3},{6,4},{7,5},{8,14},{9,15},{10,... | collective-permute-start | bytes 405512 | tf_op jit(solution)/shard_map/ppermute | solution.py:46
  66.0 1.0 %collective-permute-start.13 = (f16[528,128]{1,0:T(8,128)(2,1)S(1)}, f16[528,128]{1,0:T(8,128)(2,1)S(1)}, u32[]{:S(2)}, u32[]{:S(2)}) collective-permute-start(f16[528,128]{1,0:T(8,128)(2,1)S(1)} %convert_element_type.56), channel_id=1, source_target_pairs={{0,4},{1,5},{2,6},{3,7},{4,0},{5,1},{6,2},{7,3},{8,12},{9,13},{10,... | collective-permute-start | bytes 405512 | tf_op jit(solution)/shard_map/ppermute | solution.py:46
  67.0 0.6 collective-permute-start.14
  67.6 2.9 %collective-permute-done.12 = f16[528,128]{1,0:T(8,128)(2,1)S(1)} collective-permute-done((f16[528,128]{1,0:T(8,128)(2,1)S(1)}, f16[528,128]{1,0:T(8,128)(2,1)S(1)}, u32[]{:S(2)}, u32[]{:S(2)}) %collective-permute-start.12) | collective-permute-done | bytes 135200 | tf_op jit(solution)/shard_map/ppermute | solution.py:46
  70.6 2.4 %collective-permute-done.13 = f16[528,128]{1,0:T(8,128)(2,1)S(1)} collective-permute-done((f16[528,128]{1,0:T(8,128)(2,1)S(1)}, f16[528,128]{1,0:T(8,128)(2,1)S(1)}, u32[]{:S(2)}, u32[]{:S(2)}) %collective-permute-start.13) | collective-permute-done | bytes 135200 | tf_op jit(solution)/shard_map/ppermute | solution.py:46
  73.0 1.4 %collective-permute-done.14 = f16[528,128]{1,0:T(8,128)(2,1)S(1)} collective-permute-done((f16[528,128]{1,0:T(8,128)(2,1)S(1)}, f16[528,128]{1,0:T(8,128)(2,1)S(1)}, u32[]{:S(2)}, u32[]{:S(2)}) %collective-permute-start.14) | collective-permute-done | bytes 135200 | tf_op jit(solution)/shard_map/ppermute | solution.py:46
  74.4 1.4 %shard_map.101 = bf16[512,128]{1,0:T(8,128)(2,1)} custom-call(f32[512,128]{1,0:T(8,128)S(1)} %get-tuple-element.38.own, f32[16,128]{1,0:T(8,128)S(1)} %get-tuple-element.29.code, f32[528,128]{1,0:T(8,128)S(1)} %convert_element_type.67.g1, f32[528,128]{1,0:T(8,128)S(1)} %convert_element_type.68.g2, f32[528,128]{1,0:T(8,128)S(1)} %convert_element_type.69.g3, ...), custom_call_target="tpu_custom_call" | custom-call | flops 1048576 | bytes 1048576 | tf_op jit(solution)/shard_map/pallas_call | solution.py:133
  75.8 1.1 %all-to-all-done = bf16[16,64,128]{2,1,0:T(8,128)(2,1)S(1)} async-done(((bf16[16,64,128]{2,1,0:T(8,128)(2,1)}), bf16[16,64,128]{2,1,0:T(8,128)(2,1)S(1)}, u32[]{:S(2)}, u32[]{:S(2)}) %all-to-all-start) | async-done | bytes 262176 | tf_op jit(solution)/shard_map/all_to_all | solution.py:282
  76.9 0.7 copy.19
  (27 shorter events, 0.3 us)
Async XLA Ops:
  0.7 6.1 %copy-start = (bf16[512,512]{1,0:T(8,128)(2,1)S(1)}, bf16[512,512]{1,0:T(8,128)(2,1)}, u32[]{:S(2)}) copy-start(bf16[512,512]{1,0:T(8,128)(2,1)} %r0.5) | copy-start | bytes 1572868
  3.5 17.2 %collective-permute-start.4 = (bf16[4,512,128]{2,1,0:T(8,128)(2,1)}, bf16[4,512,128]{2,1,0:T(8,128)(2,1)S(1)}, u32[]{:S(2)}, u32[]{:S(2)}) collective-permute-start(bf16[4,512,128]{2,1,0:T(8,128)(2,1)} %bitcast.5), channel_id=1, source_target_pairs={{0,2},{1,3},{2,4},{3,5},{4,6},{5,7},{6,0},{7,1},{8,10},{9,11},{10,... | collective-permute-start | bytes 1572872 | tf_op jit(solution)/shard_map/ppermute | solution.py:46
  5.0 17.7 %collective-permute-start.5 = (bf16[4,512,128]{2,1,0:T(8,128)(2,1)}, bf16[4,512,128]{2,1,0:T(8,128)(2,1)S(1)}, u32[]{:S(2)}, u32[]{:S(2)}) collective-permute-start(bf16[4,512,128]{2,1,0:T(8,128)(2,1)} %bitcast.6), channel_id=1, source_target_pairs={{0,6},{1,7},{2,0},{3,1},{4,2},{5,3},{6,4},{7,5},{8,14},{9,15},{10,... | collective-permute-start | bytes 1572872 | tf_op jit(solution)/shard_map/ppermute | solution.py:46
  6.8 13.2 %collective-permute-start.1 = (bf16[512,512]{1,0:T(8,128)(2,1)S(1)}, bf16[512,512]{1,0:T(8,128)(2,1)}, u32[]{:S(2)}, u32[]{:S(2)}) collective-permute-start(bf16[512,512]{1,0:T(8,128)(2,1)S(1)} %copy-done), channel_id=1, source_target_pairs={{0,8},{1,9},{2,10},{3,11},{4,12},{5,13},{6,14},{7,15},{8,0},{9,1},... | collective-permute-start | bytes 1572872 | tf_op jit(solution)/shard_map/ppermute | solution.py:38
  8.6 11.4 %copy-start.1 = (bf16[512,512]{1,0:T(8,128)(2,1)S(1)}, bf16[512,512]{1,0:T(8,128)(2,1)}, u32[]{:S(2)}) copy-start(bf16[512,512]{1,0:T(8,128)(2,1)} %r0.7) | copy-start | bytes 1572868
  8.6 14.0 %copy-start.7 = (s32[8]{0:T(128)S(1)}, s32[8]{0:T(128)}, u32[]{:S(2)}) copy-start(s32[8]{0:T(128)} %param.11) | copy-start | bytes 100
  8.6 14.1 %copy-start.6 = (s32[512]{0:T(512)S(1)}, s32[512]{0:T(512)}, u32[]{:S(2)}) copy-start(s32[512]{0:T(512)} %param.13) | copy-start | bytes 6148
  20.0 12.2 %collective-permute-start.7 = (bf16[512,512]{1,0:T(8,128)(2,1)S(1)}, bf16[512,512]{1,0:T(8,128)(2,1)S(1)}, u32[]{:S(2)}, u32[]{:S(2)}) collective-permute-start(bf16[512,512]{1,0:T(8,128)(2,1)S(1)} %copy-done.1), channel_id=1, source_target_pairs={{0,8},{1,9},{2,10},{3,11},{4,12},{5,13},{6,14},{7,15},{8,0},{9,1},... | collective-permute-start | bytes 1572872 | tf_op jit(solution)/shard_map/ppermute | solution.py:38
  20.3 12.0 %collective-permute-start = (bf16[512,512]{1,0:T(8,128)(2,1)S(1)}, bf16[512,512]{1,0:T(8,128)(2,1)}, u32[]{:S(2)}, u32[]{:S(2)}) collective-permute-start(bf16[512,512]{1,0:T(8,128)(2,1)S(1)} %copy-done), channel_id=1, source_target_pairs={{0,1},{1,0},{2,3},{3,2},{4,5},{5,4},{6,7},{7,6},{8,9},{9,8},{10,11... | collective-permute-start | bytes 1572872 | tf_op jit(solution)/shard_map/ppermute | solution.py:42
  20.3 12.0 %collective-permute-start.2 = (bf16[512,512]{1,0:T(8,128)(2,1)}, bf16[512,512]{1,0:T(8,128)(2,1)}, u32[]{:S(2)}, u32[]{:S(2)}) collective-permute-start(bf16[512,512]{1,0:T(8,128)(2,1)} %collective-permute-done.1.r2), channel_id=1, source_target_pairs={{0,1},{1,0},{2,3},{3,2},{4,5},{5,4},{6,7},{7,6},{8,9},{9,8},{10,11... | collective-permute-start | bytes 1572872 | tf_op jit(solution)/shard_map/ppermute | solution.py:42
  20.8 15.7 %collective-permute-start.3 = (bf16[4,512,128]{2,1,0:T(8,128)(2,1)}, bf16[4,512,128]{2,1,0:T(8,128)(2,1)}, u32[]{:S(2)}, u32[]{:S(2)}) collective-permute-start(bf16[4,512,128]{2,1,0:T(8,128)(2,1)} %bitcast.20), channel_id=1, source_target_pairs={{0,4},{1,5},{2,6},{3,7},{4,0},{5,1},{6,2},{7,3},{8,12},{9,13},{10,... | collective-permute-start | bytes 1572872 | tf_op jit(solution)/shard_map/ppermute | solution.py:46
  22.8 25.9 %collective-permute-start.6 = (bf16[512,512]{1,0:T(8,128)(2,1)S(1)}, bf16[512,512]{1,0:T(8,128)(2,1)S(1)}, u32[]{:S(2)}, u32[]{:S(2)}) collective-permute-start(bf16[512,512]{1,0:T(8,128)(2,1)S(1)} %copy-done.1), channel_id=1, source_target_pairs={{0,1},{1,0},{2,3},{3,2},{4,5},{5,4},{6,7},{7,6},{8,9},{9,8},{10,11... | collective-permute-start | bytes 1572872 | tf_op jit(solution)/shard_map/ppermute | solution.py:42
  32.2 16.5 %collective-permute-start.8 = (bf16[512,512]{1,0:T(8,128)(2,1)S(1)}, bf16[512,512]{1,0:T(8,128)(2,1)S(1)}, u32[]{:S(2)}, u32[]{:S(2)}) collective-permute-start(bf16[512,512]{1,0:T(8,128)(2,1)S(1)} %collective-permute-done.7.r2), channel_id=1, source_target_pairs={{0,1},{1,0},{2,3},{3,2},{4,5},{5,4},{6,7},{7,6},{8,9},{9,8},{10,11... | collective-permute-start | bytes 1572872 | tf_op jit(solution)/shard_map/ppermute | solution.py:42
  38.9 8.0 %collective-permute-start.10 = (f16[528,128]{1,0:T(8,128)(2,1)S(1)}, f16[528,128]{1,0:T(8,128)(2,1)S(1)}, u32[]{:S(2)}, u32[]{:S(2)}) collective-permute-start(f16[528,128]{1,0:T(8,128)(2,1)S(1)} %convert_element_type.60), channel_id=1, source_target_pairs={{0,4},{1,5},{2,6},{3,7},{4,0},{5,1},{6,2},{7,3},{8,12},{9,13},{10,... | collective-permute-start | bytes 405512 | tf_op jit(solution)/shard_map/ppermute | solution.py:46
  40.8 6.1 %collective-permute-start.9 = (f16[528,128]{1,0:T(8,128)(2,1)S(1)}, f16[528,128]{1,0:T(8,128)(2,1)S(1)}, u32[]{:S(2)}, u32[]{:S(2)}) collective-permute-start(f16[528,128]{1,0:T(8,128)(2,1)S(1)} %convert_element_type.58), channel_id=1, source_target_pairs={{0,6},{1,7},{2,0},{3,1},{4,2},{5,3},{6,4},{7,5},{8,14},{9,15},{10,... | collective-permute-start | bytes 405512 | tf_op jit(solution)/shard_map/ppermute | solution.py:46
  42.1 6.6 %collective-permute-start.11 = (f16[528,128]{1,0:T(8,128)(2,1)S(1)}, f16[528,128]{1,0:T(8,128)(2,1)S(1)}, u32[]{:S(2)}, u32[]{:S(2)}) collective-permute-start(f16[528,128]{1,0:T(8,128)(2,1)S(1)} %convert_element_type.62), channel_id=1, source_target_pairs={{0,2},{1,3},{2,4},{3,5},{4,6},{5,7},{6,0},{7,1},{8,10},{9,11},{10,... | collective-permute-start | bytes 405512 | tf_op jit(solution)/shard_map/ppermute | solution.py:46
  49.8 2.1 %copy-start.3 = (f32[1,128]{1,0:T(1,128)S(1)}, f32[1,128]{1,0:T(1,128)}, u32[]{:S(2)}) copy-start(f32[1,128]{1,0:T(1,128)} %shard_map.95.bias) | copy-start | bytes 1540
  49.8 2.1 %copy-start.4 = (s32[8]{0:T(128)S(1)}, s32[8]{0:T(128)}, u32[]{:S(2)}) copy-start(s32[8]{0:T(128)} %owner.1) | copy-start | bytes 100
  49.8 2.1 %copy-start.5 = (s32[8]{0:T(128)S(1)}, s32[8]{0:T(128)}, u32[]{:S(2)}) copy-start(s32[8]{0:T(128)} %valid.1) | copy-start | bytes 100
  51.8 22.6 %copy-start.2 = (f32[512,128]{1,0:T(8,128)S(1)}, f32[512,128]{1,0:T(8,128)}, u32[]{:S(2)}) copy-start(f32[512,128]{1,0:T(8,128)} %get-tuple-element.47.cosine) | copy-start | bytes 786436
  53.9 23.0 %all-to-all-start = ((bf16[16,64,128]{2,1,0:T(8,128)(2,1)}), bf16[16,64,128]{2,1,0:T(8,128)(2,1)S(1)}, u32[]{:S(2)}, u32[]{:S(2)}) async-start(bf16[16,64,128]{2,1,0:T(8,128)(2,1)} %shard_map.100), calls=%async_computation | async-start | bytes 524288 | tf_op jit(solution)/shard_map/all_to_all | solution.py:282
  64.9 5.6 %collective-permute-start.12 = (f16[528,128]{1,0:T(8,128)(2,1)S(1)}, f16[528,128]{1,0:T(8,128)(2,1)S(1)}, u32[]{:S(2)}, u32[]{:S(2)}) collective-permute-start(f16[528,128]{1,0:T(8,128)(2,1)S(1)} %convert_element_type.55), channel_id=1, source_target_pairs={{0,6},{1,7},{2,0},{3,1},{4,2},{5,3},{6,4},{7,5},{8,14},{9,15},{10,... | collective-permute-start | bytes 405512 | tf_op jit(solution)/shard_map/ppermute | solution.py:46
  66.0 7.0 %collective-permute-start.13 = (f16[528,128]{1,0:T(8,128)(2,1)S(1)}, f16[528,128]{1,0:T(8,128)(2,1)S(1)}, u32[]{:S(2)}, u32[]{:S(2)}) collective-permute-start(f16[528,128]{1,0:T(8,128)(2,1)S(1)} %convert_element_type.56), channel_id=1, source_target_pairs={{0,4},{1,5},{2,6},{3,7},{4,0},{5,1},{6,2},{7,3},{8,12},{9,13},{10,... | collective-permute-start | bytes 405512 | tf_op jit(solution)/shard_map/ppermute | solution.py:46
  67.0 7.4 %collective-permute-start.14 = (f16[528,128]{1,0:T(8,128)(2,1)S(1)}, f16[528,128]{1,0:T(8,128)(2,1)S(1)}, u32[]{:S(2)}, u32[]{:S(2)}) collective-permute-start(f16[528,128]{1,0:T(8,128)(2,1)S(1)} %convert_element_type.57), channel_id=1, source_target_pairs={{0,2},{1,3},{2,4},{3,5},{4,6},{5,7},{6,0},{7,1},{8,10},{9,11},{10,... | collective-permute-start | bytes 405512 | tf_op jit(solution)/shard_map/ppermute | solution.py:46

commit v3 on v2

v3 whole, which is shorter than its diff:
```python
import functools

import jax
import jax.numpy as jnp
from jax import lax
from jax.experimental import pallas as pl
from jax.experimental.pallas import tpu as pltpu
from jax.sharding import PartitionSpec as P

D = 8192
HD = 128
BLK = 64
KVD = 1024
NZ = 2
NX = 4
NC = 2
NY = 4
LIFT = 16384.0
STEPS = 2048.0
LN2 = 0.6931471805599453
LOW = 1e-36
HIGH = 1e37


def spot(z, x, c):
    return (z * NX + x) * NC + c


def pairs(move):
    return [
        (spot(z, x, c), spot(*move(z, x, c)))
        for z in range(NZ)
        for x in range(NX)
        for c in range(NC)
    ]


def across(v, e):
    return lax.ppermute(v, "mp", pairs(lambda z, x, c: (z ^ (e // NC), x, c ^ (e % NC))))


def outward(v, groups):
    ring = groups // NY
    moves = []
    for h in range(ring):
        for y in range(NY):
            for z, x, c in ((z, x, c) for z in range(NZ) for x in range(NX) for c in range(NC)):
                g = (h + 2 * z - 1) % ring * NY + y
                src = (h * NY + y) * NZ * NX * NC + spot(z, x, c)
                moves.append((src, g * NZ * NX * NC + spot(1 - z, x, 1 - c)))
    return lax.ppermute(v, ("pool", "mp"), moves)


def along_x(v, d):
    return lax.ppermute(v, "mp", pairs(lambda z, x, c: (z, (x + d) % NX, c)))


VMEM = pl.BlockSpec(memory_space=pltpu.VMEM)
SMEM = pl.BlockSpec(memory_space=pltpu.SMEM)
HBM = pl.BlockSpec(memory_space=pltpu.HBM)
f32 = jnp.float32


def diagonal():
    shape = (HD, HD)
    return lax.broadcasted_iota(jnp.int32, shape, 0) == lax.broadcasted_iota(jnp.int32, shape, 1)


def place():
    me = lax.axis_index("mp")
    return me // (NC * NX), lax.rem(me // NC, NX), lax.rem(me, NC)


def slice_kernel(w, w1, w2, w3, sems):
    z, _, c = place()
    copies = []
    for e, out in ((2, w2), (3, w3), (1, w1)):
        for k in range(NX):
            src = w.at[lax.bitwise_xor(z, e // NC), k, lax.bitwise_xor(c, e % NC)]
            copies.append(pltpu.make_async_copy(src, out.at[k], sems.at[len(copies)]))
    for copy in copies:
        copy.start()
    for copy in copies:
        copy.wait()


def slices(w):
    part = jax.ShapeDtypeStruct((NX,) + w.shape[3:], w.dtype)
    return pl.pallas_call(
        slice_kernel,
        out_shape=(part,) * 3,
        in_specs=[pl.BlockSpec(memory_space=pl.ANY)],
        out_specs=(VMEM,) * 3,
        scratch_shapes=[pltpu.SemaphoreType.DMA((3 * NX,))],
        cost_estimate=pl.CostEstimate(flops=0, bytes_accessed=2**21, transcendentals=0),
    )(w)


def anchor_kernel(x, after, out):
    out[...] = x[...]


def anchor(x, after):
    return pl.pallas_call(
        anchor_kernel,
        out_shape=jax.ShapeDtypeStruct(x.shape, x.dtype),
        in_specs=[VMEM, pl.BlockSpec(memory_space=pl.ANY)],
        out_specs=VMEM,
        compiler_params=pltpu.CompilerParams(vmem_limit_bytes=2**20),
        cost_estimate=pl.CostEstimate(flops=10**11, bytes_accessed=3 * 10**8, transcendentals=0),
    )(x, after)


def load(w, weights, wv, ws, order):
    z, x, c = place()
    waits = {}
    for j in order:
        k = lax.rem(x - j + NX, NX)
        waits[j] = []
        for e, src in enumerate((w.at[z, k, c], *(v.at[k] for v in weights))):
            copy = pltpu.make_async_copy(src, wv.at[j, e], ws.at[j * 4 + e])
            copy.start()
            waits[j].append(copy)
    return waits


def product(piece, wv, j):
    both = jnp.concatenate([wv[j, e] for e in range(4)], axis=1)
    return jnp.dot(piece, both, preferred_element_type=f32)


def squared(piece):
    wide = piece.astype(f32)
    wide = wide * wide
    return sum(wide[:, g * HD : (g + 1) * HD] for g in range(wide.shape[1] // HD))


def first_kernel(r0, r1, r3, w, w1, w2, w3, acc, sq, rv, wv, rs, ws):
    rows = {0: r0, 1: r1, 3: r3}
    copies = {}
    for j, r in rows.items():
        copies[j] = pltpu.make_async_copy(r, rv.at[j], rs.at[j])
        copies[j].start()
    waits = load(w, (w1, w2, w3), wv, ws, rows)
    for j in rows:
        copies[j].wait()
        for copy in waits[j]:
            copy.wait()
        if j == 0:
            acc[...] = product(rv[j], wv, j)
            sq[...] = squared(rv[j])
        else:
            acc[...] += product(rv[j], wv, j)
            sq[...] += squared(rv[j])


def last_kernel(count, *refs):
    pieces, refs = refs[:count], refs[count:]
    w, w1, w2, w3, acc, sq, own, f1, f2, f3, code, rv, wv, rs, ws = refs
    size = own.shape[0] // count
    copies = []
    for n, r in enumerate(pieces):
        at = pl.ds(n * size, size)
        copies.append(pltpu.make_async_copy(r, rv.at[2, at], rs.at[n]))
        copies[n].start()
    waits = load(w, (w1, w2, w3), wv, ws, (2,))
    for copy in copies + waits[2]:
        copy.wait()
    total = acc[...] + product(rv[2], wv, 2)
    pack(total, sq[...] + squared(rv[2]), own, f1, f2, f3, code)


def whole_kernel(r0, r1, r2, r3, w, w1, w2, w3, own, f1, f2, f3, code, rv, wv, rs, ws):
    rows = (r0, r1, r2, r3)
    copies = []
    for j, r in enumerate(rows):
        copies.append(pltpu.make_async_copy(r, rv.at[j], rs.at[j]))
        copies[j].start()
    waits = load(w, (w1, w2, w3), wv, ws, range(NX))
    total = sq = 0.0
    for j in range(NX):
        copies[j].wait()
        for copy in waits[j]:
            copy.wait()
        total += product(rv[j], wv, j)
        sq += squared(rv[j])
    pack(total, sq, own, f1, f2, f3, code)


def pack(total, sq, own, f1, f2, f3, code):
    rows = own.shape[0]
    mask = diagonal()
    norm = jnp.clip(jnp.sum(sq, axis=1, keepdims=True), LOW, HIGH)
    down = LIFT * lax.rsqrt(norm)
    own[...] = total[:, :HD]
    for e, f in enumerate((f1, f2, f3)):
        f[pl.ds(0, rows), :] = total[:, (e + 1) * HD : (e + 2) * HD] * down
    lines = []
    for g in range(rows // HD):
        part = jnp.where(mask, norm[g * HD : (g + 1) * HD, :], 0.0)
        lines.append(jnp.sum(part, axis=0, keepdims=True))
    u = jnp.log(jnp.concatenate(lines, axis=0)) * (1.0 / LN2)
    whole = jnp.floor(u)
    part = (u - whole) * STEPS
    middle = jnp.floor(part)
    told = jnp.concatenate([whole, middle, part - middle, jnp.zeros_like(u)], axis=0)
    code[...] = told
    for f in (f1, f2, f3):
        f[pl.ds(rows, 16), :] = told


def scratch(rows, w):
    return [
        pltpu.VMEM((NX,) + rows, w.dtype),
        pltpu.VMEM((NX, 4) + w.shape[3:], w.dtype),
        pltpu.SemaphoreType.DMA((NX,)),
        pltpu.SemaphoreType.DMA((NX * 4,)),
    ]


def multiply(body, rows, w, weights, held, out, grant, cost):
    count, local = rows[0].shape[0], rows[0].shape[1]
    return pl.pallas_call(
        body,
        out_shape=out,
        in_specs=[HBM] * (len(rows) + 4) + [VMEM] * len(held),
        out_specs=(VMEM,) * len(out),
        scratch_shapes=scratch((out[0].shape[0], local), w),
        compiler_params=pltpu.CompilerParams(vmem_limit_bytes=grant * 2**20),
        cost_estimate=pl.CostEstimate(flops=cost * 2**30, bytes_accessed=2**22, transcendentals=0),
    )(*rows, w, *weights, *held)


def outputs(count):
    sent = jax.ShapeDtypeStruct((count + 16, HD), f32)
    return (
        jax.ShapeDtypeStruct((count, HD), f32),
        sent,
        sent,
        sent,
        jax.ShapeDtypeStruct((16, HD), f32),
    )


def half_width(parts):
    own, f1, f2, f3, code = parts
    return own, code, [f.astype(jnp.float16) for f in (f1, f2, f3)]


def call(body, out, args, flops, scalars=0):
    return pl.pallas_call(
        body,
        out_shape=out,
        in_specs=[SMEM] * scalars + [VMEM] * (len(args) - scalars),
        out_specs=jax.tree.map(lambda _: VMEM, out),
        compiler_params=pltpu.CompilerParams(vmem_limit_bytes=12 * 2**20),
        cost_estimate=pl.CostEstimate(flops=flops, bytes_accessed=2**20, transcendentals=0),
    )(*args)


def columns(own, code, got):
    lines = own.shape[0] // HD

    def norms_of(ref, first):
        u = ref[first : first + lines, :] + (
            ref[first + lines : first + 2 * lines, :]
            + ref[first + 2 * lines : first + 3 * lines, :]
        ) * (1.0 / STEPS)
        return jnp.exp(u * LN2)

    norms = [norms_of(g, own.shape[0]) for g in got]
    total = norms_of(code, 0) + norms[0] + norms[1] + norms[2]
    scale = lax.rsqrt(total / D + 1e-06)
    ups = [jnp.sqrt(n) * scale * (1.0 / LIFT) for n in norms]
    rest = jnp.zeros((HD - 4 * lines, HD), f32)
    return jnp.concatenate([scale, *ups, rest], axis=0).T


def finished(k, cols, own, got, bias, cosine, sine):
    at = slice(k * HD, (k + 1) * HD)
    lines = own.shape[0] // HD
    value = own[at, :] * cols[:, k : k + 1] + bias[...]
    for d, g in enumerate(got):
        j = (d + 1) * lines + k
        value += g[at, :] * cols[:, j : j + 1]
    return value * cosine[at, :] + pltpu.roll(value, HD // 2, 1) * sine[at, :]


def turn_kernel(arrived, own, code, g1, g2, g3, bias, cosine, sine, out, cache, held, sems):
    take = pltpu.make_async_copy(arrived, held, sems.at[0])
    take.start()
    cols = columns(own, code, (g1, g2, g3))
    give = pltpu.make_async_copy(held, cache, sems.at[1])
    for k in range(own.shape[0] // HD):
        value = finished(k, cols, own, (g1, g2, g3), bias, cosine, sine)
        out[k * HD : (k + 1) * HD, :] = value.astype(out.dtype)
        if k == 0:
            take.wait()
            give.start()
    give.wait()


def stored_kernel(owner, valid, own, code, g1, g2, g3, bias, cosine, sine, out):
    row = lax.broadcasted_iota(jnp.int32, (BLK, HD), 0)
    out[...] = jnp.zeros(out.shape, out.dtype)
    cols = columns(own, code, (g1, g2, g3))
    for k in range(own.shape[0] // HD):
        value = finished(k, cols, own, (g1, g2, g3), bias, cosine, sine)
        for h in range(HD // BLK):
            b = k * (HD // BLK) + h
            kept = jnp.where(row < valid[b], value[h * BLK : (h + 1) * BLK], 0.0)
            out[owner[b]] = kept.astype(out.dtype)


def tables(positions, is_key):
    half = HD // 2
    freq = jnp.exp(
        -jnp.log(jnp.float32(1000000.0)) * (jnp.arange(half).astype(jnp.float32) * 2.0 / HD)
    )
    angle = positions.astype(jnp.float32)[:, None] * jnp.concatenate([freq, freq])[None, :]
    sign = jnp.where(jnp.arange(HD) < half, -1.0, 1.0)
    return (
        jnp.where(is_key, jnp.cos(angle), 1.0),
        jnp.where(is_key, jnp.sin(angle) * sign[None, :], 0.0),
    )


def shards(
    stored_hidden,
    block_owner,
    block_valid,
    block_start,
    turn_hidden,
    turn_position,
    kv_weight,
    kv_bias,
):
    groups = lax.axis_size("pool")
    me = lax.axis_index("mp")
    is_key = me * HD < KVD
    count, local = stored_hidden.shape
    bias = kv_bias[None, :]

    chunks = kv_weight.reshape(NZ, NX, NC, local, HD)

    positions = (block_start[:, None] + jnp.arange(BLK)[None, :]).reshape(-1)
    s_tables = tables(positions, is_key)
    t_tables = tables(turn_position, is_key)

    s1 = along_x(stored_hidden, 1)
    s3 = along_x(stored_hidden, 3)
    parts = slices(chunks)
    held = anchor(bias, parts[0])
    w1, w2, w3 = parts
    w2 = across(w2, 2)
    w3 = outward(w3, groups)
    s1, s3, w1 = lax.optimization_barrier((s1, s3, w1))
    w1 = across(w1, 1)
    weights = [w1, w2, w3]
    half = count // 2
    s1, s3, s_tables, t_tables = lax.optimization_barrier((s1, s3, s_tables, t_tables))
    s2a = along_x(s1[:half], 1)
    s2b = along_x(s3[half:], 3)
    row, s1, s3, bias = lax.optimization_barrier((turn_hidden, s1, s3, held))
    t1 = along_x(row, 1)
    t3 = along_x(row, 3)
    partly = (
        jax.ShapeDtypeStruct((count, 4 * HD), f32),
        jax.ShapeDtypeStruct((count, HD), f32),
    )
    acc, sq = multiply(first_kernel, (stored_hidden, s1, s3), chunks, weights, (), partly, 16,1)
    last = functools.partial(last_kernel, 2)
    parts = multiply(last, (s2a, s2b), chunks, weights, (acc, sq), outputs(count), 16,1)
    s_own, s_code, s_sent = half_width(parts)
    s_g1, s_g2, s_g3 = [across(v, e) for e, v in zip((1, 2, 3), s_sent)]
    row, s_code = lax.optimization_barrier((turn_hidden, s_code))
    t2 = along_x(row, 2)
    t_rows = [turn_hidden, t1, t2, t3]

    args = [v.astype(f32) for v in (s_g1, s_g2, s_g3)]
    outgoing = call(
        stored_kernel,
        jax.ShapeDtypeStruct((groups, BLK, HD), jnp.bfloat16),
        (block_owner, block_valid, s_own, s_code, *args, bias, *s_tables),
        2**20,
        2,
    )
    arrived = lax.all_to_all(outgoing, "pool", split_axis=0, concat_axis=0, tiled=True)

    t_rows[0], outgoing = lax.optimization_barrier((t_rows[0], outgoing))
    parts = multiply(whole_kernel, t_rows, chunks, weights, (), outputs(count), 16,2)
    t_own, t_code, t_sent = half_width(parts)
    t1, t2, t3 = t_sent
    t_got = across(t1, 1), across(t2, 2), across(t3, 3)
    args = [v.astype(f32) for v in t_got]
    args = (arrived, t_own, t_code, *args, bias, *t_tables)
    cache = jax.ShapeDtypeStruct(arrived.shape, arrived.dtype)
    turn_kv, restored = pl.pallas_call(
        turn_kernel,
        out_shape=(jax.ShapeDtypeStruct((count, HD), jnp.bfloat16), cache),
        in_specs=[pl.BlockSpec(memory_space=pl.ANY)] + [VMEM] * (len(args) - 1),
        out_specs=(VMEM, pl.BlockSpec(memory_space=pl.ANY)),
        scratch_shapes=[pltpu.VMEM(arrived.shape, arrived.dtype), pltpu.SemaphoreType.DMA((2,))],
        compiler_params=pltpu.CompilerParams(vmem_limit_bytes=12 * 2**20),
        cost_estimate=pl.CostEstimate(flops=2**20, bytes_accessed=2**20, transcendentals=0),
    )(*args)
    return (restored.reshape(groups * BLK, HD), turn_kv)


def solution(mesh):
    placed = (
        P("pool", "mp"),
        P("pool"),
        P("pool"),
        P("pool"),
        P("pool", "mp"),
        P("pool"),
        P(None, "mp"),
        P("mp"),
    )
    return jax.shard_map(
        shards,
        mesh=mesh,
        in_specs=placed,
        out_specs=(P("pool", "mp"), P("pool", "mp")),
        check_vma=False,
    )
```

time: 77.9 us -> 72.4 us (0.929)
  the two profiles are of different devices: /device:TPU:32 before, /device:TPU:1 now
where the time goes in v3:
time: 72.4 us; the launch traced here: 72.1 us
  starting transfers between devices  31.1 us (43%)
  waiting for transfers between devices  17.8 us (25%)
  Pallas kernels  16.1 us (22%)
  other arithmetic  3.09 us (4%)
  local copies, waits for them, and re-layouts  2.86 us (4%)
  between operations  1.18 us (2%)
    ppermute x8, waiting for transfers between devices, across(): lax.ppermute(v, 'mp', pairs(lambda z, x, c: (z ^ e // NC, x, c ^ e % NC)))  12.6 us
    all_to_all x1, starting transfers between devices, shards(): lax.all_to_all(outgoing, 'pool', split_axis=0, concat_axis=0, tiled=True)  10.1 us
    pallas_call x3, Pallas kernels, multiply(): pl.pallas_call(body, out_shape=out, in_specs=[HBM] * (len(rows) + 4) + [V...  9.71 us
    ppermute x7, starting transfers between devices, along_x(): return lax.ppermute(v, 'mp', pairs(lambda z, x, c: (z, (x + d) % NX, c)))  8.21 us
    ppermute x8, starting transfers between devices, across(): lax.ppermute(v, 'mp', pairs(lambda z, x, c: (z ^ e // NC, x, c ^ e % NC)))  6.66 us
    ppermute x1, starting transfers between devices, outward(): return lax.ppermute(v, ('pool', 'mp'), moves)  6.07 us
    ppermute x1, waiting for transfers between devices, outward(): return lax.ppermute(v, ('pool', 'mp'), moves)  5.18 us
    unnamed x36, local copies, waits for them, and re-layouts  2.75 us
  transfers between devices with their start and end apart: 17, of which 6 were waited for; matrix products, arithmetic and copies ran while one was open for 4% of the time, Pallas kernels for 19%

profile of v3, /device:TPU:1, one launch (start us, length us, event | category | flops | bytes accessed | tf_op | source)
XLA Modules:
  0.0 72.1 jit_solution(12671579895037686608)
XLA Ops:
  0.7 2.1 %collective-permute-start = (bf16[512,512]{1,0:T(8,128)(2,1)}, bf16[512,512]{1,0:T(8,128)(2,1)S(1)}, u32[]{:S(2)}, u32[]{:S(2)}) collective-permute-start(bf16[512,512]{1,0:T(8,128)(2,1)} %r0.1), channel_id=1, source_target_pairs={{0,2},{1,3},{2,4},{3,5},{4,6},{5,7},{6,0},{7,1},{8,10},{9,11},{10,... | collective-permute-start | bytes 1572872 | tf_op jit(solution)/shard_map/ppermute | solution.py:55
  2.8 1.4 %collective-permute-start.1 = (bf16[512,512]{1,0:T(8,128)(2,1)}, bf16[512,512]{1,0:T(8,128)(2,1)S(1)}, u32[]{:S(2)}, u32[]{:S(2)}) collective-permute-start(bf16[512,512]{1,0:T(8,128)(2,1)} %r0.1), channel_id=1, source_target_pairs={{0,6},{1,7},{2,0},{3,1},{4,2},{5,3},{6,4},{7,5},{8,14},{9,15},{10,... | collective-permute-start | bytes 1572872 | tf_op jit(solution)/shard_map/ppermute | solution.py:55
  4.1 2.7 %shard_map.95 = (bf16[4,512,128]{2,1,0:T(8,128)(2,1)}, bf16[4,512,128]{2,1,0:T(8,128)(2,1)}, bf16[4,512,128]{2,1,0:T(8,128)(2,1)}) custom-call(bf16[2,4,2,512,128]{4,3,2,1,0:T(8,128)(2,1)} %bitcast.3), custom_call_target="tpu_custom_call" | custom-call | bytes 2097152 | tf_op jit(solution)/shard_map/pallas_call | solution.py:89
  6.9 1.8 %collective-permute-start.5 = (bf16[4,512,128]{2,1,0:T(8,128)(2,1)}, bf16[4,512,128]{2,1,0:T(8,128)(2,1)S(1)}, u32[]{:S(2)}, u32[]{:S(2)}) collective-permute-start(bf16[4,512,128]{2,1,0:T(8,128)(2,1)} %get-tuple-element.41), channel_id=1, source_target_pairs={{0,8},{1,9},{2,10},{3,11},{4,12},{5,13},{6,14},{7,15},{8,0},{9,1},... | collective-permute-start | bytes 1572872 | tf_op jit(solution)/shard_map/ppermute | solution.py:39
  8.7 6.1 %collective-permute-start.6 = (bf16[4,512,128]{2,1,0:T(8,128)(2,1)}, bf16[4,512,128]{2,1,0:T(8,128)(2,1)S(1)}, u32[]{:S(2)}, u32[]{:S(2)}) collective-permute-start(bf16[4,512,128]{2,1,0:T(8,128)(2,1)} %get-tuple-element.42), channel_id=1, source_target_pairs={{0,201},{1,200},{2,203},{3,202},{4,205},{5,204},{6,207},{7,206},{8... | collective-permute-start | bytes 1572872 | tf_op jit(solution)/shard_map/ppermute | solution.py:51
  14.8 0.1 add_convert_fusion
  14.8 0.1 convert_element_type.56
  14.9 0.1 compare_select_fusion
  15.0 2.7 %fusion.5 = (f32[512,128]{1,0:T(8,128)S(1)}, f32[512,128]{1,0:T(8,128)}, f32[512,128]{1,0:T(8,128)S(1)}, f32[512,128]{1,0:T(8,128)S(1)}) fusion(f32[512]{0:T(512)S(1)} %convert_element_type.58, f32[128]{0:T(128)S(1)} %get-tuple-element.74, f32[128]{0:T(128)S(1)} %get-tuple-element.75, pred[]{:T(512)S(6)} %lt.13, f32[512]{0:T(512)S(1)} %convert_element_type.56), kind=kLoop, calls=%fused_computation.9 | loop fusion | flops 524288 | bytes 1053697 | tf_op jit(solution)/shard_map/jit(_where)/select_n | solution.py:324
  17.7 0.0 collective-permute-done.r1
  17.7 0.1 collective-permute-start.4
  17.8 0.8 %collective-permute-start.2 = (bf16[256,512]{1,0:T(8,128)(2,1)S(1)}, bf16[256,512]{1,0:T(8,128)(2,1)S(1)}, u32[]{:S(2)}, u32[]{:S(2)}) collective-permute-start(bf16[256,512]{1,0:T(8,128)(2,1)S(1)} %slice.6), channel_id=1, source_target_pairs={{0,2},{1,3},{2,4},{3,5},{4,6},{5,7},{6,0},{7,1},{8,10},{9,11},{10,... | collective-permute-start | bytes 786440 | tf_op jit(solution)/shard_map/ppermute | solution.py:55
  18.7 2.0 %collective-permute-start.3 = (bf16[256,512]{1,0:T(8,128)(2,1)S(1)}, bf16[256,512]{1,0:T(8,128)(2,1)S(1)}, u32[]{:S(2)}, u32[]{:S(2)}) collective-permute-start(bf16[256,512]{1,0:T(8,128)(2,1)S(1)} %slice.7), channel_id=1, source_target_pairs={{0,6},{1,7},{2,0},{3,1},{4,2},{5,3},{6,4},{7,5},{8,14},{9,15},{10,... | collective-permute-start | bytes 786440 | tf_op jit(solution)/shard_map/ppermute | solution.py:55
  20.7 0.0 copy-start
  20.7 0.0 copy-start.9
  20.8 0.0 collective-permute-done.5.w2.refs_4_
  20.8 0.1 collective-permute-start.10
  20.9 5.2 %collective-permute-done.6.w3.refs_5_ = bf16[4,512,128]{2,1,0:T(8,128)(2,1)S(1)} collective-permute-done((bf16[4,512,128]{2,1,0:T(8,128)(2,1)}, bf16[4,512,128]{2,1,0:T(8,128)(2,1)S(1)}, u32[]{:S(2)}, u32[]{:S(2)}) %collective-permute-start.6) | collective-permute-done | bytes 524320 | tf_op jit(solution)/shard_map/ppermute | solution.py:51
  26.1 1.3 %collective-permute-start.12 = (bf16[512,512]{1,0:T(8,128)(2,1)}, bf16[512,512]{1,0:T(8,128)(2,1)}, u32[]{:S(2)}, u32[]{:S(2)}) collective-permute-start(bf16[512,512]{1,0:T(8,128)(2,1)} %r0.2), channel_id=1, source_target_pairs={{0,6},{1,7},{2,0},{3,1},{4,2},{5,3},{6,4},{7,5},{8,14},{9,15},{10,... | collective-permute-start | bytes 1572872 | tf_op jit(solution)/shard_map/ppermute | solution.py:55
  27.4 3.9 %shard_map.97 = (f32[512,512]{1,0:T(8,128)S(1)}, f32[512,128]{1,0:T(8,128)S(1)}) custom-call(bf16[512,512]{1,0:T(8,128)(2,1)S(1)} %copy-done.9, bf16[512,512]{1,0:T(8,128)(2,1)S(1)} %copy-done.4, bf16[512,512]{1,0:T(8,128)(2,1)S(1)} %copy-done.6, bf16[2,4,2,512,128]{4,3,2,1,0:T(8,128)(2,1)S(1)} %bitcast.4, ...), custom_call_target="tpu_custom_call" | custom-call | flops 1073741824 | bytes 4194304 | tf_op jit(solution)/shard_map/pallas_call | solution.py:223
  31.3 0.0 collective-permute-done.2.refs_0_
  31.3 0.0 collective-permute-done.3.refs_1_
  31.3 1.4 %shard_map.98 = (f32[512,128]{1,0:T(8,128)S(1)}, f32[528,128]{1,0:T(8,128)S(1)}, f32[528,128]{1,0:T(8,128)S(1)}, f32[528,128]{1,0:T(8,128)S(1)}, f32[16,128]{1,0:T(8,128)S(1)}) custom-call(bf16[256,512]{1,0:T(8,128)(2,1)S(1)} %collective-permute-done.2.refs_0_, bf16[256,512]{1,0:T(8,128)(2,1)S(1)} %collective-permute-done.3.refs_1_, ...), custom_call_target="tpu_custom_call" | custom-call | flops 1073741824 | bytes 4194304 | tf_op jit(solution)/shard_map/pallas_call | solution.py:223
  32.7 0.0 copy-start.12
  32.7 0.0 copy-start.13
  32.7 0.5 collective-permute-start.11
  33.3 0.2 collective-permute-start.7
  33.5 0.9 %collective-permute-start.8 = (f16[528,128]{1,0:T(8,128)(2,1)S(1)}, f16[528,128]{1,0:T(8,128)(2,1)S(1)}, u32[]{:S(2)}, u32[]{:S(2)}) collective-permute-start(f16[528,128]{1,0:T(8,128)(2,1)S(1)} %convert_element_type.61), channel_id=1, source_target_pairs={{0,8},{1,9},{2,10},{3,11},{4,12},{5,13},{6,14},{7,15},{8,0},{9,1},... | collective-permute-start | bytes 405512 | tf_op jit(solution)/shard_map/ppermute | solution.py:39
  34.5 0.3 collective-permute-done.7
  34.7 1.2 %collective-permute-start.9 = (f16[528,128]{1,0:T(8,128)(2,1)S(1)}, f16[528,128]{1,0:T(8,128)(2,1)S(1)}, u32[]{:S(2)}, u32[]{:S(2)}) collective-permute-start(f16[528,128]{1,0:T(8,128)(2,1)S(1)} %convert_element_type.63), channel_id=1, source_target_pairs={{0,9},{1,8},{2,11},{3,10},{4,13},{5,12},{6,15},{7,14},{8,1},{9,0},... | collective-permute-start | bytes 405512 | tf_op jit(solution)/shard_map/ppermute | solution.py:39
  35.9 2.6 %collective-permute-done.8 = f16[528,128]{1,0:T(8,128)(2,1)S(1)} collective-permute-done((f16[528,128]{1,0:T(8,128)(2,1)S(1)}, f16[528,128]{1,0:T(8,128)(2,1)S(1)}, u32[]{:S(2)}, u32[]{:S(2)}) %collective-permute-start.8) | collective-permute-done | bytes 135200 | tf_op jit(solution)/shard_map/ppermute | solution.py:39
  38.6 3.7 %collective-permute-done.9 = f16[528,128]{1,0:T(8,128)(2,1)S(1)} collective-permute-done((f16[528,128]{1,0:T(8,128)(2,1)S(1)}, f16[528,128]{1,0:T(8,128)(2,1)S(1)}, u32[]{:S(2)}, u32[]{:S(2)}) %collective-permute-start.9) | collective-permute-done | bytes 135200 | tf_op jit(solution)/shard_map/ppermute | solution.py:39
  42.3 1.3 %shard_map.99 = bf16[16,64,128]{2,1,0:T(8,128)(2,1)S(1)} custom-call(s32[8]{0:T(128)S(1)} %copy-done.12, s32[8]{0:T(128)S(1)} %copy-done.13, f32[512,128]{1,0:T(8,128)S(1)} %get-tuple-element.47.own, f32[16,128]{1,0:T(8,128)S(1)} %get-tuple-element.49.code, f32[528,128]{1,0:T(8,128)S(1)} %convert_element_type.60.g1, f32[528,128]{1,0:T(8,128)S(1)} %convert_element_type.62.g2, ...), custom_call_target="tpu_custom_call" | custom-call | flops 1048576 | bytes 1048576 | tf_op jit(solution)/shard_map/pallas_call | solution.py:251
  43.6 0.7 copy-done.8
  44.3 10.1 %all-to-all-start = ((bf16[16,64,128]{2,1,0:T(8,128)(2,1)}), bf16[16,64,128]{2,1,0:T(8,128)(2,1)}, u32[]{:S(2)}, u32[]{:S(2)}) async-start(bf16[16,64,128]{2,1,0:T(8,128)(2,1)} %copy-done.8), calls=%async_computation | async-start | bytes 524288 | tf_op jit(solution)/shard_map/all_to_all | solution.py:388
  54.4 0.0 collective-permute-done.10.r1
  54.4 0.0 collective-permute-done.12.r3
  54.5 1.0 %copy-done.2 = bf16[4,512,128]{2,1,0:T(8,128)(2,1)S(1)} copy-done((bf16[4,512,128]{2,1,0:T(8,128)(2,1)S(1)}, bf16[4,512,128]{2,1,0:T(8,128)(2,1)}, u32[]{:S(2)}) %copy-start.2) | copy-done | bytes 524312
  55.5 4.5 %shard_map.100 = (f32[512,128]{1,0:T(8,128)S(1)}, f32[528,128]{1,0:T(8,128)S(1)}, f32[528,128]{1,0:T(8,128)S(1)}, f32[528,128]{1,0:T(8,128)S(1)}, f32[16,128]{1,0:T(8,128)S(1)}) custom-call(bf16[512,512]{1,0:T(8,128)(2,1)} %r0.2, bf16[512,512]{1,0:T(8,128)(2,1)} %collective-permute-done.10.r1, bf16[512,512]{1,0:T(8,128)(2,1)} %collective-permute-done.11.r2, ...), custom_call_target="tpu_custom_call" | custom-call | flops 2147483648 | bytes 4194304 | tf_op jit(solution)/shard_map/pallas_call | solution.py:223
  60.0 0.0 copy-start.7
  60.0 0.3 collective-permute-start.13
  60.3 0.8 %collective-permute-start.14 = (f16[528,128]{1,0:T(8,128)(2,1)S(1)}, f16[528,128]{1,0:T(8,128)(2,1)S(1)}, u32[]{:S(2)}, u32[]{:S(2)}) collective-permute-start(f16[528,128]{1,0:T(8,128)(2,1)S(1)} %convert_element_type.67), channel_id=1, source_target_pairs={{0,8},{1,9},{2,10},{3,11},{4,12},{5,13},{6,14},{7,15},{8,0},{9,1},... | collective-permute-start | bytes 405512 | tf_op jit(solution)/shard_map/ppermute | solution.py:39
  61.1 1.3 %collective-permute-start.15 = (f16[528,128]{1,0:T(8,128)(2,1)S(1)}, f16[528,128]{1,0:T(8,128)(2,1)S(1)}, u32[]{:S(2)}, u32[]{:S(2)}) collective-permute-start(f16[528,128]{1,0:T(8,128)(2,1)S(1)} %convert_element_type.69), channel_id=1, source_target_pairs={{0,9},{1,8},{2,11},{3,10},{4,13},{5,12},{6,15},{7,14},{8,1},{9,0},... | collective-permute-start | bytes 405512 | tf_op jit(solution)/shard_map/ppermute | solution.py:39
  62.5 0.0 collective-permute-done.13
  62.5 2.8 %collective-permute-done.14 = f16[528,128]{1,0:T(8,128)(2,1)S(1)} collective-permute-done((f16[528,128]{1,0:T(8,128)(2,1)S(1)}, f16[528,128]{1,0:T(8,128)(2,1)S(1)}, u32[]{:S(2)}, u32[]{:S(2)}) %collective-permute-start.14) | collective-permute-done | bytes 135200 | tf_op jit(solution)/shard_map/ppermute | solution.py:39
  65.3 3.2 %collective-permute-done.15 = f16[528,128]{1,0:T(8,128)(2,1)S(1)} collective-permute-done((f16[528,128]{1,0:T(8,128)(2,1)S(1)}, f16[528,128]{1,0:T(8,128)(2,1)S(1)}, u32[]{:S(2)}, u32[]{:S(2)}) %collective-permute-start.15) | collective-permute-done | bytes 135200 | tf_op jit(solution)/shard_map/ppermute | solution.py:39
  68.6 0.9 %copy-done.11 = f32[512,128]{1,0:T(8,128)S(1)} copy-done((f32[512,128]{1,0:T(8,128)S(1)}, f32[512,128]{1,0:T(8,128)}, u32[]{:S(2)}) %copy-start.11) | copy-done | bytes 262168
  69.6 2.3 %shard_map.101 = (bf16[512,128]{1,0:T(8,128)(2,1)}, bf16[16,64,128]{2,1,0:T(8,128)(2,1)}) custom-call(bf16[16,64,128]{2,1,0:T(8,128)(2,1)} %all-to-all-done.arrived, f32[512,128]{1,0:T(8,128)S(1)} %copy-done.11, f32[16,128]{1,0:T(8,128)S(1)} %get-tuple-element.60.code, f32[528,128]{1,0:T(8,128)S(1)} %convert_element_type.66.g1, ...), custom_call_target="tpu_custom_call" | custom-call | flops 1048576 | bytes 1048576 | tf_op jit(solution)/shard_map/pallas_call | solution.py:398
  (49 shorter events, 0.4 us)
Async XLA Ops:
  0.6 14.1 %copy-start.17 = (s32[8]{0:T(128)S(1)}, s32[8]{0:T(128)}, u32[]{:S(2)}) copy-start(s32[8]{0:T(128)} %param.11) | copy-start | bytes 100
  0.6 14.3 %copy-start.16 = (s32[512]{0:T(512)S(1)}, s32[512]{0:T(512)}, u32[]{:S(2)}) copy-start(s32[512]{0:T(512)} %param.13) | copy-start | bytes 6148
  0.7 17.1 %collective-permute-start = (bf16[512,512]{1,0:T(8,128)(2,1)}, bf16[512,512]{1,0:T(8,128)(2,1)S(1)}, u32[]{:S(2)}, u32[]{:S(2)}) collective-permute-start(bf16[512,512]{1,0:T(8,128)(2,1)} %r0.1), channel_id=1, source_target_pairs={{0,2},{1,3},{2,4},{3,5},{4,6},{5,7},{6,0},{7,1},{8,10},{9,11},{10,... | collective-permute-start | bytes 1572872 | tf_op jit(solution)/shard_map/ppermute | solution.py:55
  2.8 14.9 %collective-permute-start.1 = (bf16[512,512]{1,0:T(8,128)(2,1)}, bf16[512,512]{1,0:T(8,128)(2,1)S(1)}, u32[]{:S(2)}, u32[]{:S(2)}) collective-permute-start(bf16[512,512]{1,0:T(8,128)(2,1)} %r0.1), channel_id=1, source_target_pairs={{0,6},{1,7},{2,0},{3,1},{4,2},{5,3},{6,4},{7,5},{8,14},{9,15},{10,... | collective-permute-start | bytes 1572872 | tf_op jit(solution)/shard_map/ppermute | solution.py:55
  4.1 16.6 %copy-start.15 = (f32[128]{0:T(128)S(1)}, f32[128]{0:T(128)}, u32[]{:S(2)}) copy-start(f32[128]{0:T(128)} %param.15) | copy-start | bytes 1540
  6.9 13.9 %collective-permute-start.5 = (bf16[4,512,128]{2,1,0:T(8,128)(2,1)}, bf16[4,512,128]{2,1,0:T(8,128)(2,1)S(1)}, u32[]{:S(2)}, u32[]{:S(2)}) collective-permute-start(bf16[4,512,128]{2,1,0:T(8,128)(2,1)} %get-tuple-element.41), channel_id=1, source_target_pairs={{0,8},{1,9},{2,10},{3,11},{4,12},{5,13},{6,14},{7,15},{8,0},{9,1},... | collective-permute-start | bytes 1572872 | tf_op jit(solution)/shard_map/ppermute | solution.py:39
  8.7 17.4 %collective-permute-start.6 = (bf16[4,512,128]{2,1,0:T(8,128)(2,1)}, bf16[4,512,128]{2,1,0:T(8,128)(2,1)S(1)}, u32[]{:S(2)}, u32[]{:S(2)}) collective-permute-start(bf16[4,512,128]{2,1,0:T(8,128)(2,1)} %get-tuple-element.42), channel_id=1, source_target_pairs={{0,201},{1,200},{2,203},{3,202},{4,205},{5,204},{6,207},{7,206},{8... | collective-permute-start | bytes 1572872 | tf_op jit(solution)/shard_map/ppermute | solution.py:51
  14.9 5.8 %copy-start.14 = (bf16[4,512,128]{2,1,0:T(8,128)(2,1)S(1)}, bf16[4,512,128]{2,1,0:T(8,128)(2,1)}, u32[]{:S(2)}) copy-start(bf16[4,512,128]{2,1,0:T(8,128)(2,1)} %get-tuple-element.40.after) | copy-start | bytes 1572868
  17.7 3.0 %copy-start.3 = (bf16[512,512]{1,0:T(8,128)(2,1)}, bf16[512,512]{1,0:T(8,128)(2,1)S(1)}, u32[]{:S(2)}) copy-start(bf16[512,512]{1,0:T(8,128)(2,1)S(1)} %collective-permute-done.r1) | copy-start | bytes 1572868
  17.7 3.0 %copy-start.5 = (bf16[512,512]{1,0:T(8,128)(2,1)}, bf16[512,512]{1,0:T(8,128)(2,1)S(1)}, u32[]{:S(2)}) copy-start(bf16[512,512]{1,0:T(8,128)(2,1)S(1)} %collective-permute-done.1.r3) | copy-start | bytes 1572868
  17.7 9.6 %collective-permute-start.4 = (bf16[4,512,128]{2,1,0:T(8,128)(2,1)}, bf16[4,512,128]{2,1,0:T(8,128)(2,1)S(1)}, u32[]{:S(2)}, u32[]{:S(2)}) collective-permute-start(bf16[4,512,128]{2,1,0:T(8,128)(2,1)} %get-tuple-element.40.after), channel_id=1, source_target_pairs={{0,1},{1,0},{2,3},{3,2},{4,5},{5,4},{6,7},{7,6},{8,9},{9,8},{10,11... | collective-permute-start | bytes 1572872 | tf_op jit(solution)/shard_map/ppermute | solution.py:39
  17.8 13.4 %collective-permute-start.2 = (bf16[256,512]{1,0:T(8,128)(2,1)S(1)}, bf16[256,512]{1,0:T(8,128)(2,1)S(1)}, u32[]{:S(2)}, u32[]{:S(2)}) collective-permute-start(bf16[256,512]{1,0:T(8,128)(2,1)S(1)} %slice.6), channel_id=1, source_target_pairs={{0,2},{1,3},{2,4},{3,5},{4,6},{5,7},{6,0},{7,1},{8,10},{9,11},{10,... | collective-permute-start | bytes 786440 | tf_op jit(solution)/shard_map/ppermute | solution.py:55
  18.7 12.6 %collective-permute-start.3 = (bf16[256,512]{1,0:T(8,128)(2,1)S(1)}, bf16[256,512]{1,0:T(8,128)(2,1)S(1)}, u32[]{:S(2)}, u32[]{:S(2)}) collective-permute-start(bf16[256,512]{1,0:T(8,128)(2,1)S(1)} %slice.7), channel_id=1, source_target_pairs={{0,6},{1,7},{2,0},{3,1},{4,2},{5,3},{6,4},{7,5},{8,14},{9,15},{10,... | collective-permute-start | bytes 786440 | tf_op jit(solution)/shard_map/ppermute | solution.py:55
  20.7 6.6 %copy-start = (bf16[8192,128]{1,0:T(8,128)(2,1)S(1)}, bf16[8192,128]{1,0:T(8,128)(2,1)}, u32[]{:S(2)}) copy-start(bf16[8192,128]{1,0:T(8,128)(2,1)} %param.14) | copy-start | bytes 6291460
  20.7 6.6 %copy-start.4 = (bf16[512,512]{1,0:T(8,128)(2,1)S(1)}, bf16[512,512]{1,0:T(8,128)(2,1)}, u32[]{:S(2)}) copy-start(bf16[512,512]{1,0:T(8,128)(2,1)} %copy-done.3) | copy-start | bytes 1572868
  20.7 6.6 %copy-start.6 = (bf16[512,512]{1,0:T(8,128)(2,1)S(1)}, bf16[512,512]{1,0:T(8,128)(2,1)}, u32[]{:S(2)}) copy-start(bf16[512,512]{1,0:T(8,128)(2,1)} %copy-done.5) | copy-start | bytes 1572868
  20.7 6.6 %copy-start.9 = (bf16[512,512]{1,0:T(8,128)(2,1)S(1)}, bf16[512,512]{1,0:T(8,128)(2,1)}, u32[]{:S(2)}) copy-start(bf16[512,512]{1,0:T(8,128)(2,1)} %r0.1) | copy-start | bytes 1572868
  20.8 33.6 %collective-permute-start.10 = (bf16[512,512]{1,0:T(8,128)(2,1)}, bf16[512,512]{1,0:T(8,128)(2,1)}, u32[]{:S(2)}, u32[]{:S(2)}) collective-permute-start(bf16[512,512]{1,0:T(8,128)(2,1)} %r0.2), channel_id=1, source_target_pairs={{0,2},{1,3},{2,4},{3,5},{4,6},{5,7},{6,0},{7,1},{8,10},{9,11},{10,... | collective-permute-start | bytes 1572872 | tf_op jit(solution)/shard_map/ppermute | solution.py:55
  26.1 28.4 %collective-permute-start.12 = (bf16[512,512]{1,0:T(8,128)(2,1)}, bf16[512,512]{1,0:T(8,128)(2,1)}, u32[]{:S(2)}, u32[]{:S(2)}) collective-permute-start(bf16[512,512]{1,0:T(8,128)(2,1)} %r0.2), channel_id=1, source_target_pairs={{0,6},{1,7},{2,0},{3,1},{4,2},{5,3},{6,4},{7,5},{8,14},{9,15},{10,... | collective-permute-start | bytes 1572872 | tf_op jit(solution)/shard_map/ppermute | solution.py:55
  27.4 3.9 %copy-start.1 = (bf16[4,512,128]{2,1,0:T(8,128)(2,1)}, bf16[4,512,128]{2,1,0:T(8,128)(2,1)S(1)}, u32[]{:S(2)}) copy-start(bf16[4,512,128]{2,1,0:T(8,128)(2,1)S(1)} %collective-permute-done.4.w1.refs_3_) | copy-start | bytes 1572868
  32.7 9.6 %copy-start.12 = (s32[8]{0:T(128)S(1)}, s32[8]{0:T(128)}, u32[]{:S(2)}) copy-start(s32[8]{0:T(128)} %owner.1) | copy-start | bytes 100
  32.7 9.6 %copy-start.13 = (s32[8]{0:T(128)S(1)}, s32[8]{0:T(128)}, u32[]{:S(2)}) copy-start(s32[8]{0:T(128)} %valid.1) | copy-start | bytes 100
  32.7 21.7 %collective-permute-start.11 = (bf16[512,512]{1,0:T(8,128)(2,1)}, bf16[512,512]{1,0:T(8,128)(2,1)}, u32[]{:S(2)}, u32[]{:S(2)}) collective-permute-start(bf16[512,512]{1,0:T(8,128)(2,1)} %r0.2), channel_id=1, source_target_pairs={{0,4},{1,5},{2,6},{3,7},{4,0},{5,1},{6,2},{7,3},{8,12},{9,13},{10,... | collective-permute-start | bytes 1572872 | tf_op jit(solution)/shard_map/ppermute | solution.py:55
  33.3 1.4 %collective-permute-start.7 = (f16[528,128]{1,0:T(8,128)(2,1)S(1)}, f16[528,128]{1,0:T(8,128)(2,1)S(1)}, u32[]{:S(2)}, u32[]{:S(2)}) collective-permute-start(f16[528,128]{1,0:T(8,128)(2,1)S(1)} %convert_element_type.59), channel_id=1, source_target_pairs={{0,1},{1,0},{2,3},{3,2},{4,5},{5,4},{6,7},{7,6},{8,9},{9,8},{10,11... | collective-permute-start | bytes 405512 | tf_op jit(solution)/shard_map/ppermute | solution.py:39
  33.5 5.0 %collective-permute-start.8 = (f16[528,128]{1,0:T(8,128)(2,1)S(1)}, f16[528,128]{1,0:T(8,128)(2,1)S(1)}, u32[]{:S(2)}, u32[]{:S(2)}) collective-permute-start(f16[528,128]{1,0:T(8,128)(2,1)S(1)} %convert_element_type.61), channel_id=1, source_target_pairs={{0,8},{1,9},{2,10},{3,11},{4,12},{5,13},{6,14},{7,15},{8,0},{9,1},... | collective-permute-start | bytes 405512 | tf_op jit(solution)/shard_map/ppermute | solution.py:39
  34.7 7.5 %collective-permute-start.9 = (f16[528,128]{1,0:T(8,128)(2,1)S(1)}, f16[528,128]{1,0:T(8,128)(2,1)S(1)}, u32[]{:S(2)}, u32[]{:S(2)}) collective-permute-start(f16[528,128]{1,0:T(8,128)(2,1)S(1)} %convert_element_type.63), channel_id=1, source_target_pairs={{0,9},{1,8},{2,11},{3,10},{4,13},{5,12},{6,15},{7,14},{8,1},{9,0},... | collective-permute-start | bytes 405512 | tf_op jit(solution)/shard_map/ppermute | solution.py:39
  43.6 0.7 copy-start.8
  44.3 24.3 %all-to-all-start = ((bf16[16,64,128]{2,1,0:T(8,128)(2,1)}), bf16[16,64,128]{2,1,0:T(8,128)(2,1)}, u32[]{:S(2)}, u32[]{:S(2)}) async-start(bf16[16,64,128]{2,1,0:T(8,128)(2,1)} %copy-done.8), calls=%async_computation | async-start | bytes 524288 | tf_op jit(solution)/shard_map/all_to_all | solution.py:388
  54.5 1.0 %copy-start.2 = (bf16[4,512,128]{2,1,0:T(8,128)(2,1)S(1)}, bf16[4,512,128]{2,1,0:T(8,128)(2,1)}, u32[]{:S(2)}) copy-start(bf16[4,512,128]{2,1,0:T(8,128)(2,1)} %copy-done.1) | copy-start | bytes 1572868
  60.0 5.4 %copy-start.10 = (f32[512,128]{1,0:T(8,128)}, f32[512,128]{1,0:T(8,128)S(1)}, u32[]{:S(2)}) copy-start(f32[512,128]{1,0:T(8,128)S(1)} %get-tuple-element.59.own) | copy-start | bytes 786436
  60.0 8.6 %copy-start.7 = (f32[512,128]{1,0:T(8,128)S(1)}, f32[512,128]{1,0:T(8,128)}, u32[]{:S(2)}) copy-start(f32[512,128]{1,0:T(8,128)} %get-tuple-element.64.cosine) | copy-start | bytes 786436
  60.0 2.5 %collective-permute-start.13 = (f16[528,128]{1,0:T(8,128)(2,1)S(1)}, f16[528,128]{1,0:T(8,128)(2,1)S(1)}, u32[]{:S(2)}, u32[]{:S(2)}) collective-permute-start(f16[528,128]{1,0:T(8,128)(2,1)S(1)} %convert_element_type.65), channel_id=1, source_target_pairs={{0,1},{1,0},{2,3},{3,2},{4,5},{5,4},{6,7},{7,6},{8,9},{9,8},{10,11... | collective-permute-start | bytes 405512 | tf_op jit(solution)/shard_map/ppermute | solution.py:39
  60.3 5.0 %collective-permute-start.14 = (f16[528,128]{1,0:T(8,128)(2,1)S(1)}, f16[528,128]{1,0:T(8,128)(2,1)S(1)}, u32[]{:S(2)}, u32[]{:S(2)}) collective-permute-start(f16[528,128]{1,0:T(8,128)(2,1)S(1)} %convert_element_type.67), channel_id=1, source_target_pairs={{0,8},{1,9},{2,10},{3,11},{4,12},{5,13},{6,14},{7,15},{8,0},{9,1},... | collective-permute-start | bytes 405512 | tf_op jit(solution)/shard_map/ppermute | solution.py:39
  61.1 7.5 %collective-permute-start.15 = (f16[528,128]{1,0:T(8,128)(2,1)S(1)}, f16[528,128]{1,0:T(8,128)(2,1)S(1)}, u32[]{:S(2)}, u32[]{:S(2)}) collective-permute-start(f16[528,128]{1,0:T(8,128)(2,1)S(1)} %convert_element_type.69), channel_id=1, source_target_pairs={{0,9},{1,8},{2,11},{3,10},{4,13},{5,12},{6,15},{7,14},{8,1},{9,0},... | collective-permute-start | bytes 405512 | tf_op jit(solution)/shard_map/ppermute | solution.py:39
  68.6 1.0 %copy-start.11 = (f32[512,128]{1,0:T(8,128)S(1)}, f32[512,128]{1,0:T(8,128)}, u32[]{:S(2)}) copy-start(f32[512,128]{1,0:T(8,128)} %copy-done.10) | copy-start | bytes 786436

commit v4 on v3

--- a/solution.py
+++ b/solution.py
@@ -57,7 +57,7 @@
 
 VMEM = pl.BlockSpec(memory_space=pltpu.VMEM)
 SMEM = pl.BlockSpec(memory_space=pltpu.SMEM)
-HBM = pl.BlockSpec(memory_space=pltpu.HBM)
+ANY = pl.BlockSpec(memory_space=pl.ANY)
 f32 = jnp.float32
 
 
@@ -111,21 +111,10 @@
     )(x, after)
 
 
-def load(w, weights, wv, ws, order):
-    z, x, c = place()
-    waits = {}
-    for j in order:
-        k = lax.rem(x - j + NX, NX)
-        waits[j] = []
-        for e, src in enumerate((w.at[z, k, c], *(v.at[k] for v in weights))):
-            copy = pltpu.make_async_copy(src, wv.at[j, e], ws.at[j * 4 + e])
-            copy.start()
-            waits[j].append(copy)
-    return waits
-
-
-def product(piece, wv, j):
-    both = jnp.concatenate([wv[j, e] for e in range(4)], axis=1)
+def product(piece, j, weights, w0):
+    _, x, _ = place()
+    k = lax.rem(x - j + NX, NX)
+    both = jnp.concatenate([w0[j]] + [w[k] for w in weights], axis=1)
     return jnp.dot(piece, both, preferred_element_type=f32)
 
 
@@ -135,54 +124,52 @@
     return sum(wide[:, g * HD : (g + 1) * HD] for g in range(wide.shape[1] // HD))
 
 
-def first_kernel(r0, r1, r3, w, w1, w2, w3, acc, sq, rv, wv, rs, ws):
+def fetch(w, w0, sems, order):
+    z, x, c = place()
+    copies = {}
+    for j in order:
+        src = w.at[z, lax.rem(x - j + NX, NX), c]
+        copies[j] = pltpu.make_async_copy(src, w0.at[j], sems.at[j])
+        copies[j].start()
+    return copies
+
+
+def first_kernel(w, r0, r1, r3, w1, w2, w3, acc, sq, w0, sems):
     rows = {0: r0, 1: r1, 3: r3}
-    copies = {}
+    copies = fetch(w, w0, sems, rows)
     for j, r in rows.items():
-        copies[j] = pltpu.make_async_copy(r, rv.at[j], rs.at[j])
-        copies[j].start()
-    waits = load(w, (w1, w2, w3), wv, ws, rows)
-    for j in rows:
         copies[j].wait()
-        for copy in waits[j]:
-            copy.wait()
         if j == 0:
-            acc[...] = product(rv[j], wv, j)
-            sq[...] = squared(rv[j])
+            acc[...] = product(r[...], j, (w1, w2, w3), w0)
+            sq[...] = squared(r[...])
         else:
-            acc[...] += product(rv[j], wv, j)
-            sq[...] += squared(rv[j])
-
-
-def last_kernel(count, *refs):
+            acc[...] += product(r[...], j, (w1, w2, w3), w0)
+            sq[...] += squared(r[...])
+
+
+def last_kernel(count, w, *refs):
     pieces, refs = refs[:count], refs[count:]
-    w, w1, w2, w3, acc, sq, own, f1, f2, f3, code, rv, wv, rs, ws = refs
-    size = own.shape[0] // count
-    copies = []
-    for n, r in enumerate(pieces):
-        at = pl.ds(n * size, size)
-        copies.append(pltpu.make_async_copy(r, rv.at[2, at], rs.at[n]))
-        copies[n].start()
-    waits = load(w, (w1, w2, w3), wv, ws, (2,))
-    for copy in copies + waits[2]:
-        copy.wait()
-    total = acc[...] + product(rv[2], wv, 2)
-    pack(total, sq[...] + squared(rv[2]), own, f1, f2, f3, code)
-
-
-def whole_kernel(r0, r1, r2, r3, w, w1, w2, w3, own, f1, f2, f3, code, rv, wv, rs, ws):
-    rows = (r0, r1, r2, r3)
-    copies = []
-    for j, r in enumerate(rows):
-        copies.append(pltpu.make_async_copy(r, rv.at[j], rs.at[j]))
-        copies[j].start()
-    waits = load(w, (w1, w2, w3), wv, ws, range(NX))
+    w1, w2, w3, acc, sq, own, f1, f2, f3, code, w0, sems = refs
+    fetch(w, w0, sems, (2,))[2].wait()
+    piece = jnp.concatenate([r[...] for r in pieces], axis=0)
+    total = acc[...] + product(piece, 2, (w1, w2, w3), w0)
+    pack(total, sq[...] + squared(piece), own, f1, f2, f3, code)
+
+
+def whole_kernel(w, r0, r1, r2, r3, w1, w2, w3, own, f1, f2, f3, code, w0, sems, rv, rs):
+    order = (0, 1, 3, 2)
+    moves = {}
+    for j, r in enumerate((r0, r1, r2, r3)):
+        moves[j] = pltpu.make_async_copy(r, rv.at[j], rs.at[j])
+    moves[0].start()
+    copies = fetch(w, w0, sems, order)
+    for j in order[1:]:
+        moves[j].start()
     total = sq = 0.0
-    for j in range(NX):
+    for j in order:
         copies[j].wait()
-        for copy in waits[j]:
-            copy.wait()
-        total += product(rv[j], wv, j)
+        moves[j].wait()
+        total += product(rv[j], j, (w1, w2, w3), w0)
         sq += squared(rv[j])
     pack(total, sq, own, f1, f2, f3, code)
 
@@ -209,26 +196,22 @@
         f[pl.ds(rows, 16), :] = told
 
 
-def scratch(rows, w):
-    return [
-        pltpu.VMEM((NX,) + rows, w.dtype),
-        pltpu.VMEM((NX, 4) + w.shape[3:], w.dtype),
-        pltpu.SemaphoreType.DMA((NX,)),
-        pltpu.SemaphoreType.DMA((NX * 4,)),
-    ]
-
-
 def multiply(body, rows, w, weights, held, out, grant, cost):
-    count, local = rows[0].shape[0], rows[0].shape[1]
+    stay = body is not whole_kernel
+    moved = [pltpu.VMEM((NX,) + rows[0].shape, w.dtype), pltpu.SemaphoreType.DMA((NX,))]
     return pl.pallas_call(
         body,
         out_shape=out,
-        in_specs=[HBM] * (len(rows) + 4) + [VMEM] * len(held),
+        in_specs=[ANY] + [VMEM if stay else ANY] * len(rows) + [VMEM] * (3 + len(held)),
         out_specs=(VMEM,) * len(out),
-        scratch_shapes=scratch((out[0].shape[0], local), w),
+        scratch_shapes=[
+            pltpu.VMEM((NX,) + w.shape[3:], w.dtype),
+            pltpu.SemaphoreType.DMA((NX,)),
+        ]
+        + ([] if stay else moved),
         compiler_params=pltpu.CompilerParams(vmem_limit_bytes=grant * 2**20),
         cost_estimate=pl.CostEstimate(flops=cost * 2**30, bytes_accessed=2**22, transcendentals=0),
-    )(*rows, w, *weights, *held)
+    )(w, *rows, *weights, *held)
 
 
 def outputs(count):
@@ -276,36 +259,38 @@
     return jnp.concatenate([scale, *ups, rest], axis=0).T
 
 
-def finished(k, cols, own, got, bias, cosine, sine):
+def finished(k, cols, own, got, bias, turns):
     at = slice(k * HD, (k + 1) * HD)
     lines = own.shape[0] // HD
     value = own[at, :] * cols[:, k : k + 1] + bias[...]
     for d, g in enumerate(got):
         j = (d + 1) * lines + k
         value += g[at, :] * cols[:, j : j + 1]
-    return value * cosine[at, :] + pltpu.roll(value, HD // 2, 1) * sine[at, :]
-
-
-def turn_kernel(arrived, own, code, g1, g2, g3, bias, cosine, sine, out, cache, held, sems):
-    take = pltpu.make_async_copy(arrived, held, sems.at[0])
-    take.start()
+    turn = turns[at, :]
+    swapped = pltpu.roll(turn, HD // 2, 1)
+    first = lax.broadcasted_iota(jnp.int32, turn.shape, 1) < HD // 2
+    cosine = jnp.where(first, turn, swapped)
+    sine = jnp.where(first, -swapped, turn)
+    return value * cosine + pltpu.roll(value, HD // 2, 1) * sine
+
+
+def emit_kernel(arrived, cache):
+    cache[...] = arrived[...]
+
+
+def turn_kernel(own, code, g1, g2, g3, bias, turns, out):
     cols = columns(own, code, (g1, g2, g3))
-    give = pltpu.make_async_copy(held, cache, sems.at[1])
     for k in range(own.shape[0] // HD):
-        value = finished(k, cols, own, (g1, g2, g3), bias, cosine, sine)
+        value = finished(k, cols, own, (g1, g2, g3), bias, turns)
         out[k * HD : (k + 1) * HD, :] = value.astype(out.dtype)
-        if k == 0:
-            take.wait()
-            give.start()
-    give.wait()
-
-
-def stored_kernel(owner, valid, own, code, g1, g2, g3, bias, cosine, sine, out):
+
+
+def stored_kernel(owner, valid, own, code, g1, g2, g3, bias, turns, out):
     row = lax.broadcasted_iota(jnp.int32, (BLK, HD), 0)
     out[...] = jnp.zeros(out.shape, out.dtype)
     cols = columns(own, code, (g1, g2, g3))
     for k in range(own.shape[0] // HD):
-        value = finished(k, cols, own, (g1, g2, g3), bias, cosine, sine)
+        value = finished(k, cols, own, (g1, g2, g3), bias, turns)
         for h in range(HD // BLK):
             b = k * (HD // BLK) + h
             kept = jnp.where(row < valid[b], value[h * BLK : (h + 1) * BLK], 0.0)
@@ -318,11 +303,9 @@
         -jnp.log(jnp.float32(1000000.0)) * (jnp.arange(half).astype(jnp.float32) * 2.0 / HD)
     )
     angle = positions.astype(jnp.float32)[:, None] * jnp.concatenate([freq, freq])[None, :]
-    sign = jnp.where(jnp.arange(HD) < half, -1.0, 1.0)
-    return (
-        jnp.where(is_key, jnp.cos(angle), 1.0),
-        jnp.where(is_key, jnp.sin(angle) * sign[None, :], 0.0),
-    )
+    first = (jnp.arange(HD) < half)[None, :]
+    plain = jnp.where(first, 1.0, 0.0)
+    return jnp.where(is_key, jnp.where(first, jnp.cos(angle), jnp.sin(angle)), plain)
 
 
 def shards(
@@ -354,11 +337,11 @@
     w1, w2, w3 = parts
     w2 = across(w2, 2)
     w3 = outward(w3, groups)
-    s1, s3, w1 = lax.optimization_barrier((s1, s3, w1))
+    w1, _ = lax.optimization_barrier((w1, s3))
     w1 = across(w1, 1)
     weights = [w1, w2, w3]
     half = count // 2
-    s1, s3, s_tables, t_tables = lax.optimization_barrier((s1, s3, s_tables, t_tables))
+    s1, s_tables, t_tables = lax.optimization_barrier((s1, s_tables, t_tables))
     s2a = along_x(s1[:half], 1)
     s2b = along_x(s3[half:], 3)
     row, s1, s3, bias = lax.optimization_barrier((turn_hidden, s1, s3, held))
@@ -369,19 +352,19 @@
         jax.ShapeDtypeStruct((count, HD), f32),
     )
     acc, sq = multiply(first_kernel, (stored_hidden, s1, s3), chunks, weights, (), partly, 16,1)
+    row, acc = lax.optimization_barrier((turn_hidden, acc))
+    t2 = along_x(row, 2)
     last = functools.partial(last_kernel, 2)
     parts = multiply(last, (s2a, s2b), chunks, weights, (acc, sq), outputs(count), 16,1)
     s_own, s_code, s_sent = half_width(parts)
     s_g1, s_g2, s_g3 = [across(v, e) for e, v in zip((1, 2, 3), s_sent)]
-    row, s_code = lax.optimization_barrier((turn_hidden, s_code))
-    t2 = along_x(row, 2)
     t_rows = [turn_hidden, t1, t2, t3]
 
     args = [v.astype(f32) for v in (s_g1, s_g2, s_g3)]
     outgoing = call(
         stored_kernel,
         jax.ShapeDtypeStruct((groups, BLK, HD), jnp.bfloat16),
-        (block_owner, block_valid, s_own, s_code, *args, bias, *s_tables),
+        (block_owner, block_valid, s_own, s_code, *args, bias, s_tables),
         2**20,
         2,
     )
@@ -393,17 +376,15 @@
     t1, t2, t3 = t_sent
     t_got = across(t1, 1), across(t2, 2), across(t3, 3)
     args = [v.astype(f32) for v in t_got]
-    args = (arrived, t_own, t_code, *args, bias, *t_tables)
-    cache = jax.ShapeDtypeStruct(arrived.shape, arrived.dtype)
-    turn_kv, restored = pl.pallas_call(
+    shape = jax.ShapeDtypeStruct(arrived.shape, arrived.dtype)
+    restored = call(emit_kernel, shape, (arrived,), 2**20)
+    args[1], restored = lax.optimization_barrier((args[1], restored))
+    turn_kv = call(
         turn_kernel,
-        out_shape=(jax.ShapeDtypeStruct((count, HD), jnp.bfloat16), cache),
-        in_specs=[pl.BlockSpec(memory_space=pl.ANY)] + [VMEM] * (len(args) - 1),
-        out_specs=(VMEM, pl.BlockSpec(memory_space=pl.ANY)),
-        scratch_shapes=[pltpu.VMEM(arrived.shape, arrived.dtype), pltpu.SemaphoreType.DMA((2,))],
-        compiler_params=pltpu.CompilerParams(vmem_limit_bytes=12 * 2**20),
-        cost_estimate=pl.CostEstimate(flops=2**20, bytes_accessed=2**20, transcendentals=0),
-    )(*args)
+        jax.ShapeDtypeStruct((count, HD), jnp.bfloat16),
+        (t_own, t_code, *args, bias, t_tables),
+        2**20,
+    )
     return (restored.reshape(groups * BLK, HD), turn_kv)
 
 

time: 72.4 us -> 67.6 us (0.934)
  Pallas kernels: 16.1 us -> 12.7 us
  starting transfers between devices: 31.1 us -> 29.3 us
    pallas_call x4 -> x3, Pallas kernels: 12 us -> 5.84 us  [multiply(): pl.pallas_call(body, out_shape=out, in_specs=[ANY] + [VMEM if stay else A...]
    all_to_all x1, waiting for transfers between devices: 0.01 us -> 4.84 us  [shards(): lax.all_to_all(outgoing, 'pool', split_axis=0, concat_axis=0, tiled=True)]
    ppermute x8, waiting for transfers between devices: 12.6 us -> 8.93 us  [across(): lax.ppermute(v, 'mp', pairs(lambda z, x, c: (z ^ e // NC, x, c ^ e % NC)))]
    pallas_call x1 -> x3, Pallas kernels: 1.28 us -> 4.16 us  [call(): pl.pallas_call(body, out_shape=out, in_specs=[SMEM] * scalars + [VMEM] *...]
    ppermute x8, starting transfers between devices: 6.66 us -> 5.57 us  [across(): lax.ppermute(v, 'mp', pairs(lambda z, x, c: (z ^ e // NC, x, c ^ e % NC)))]
    ppermute x1, waiting for transfers between devices: 5.18 us -> 4.15 us  [outward(): return lax.ppermute(v, ('pool', 'mp'), moves)]
    unnamed x36 -> x34, local copies, waits for them, and re-layouts: 2.75 us -> 3.08 us
    select_n x2 -> x1, other arithmetic: 2.76 us -> 2.71 us  [tables(): jnp.where(is_key, jnp.where(first, jnp.cos(angle), jnp.sin(angle)), plain)]
  transfers between devices with their start and end apart: 17 -> 17, of which waited for: 6 -> 6; matrix products, arithmetic and copies ran while one was open for 4% -> 5% of each run, Pallas kernels for 19% -> 17%
where the time goes in v4:
time: 67.6 us; the launch traced here: 67.3 us
  starting transfers between devices  29.3 us (43%)
  waiting for transfers between devices  17.9 us (26%)
  Pallas kernels  12.7 us (19%)
  local copies, waits for them, and re-layouts  3.19 us (5%)
  other arithmetic  3.11 us (5%)
  between operations  0.99 us (1%)
    all_to_all x1, starting transfers between devices, shards(): lax.all_to_all(outgoing, 'pool', split_axis=0, concat_axis=0, tiled=True)  9.46 us
    ppermute x8, waiting for transfers between devices, across(): lax.ppermute(v, 'mp', pairs(lambda z, x, c: (z ^ e // NC, x, c ^ e % NC)))  8.93 us
    ppermute x7, starting transfers between devices, along_x(): return lax.ppermute(v, 'mp', pairs(lambda z, x, c: (z, (x + d) % NX, c)))  8.21 us
    ppermute x1, starting transfers between devices, outward(): return lax.ppermute(v, ('pool', 'mp'), moves)  6.07 us
    pallas_call x3, Pallas kernels, multiply(): pl.pallas_call(body, out_shape=out, in_specs=[ANY] + [VMEM if stay else A...  5.84 us
    ppermute x8, starting transfers between devices, across(): lax.ppermute(v, 'mp', pairs(lambda z, x, c: (z ^ e // NC, x, c ^ e % NC)))  5.57 us
    all_to_all x1, waiting for transfers between devices, shards(): lax.all_to_all(outgoing, 'pool', split_axis=0, concat_axis=0, tiled=True)  4.84 us
    pallas_call x3, Pallas kernels, call(): pl.pallas_call(body, out_shape=out, in_specs=[SMEM] * scalars + [VMEM] *...  4.16 us
  transfers between devices with their start and end apart: 17, of which 6 were waited for; matrix products, arithmetic and copies ran while one was open for 5% of the time, Pallas kernels for 17%

profile of v4, /device:TPU:1, one launch (start us, length us, event | category | flops | bytes accessed | tf_op | source)
XLA Modules:
  0.0 67.3 jit_solution(13002476400422874599)
XLA Ops:
  0.7 2.1 %collective-permute-start = (bf16[512,512]{1,0:T(8,128)(2,1)}, bf16[512,512]{1,0:T(8,128)(2,1)S(1)}, u32[]{:S(2)}, u32[]{:S(2)}) collective-permute-start(bf16[512,512]{1,0:T(8,128)(2,1)} %r0.1), channel_id=1, source_target_pairs={{0,2},{1,3},{2,4},{3,5},{4,6},{5,7},{6,0},{7,1},{8,10},{9,11},{10,... | collective-permute-start | bytes 1572872 | tf_op jit(solution)/shard_map/ppermute | solution.py:55
  2.8 1.4 %collective-permute-start.2 = (bf16[512,512]{1,0:T(8,128)(2,1)}, bf16[512,512]{1,0:T(8,128)(2,1)S(1)}, u32[]{:S(2)}, u32[]{:S(2)}) collective-permute-start(bf16[512,512]{1,0:T(8,128)(2,1)} %r0.1), channel_id=1, source_target_pairs={{0,6},{1,7},{2,0},{3,1},{4,2},{5,3},{6,4},{7,5},{8,14},{9,15},{10,... | collective-permute-start | bytes 1572872 | tf_op jit(solution)/shard_map/ppermute | solution.py:55
  4.1 2.7 %shard_map.95 = (bf16[4,512,128]{2,1,0:T(8,128)(2,1)}, bf16[4,512,128]{2,1,0:T(8,128)(2,1)}, bf16[4,512,128]{2,1,0:T(8,128)(2,1)}) custom-call(bf16[2,4,2,512,128]{4,3,2,1,0:T(8,128)(2,1)} %bitcast.3), custom_call_target="tpu_custom_call" | custom-call | bytes 2097152 | tf_op jit(solution)/shard_map/pallas_call | solution.py:89
  6.9 1.8 %collective-permute-start.5 = (bf16[4,512,128]{2,1,0:T(8,128)(2,1)}, bf16[4,512,128]{2,1,0:T(8,128)(2,1)S(1)}, u32[]{:S(2)}, u32[]{:S(2)}) collective-permute-start(bf16[4,512,128]{2,1,0:T(8,128)(2,1)} %get-tuple-element.33), channel_id=1, source_target_pairs={{0,8},{1,9},{2,10},{3,11},{4,12},{5,13},{6,14},{7,15},{8,0},{9,1},... | collective-permute-start | bytes 1572872 | tf_op jit(solution)/shard_map/ppermute | solution.py:39
  8.7 6.1 %collective-permute-start.6 = (bf16[4,512,128]{2,1,0:T(8,128)(2,1)}, bf16[4,512,128]{2,1,0:T(8,128)(2,1)S(1)}, u32[]{:S(2)}, u32[]{:S(2)}) collective-permute-start(bf16[4,512,128]{2,1,0:T(8,128)(2,1)} %get-tuple-element.34), channel_id=1, source_target_pairs={{0,201},{1,200},{2,203},{3,202},{4,205},{5,204},{6,207},{7,206},{8... | collective-permute-start | bytes 1572872 | tf_op jit(solution)/shard_map/ppermute | solution.py:51
  14.8 0.1 add_convert_fusion
  14.8 0.1 convert_element_type.56
  15.0 0.1 pad_maximum_fusion
  15.0 2.7 %fusion.3 = (f32[512,128]{1,0:T(8,128)}, f32[512,128]{1,0:T(8,128)S(1)}) fusion(f32[512]{0:T(512)S(1)} %convert_element_type.58, f32[128]{0:T(128)S(1)} %get-tuple-element.61, f32[128]{0:T(128)S(1)} %get-tuple-element.60, pred[128]{0:T(512)(128)(4,1)S(1)} %iota_compare_fusion, pred[]{:T(512)S(6)} %lt.20, f32[512]{0:T(512)S(1)} %convert_element_type.56), kind=kLoop, calls=%fused_computation.7 | loop fusion | flops 393216 | bytes 529537 | tf_op jit(solution)/shard_map/jit(_where)/select_n | solution.py:308
  17.7 0.0 collective-permute-done.r1
  17.7 0.0 collective-permute-done.2.r3
  17.8 0.1 collective-permute-start.4
  17.9 0.8 %collective-permute-start.1 = (bf16[256,512]{1,0:T(8,128)(2,1)S(1)}, bf16[256,512]{1,0:T(8,128)(2,1)S(1)}, u32[]{:S(2)}, u32[]{:S(2)}) collective-permute-start(bf16[256,512]{1,0:T(8,128)(2,1)S(1)} %slice.6), channel_id=1, source_target_pairs={{0,2},{1,3},{2,4},{3,5},{4,6},{5,7},{6,0},{7,1},{8,10},{9,11},{10,... | collective-permute-start | bytes 786440 | tf_op jit(solution)/shard_map/ppermute | solution.py:55
  18.7 2.1 %collective-permute-start.3 = (bf16[256,512]{1,0:T(8,128)(2,1)S(1)}, bf16[256,512]{1,0:T(8,128)(2,1)S(1)}, u32[]{:S(2)}, u32[]{:S(2)}) collective-permute-start(bf16[256,512]{1,0:T(8,128)(2,1)S(1)} %slice.8), channel_id=1, source_target_pairs={{0,6},{1,7},{2,0},{3,1},{4,2},{5,3},{6,4},{7,5},{8,14},{9,15},{10,... | collective-permute-start | bytes 786440 | tf_op jit(solution)/shard_map/ppermute | solution.py:55
  20.7 1.0 %copy-done.13 = bf16[4,512,128]{2,1,0:T(8,128)(2,1)S(1)} copy-done((bf16[4,512,128]{2,1,0:T(8,128)(2,1)S(1)}, bf16[4,512,128]{2,1,0:T(8,128)(2,1)}, u32[]{:S(2)}) %copy-start.13) | copy-done | bytes 524312
  21.8 0.0 collective-permute-done.5.w2.refs_3_
  21.8 0.1 collective-permute-start.10
  21.9 4.1 %collective-permute-done.6.w3.refs_4_ = bf16[4,512,128]{2,1,0:T(8,128)(2,1)S(1)} collective-permute-done((bf16[4,512,128]{2,1,0:T(8,128)(2,1)}, bf16[4,512,128]{2,1,0:T(8,128)(2,1)S(1)}, u32[]{:S(2)}, u32[]{:S(2)}) %collective-permute-start.6) | collective-permute-done | bytes 524320 | tf_op jit(solution)/shard_map/ppermute | solution.py:51
  26.1 1.3 %collective-permute-start.12 = (bf16[512,512]{1,0:T(8,128)(2,1)}, bf16[512,512]{1,0:T(8,128)(2,1)}, u32[]{:S(2)}, u32[]{:S(2)}) collective-permute-start(bf16[512,512]{1,0:T(8,128)(2,1)} %r0.2), channel_id=1, source_target_pairs={{0,6},{1,7},{2,0},{3,1},{4,2},{5,3},{6,4},{7,5},{8,14},{9,15},{10,... | collective-permute-start | bytes 1572872 | tf_op jit(solution)/shard_map/ppermute | solution.py:55
  27.3 0.0 collective-permute-done.4.w1.refs_2_
  27.4 2.0 %shard_map.97 = (f32[512,512]{1,0:T(8,128)S(1)}, f32[512,128]{1,0:T(8,128)S(1)}) custom-call(bf16[2,4,2,512,128]{4,3,2,1,0:T(8,128)(2,1)S(1)} %bitcast.4, bf16[512,512]{1,0:T(8,128)(2,1)S(1)} %copy-done.8, bf16[512,512]{1,0:T(8,128)(2,1)S(1)} %copy-done.4, bf16[512,512]{1,0:T(8,128)(2,1)S(1)} %copy-done.6, ...), custom_call_target="tpu_custom_call" | custom-call | flops 1073741824 | bytes 4194304 | tf_op jit(solution)/shard_map/pallas_call | solution.py:202
  29.4 0.5 collective-permute-start.11
  29.9 0.0 collective-permute-done.1.refs_0_
  29.9 0.0 collective-permute-done.3.refs_1_
  29.9 0.7 %shard_map.98 = (f32[512,128]{1,0:T(8,128)S(1)}, f32[528,128]{1,0:T(8,128)S(1)}, f32[528,128]{1,0:T(8,128)S(1)}, f32[528,128]{1,0:T(8,128)S(1)}, f32[16,128]{1,0:T(8,128)S(1)}) custom-call(bf16[2,4,2,512,128]{4,3,2,1,0:T(8,128)(2,1)S(1)} %bitcast.5, bf16[256,512]{1,0:T(8,128)(2,1)S(1)} %collective-permute-done.1.refs_0_, ...), custom_call_target="tpu_custom_call" | custom-call | flops 1073741824 | bytes 4194304 | tf_op jit(solution)/shard_map/pallas_call | solution.py:202
  30.6 0.0 copy-start.11
  30.6 0.0 copy-start.12
  30.7 0.2 collective-permute-start.7
  30.9 0.1 collective-permute-start.8
  31.1 1.0 %collective-permute-done.7 = f16[528,128]{1,0:T(8,128)(2,1)S(1)} collective-permute-done((f16[528,128]{1,0:T(8,128)(2,1)S(1)}, f16[528,128]{1,0:T(8,128)(2,1)S(1)}, u32[]{:S(2)}, u32[]{:S(2)}) %collective-permute-start.7) | collective-permute-done | bytes 135200 | tf_op jit(solution)/shard_map/ppermute | solution.py:39
  32.1 1.2 %collective-permute-start.9 = (f16[528,128]{1,0:T(8,128)(2,1)S(1)}, f16[528,128]{1,0:T(8,128)(2,1)S(1)}, u32[]{:S(2)}, u32[]{:S(2)}) collective-permute-start(f16[528,128]{1,0:T(8,128)(2,1)S(1)} %convert_element_type.63), channel_id=1, source_target_pairs={{0,9},{1,8},{2,11},{3,10},{4,13},{5,12},{6,15},{7,14},{8,1},{9,0},... | collective-permute-start | bytes 405512 | tf_op jit(solution)/shard_map/ppermute | solution.py:39
  33.3 2.6 %collective-permute-done.8 = f16[528,128]{1,0:T(8,128)(2,1)S(1)} collective-permute-done((f16[528,128]{1,0:T(8,128)(2,1)S(1)}, f16[528,128]{1,0:T(8,128)(2,1)S(1)}, u32[]{:S(2)}, u32[]{:S(2)}) %collective-permute-start.8) | collective-permute-done | bytes 135200 | tf_op jit(solution)/shard_map/ppermute | solution.py:39
  36.0 3.7 %collective-permute-done.9 = f16[528,128]{1,0:T(8,128)(2,1)S(1)} collective-permute-done((f16[528,128]{1,0:T(8,128)(2,1)S(1)}, f16[528,128]{1,0:T(8,128)(2,1)S(1)}, u32[]{:S(2)}, u32[]{:S(2)}) %collective-permute-start.9) | collective-permute-done | bytes 135200 | tf_op jit(solution)/shard_map/ppermute | solution.py:39
  39.7 2.0 %shard_map.99 = bf16[16,64,128]{2,1,0:T(8,128)(2,1)} custom-call(s32[8]{0:T(128)S(1)} %copy-done.11, s32[8]{0:T(128)S(1)} %copy-done.12, f32[512,128]{1,0:T(8,128)S(1)} %get-tuple-element.40.own, f32[16,128]{1,0:T(8,128)S(1)} %get-tuple-element.41.code, f32[528,128]{1,0:T(8,128)S(1)} %convert_element_type.60.g1, f32[528,128]{1,0:T(8,128)S(1)} %convert_element_type.62.g2, ...), custom_call_target="tpu_custom_call" | custom-call | flops 1048576 | bytes 1048576 | tf_op jit(solution)/shard_map/pallas_call | solution.py:234
  41.7 9.5 %all-to-all-start = ((bf16[16,64,128]{2,1,0:T(8,128)(2,1)}), bf16[16,64,128]{2,1,0:T(8,128)(2,1)S(1)}, u32[]{:S(2)}, u32[]{:S(2)}) async-start(bf16[16,64,128]{2,1,0:T(8,128)(2,1)} %shard_map.99), calls=%async_computation | async-start | bytes 524288 | tf_op jit(solution)/shard_map/all_to_all | solution.py:371
  51.2 0.0 collective-permute-done.10.r1
  51.2 0.0 collective-permute-done.12.r3
  51.2 1.0 %copy-done.2 = bf16[4,512,128]{2,1,0:T(8,128)(2,1)S(1)} copy-done((bf16[4,512,128]{2,1,0:T(8,128)(2,1)S(1)}, bf16[4,512,128]{2,1,0:T(8,128)(2,1)}, u32[]{:S(2)}) %copy-start.2) | copy-done | bytes 524312
  52.2 3.2 %shard_map.100 = (f32[512,128]{1,0:T(8,128)S(1)}, f32[528,128]{1,0:T(8,128)S(1)}, f32[528,128]{1,0:T(8,128)S(1)}, f32[528,128]{1,0:T(8,128)S(1)}, f32[16,128]{1,0:T(8,128)S(1)}) custom-call(bf16[2,4,2,512,128]{4,3,2,1,0:T(8,128)(2,1)S(1)} %bitcast.6, bf16[512,512]{1,0:T(8,128)(2,1)} %r0.2, bf16[512,512]{1,0:T(8,128)(2,1)} %collective-permute-done.10.r1, ...), custom_call_target="tpu_custom_call" | custom-call | flops 2147483648 | bytes 4194304 | tf_op jit(solution)/shard_map/pallas_call | solution.py:202
  55.5 0.9 %collective-permute-start.13 = (f16[528,128]{1,0:T(8,128)(2,1)S(1)}, f16[528,128]{1,0:T(8,128)(2,1)S(1)}, u32[]{:S(2)}, u32[]{:S(2)}) collective-permute-start(f16[528,128]{1,0:T(8,128)(2,1)S(1)} %convert_element_type.65), channel_id=1, source_target_pairs={{0,8},{1,9},{2,10},{3,11},{4,12},{5,13},{6,14},{7,15},{8,0},{9,1},... | collective-permute-start | bytes 405512 | tf_op jit(solution)/shard_map/ppermute | solution.py:39
  56.4 1.2 %collective-permute-start.14 = (f16[528,128]{1,0:T(8,128)(2,1)S(1)}, f16[528,128]{1,0:T(8,128)(2,1)S(1)}, u32[]{:S(2)}, u32[]{:S(2)}) collective-permute-start(f16[528,128]{1,0:T(8,128)(2,1)S(1)} %convert_element_type.67), channel_id=1, source_target_pairs={{0,1},{1,0},{2,3},{3,2},{4,5},{5,4},{6,7},{7,6},{8,9},{9,8},{10,11... | collective-permute-start | bytes 405512 | tf_op jit(solution)/shard_map/ppermute | solution.py:39
  57.5 0.1 collective-permute-start.15
  57.6 4.8 %all-to-all-done.arrived = bf16[16,64,128]{2,1,0:T(8,128)(2,1)S(1)} async-done(((bf16[16,64,128]{2,1,0:T(8,128)(2,1)}), bf16[16,64,128]{2,1,0:T(8,128)(2,1)S(1)}, u32[]{:S(2)}, u32[]{:S(2)}) %all-to-all-start) | async-done | bytes 262176 | tf_op jit(solution)/shard_map/all_to_all | solution.py:371
  62.5 0.7 %shard_map.101 = bf16[16,64,128]{2,1,0:T(8,128)(2,1)} custom-call(bf16[16,64,128]{2,1,0:T(8,128)(2,1)S(1)} %all-to-all-done.arrived), custom_call_target="tpu_custom_call" | custom-call | flops 1048576 | bytes 1048576 | tf_op jit(solution)/shard_map/pallas_call | solution.py:234
  63.2 0.0 collective-permute-done.14
  63.3 1.6 %collective-permute-done.15 = f16[528,128]{1,0:T(8,128)(2,1)S(1)} collective-permute-done((f16[528,128]{1,0:T(8,128)(2,1)S(1)}, f16[528,128]{1,0:T(8,128)(2,1)S(1)}, u32[]{:S(2)}, u32[]{:S(2)}) %collective-permute-start.15) | collective-permute-done | bytes 135200 | tf_op jit(solution)/shard_map/ppermute | solution.py:39
  64.9 0.9 %copy-done.10 = f32[512,128]{1,0:T(8,128)S(1)} copy-done((f32[512,128]{1,0:T(8,128)S(1)}, f32[512,128]{1,0:T(8,128)}, u32[]{:S(2)}) %copy-start.10) | copy-done | bytes 262168
  65.9 1.4 %shard_map.102 = bf16[512,128]{1,0:T(8,128)(2,1)} custom-call(f32[512,128]{1,0:T(8,128)S(1)} %copy-done.10, f32[16,128]{1,0:T(8,128)S(1)} %get-tuple-element.53.code, f32[528,128]{1,0:T(8,128)S(1)} %convert_element_type.68.g1, f32[528,128]{1,0:T(8,128)S(1)} %convert_element_type.66.g2, f32[528,128]{1,0:T(8,128)S(1)} %convert_element_type.70.g3, ...), custom_call_target="tpu_custom_call" | custom-call | flops 1048576 | bytes 1048576 | tf_op jit(solution)/shard_map/pallas_call | solution.py:234
  (49 shorter events, 0.4 us)
Async XLA Ops:
  0.6 14.1 %copy-start.16 = (s32[8]{0:T(128)S(1)}, s32[8]{0:T(128)}, u32[]{:S(2)}) copy-start(s32[8]{0:T(128)} %param.11) | copy-start | bytes 100
  0.6 14.3 %copy-start.15 = (s32[512]{0:T(512)S(1)}, s32[512]{0:T(512)}, u32[]{:S(2)}) copy-start(s32[512]{0:T(512)} %param.13) | copy-start | bytes 6148
  0.7 20.1 %copy-start.14 = (f32[128]{0:T(128)S(1)}, f32[128]{0:T(128)}, u32[]{:S(2)}) copy-start(f32[128]{0:T(128)} %param.15) | copy-start | bytes 1540
  0.7 17.1 %collective-permute-start = (bf16[512,512]{1,0:T(8,128)(2,1)}, bf16[512,512]{1,0:T(8,128)(2,1)S(1)}, u32[]{:S(2)}, u32[]{:S(2)}) collective-permute-start(bf16[512,512]{1,0:T(8,128)(2,1)} %r0.1), channel_id=1, source_target_pairs={{0,2},{1,3},{2,4},{3,5},{4,6},{5,7},{6,0},{7,1},{8,10},{9,11},{10,... | collective-permute-start | bytes 1572872 | tf_op jit(solution)/shard_map/ppermute | solution.py:55
  2.8 15.0 %collective-permute-start.2 = (bf16[512,512]{1,0:T(8,128)(2,1)}, bf16[512,512]{1,0:T(8,128)(2,1)S(1)}, u32[]{:S(2)}, u32[]{:S(2)}) collective-permute-start(bf16[512,512]{1,0:T(8,128)(2,1)} %r0.1), channel_id=1, source_target_pairs={{0,6},{1,7},{2,0},{3,1},{4,2},{5,3},{6,4},{7,5},{8,14},{9,15},{10,... | collective-permute-start | bytes 1572872 | tf_op jit(solution)/shard_map/ppermute | solution.py:55
  6.9 14.9 %collective-permute-start.5 = (bf16[4,512,128]{2,1,0:T(8,128)(2,1)}, bf16[4,512,128]{2,1,0:T(8,128)(2,1)S(1)}, u32[]{:S(2)}, u32[]{:S(2)}) collective-permute-start(bf16[4,512,128]{2,1,0:T(8,128)(2,1)} %get-tuple-element.33), channel_id=1, source_target_pairs={{0,8},{1,9},{2,10},{3,11},{4,12},{5,13},{6,14},{7,15},{8,0},{9,1},... | collective-permute-start | bytes 1572872 | tf_op jit(solution)/shard_map/ppermute | solution.py:39
  8.7 17.4 %collective-permute-start.6 = (bf16[4,512,128]{2,1,0:T(8,128)(2,1)}, bf16[4,512,128]{2,1,0:T(8,128)(2,1)S(1)}, u32[]{:S(2)}, u32[]{:S(2)}) collective-permute-start(bf16[4,512,128]{2,1,0:T(8,128)(2,1)} %get-tuple-element.34), channel_id=1, source_target_pairs={{0,201},{1,200},{2,203},{3,202},{4,205},{5,204},{6,207},{7,206},{8... | collective-permute-start | bytes 1572872 | tf_op jit(solution)/shard_map/ppermute | solution.py:51
  17.7 3.0 %copy-start.3 = (bf16[512,512]{1,0:T(8,128)(2,1)}, bf16[512,512]{1,0:T(8,128)(2,1)S(1)}, u32[]{:S(2)}) copy-start(bf16[512,512]{1,0:T(8,128)(2,1)S(1)} %collective-permute-done.r1) | copy-start | bytes 1572868
  17.7 3.0 %copy-start.5 = (bf16[512,512]{1,0:T(8,128)(2,1)}, bf16[512,512]{1,0:T(8,128)(2,1)S(1)}, u32[]{:S(2)}) copy-start(bf16[512,512]{1,0:T(8,128)(2,1)S(1)} %collective-permute-done.2.r3) | copy-start | bytes 1572868
  17.8 9.6 %collective-permute-start.4 = (bf16[4,512,128]{2,1,0:T(8,128)(2,1)}, bf16[4,512,128]{2,1,0:T(8,128)(2,1)S(1)}, u32[]{:S(2)}, u32[]{:S(2)}) collective-permute-start(bf16[4,512,128]{2,1,0:T(8,128)(2,1)} %get-tuple-element.32.after), channel_id=1, source_target_pairs={{0,1},{1,0},{2,3},{3,2},{4,5},{5,4},{6,7},{7,6},{8,9},{9,8},{10,11... | collective-permute-start | bytes 1572872 | tf_op jit(solution)/shard_map/ppermute | solution.py:39
  17.9 12.0 %collective-permute-start.1 = (bf16[256,512]{1,0:T(8,128)(2,1)S(1)}, bf16[256,512]{1,0:T(8,128)(2,1)S(1)}, u32[]{:S(2)}, u32[]{:S(2)}) collective-permute-start(bf16[256,512]{1,0:T(8,128)(2,1)S(1)} %slice.6), channel_id=1, source_target_pairs={{0,2},{1,3},{2,4},{3,5},{4,6},{5,7},{6,0},{7,1},{8,10},{9,11},{10,... | collective-permute-start | bytes 786440 | tf_op jit(solution)/shard_map/ppermute | solution.py:55
  18.7 11.3 %collective-permute-start.3 = (bf16[256,512]{1,0:T(8,128)(2,1)S(1)}, bf16[256,512]{1,0:T(8,128)(2,1)S(1)}, u32[]{:S(2)}, u32[]{:S(2)}) collective-permute-start(bf16[256,512]{1,0:T(8,128)(2,1)S(1)} %slice.8), channel_id=1, source_target_pairs={{0,6},{1,7},{2,0},{3,1},{4,2},{5,3},{6,4},{7,5},{8,14},{9,15},{10,... | collective-permute-start | bytes 786440 | tf_op jit(solution)/shard_map/ppermute | solution.py:55
  20.7 1.0 %copy-start.13 = (bf16[4,512,128]{2,1,0:T(8,128)(2,1)S(1)}, bf16[4,512,128]{2,1,0:T(8,128)(2,1)}, u32[]{:S(2)}) copy-start(bf16[4,512,128]{2,1,0:T(8,128)(2,1)} %get-tuple-element.32.after) | copy-start | bytes 1572868
  21.8 5.6 %copy-start = (bf16[8192,128]{1,0:T(8,128)(2,1)S(1)}, bf16[8192,128]{1,0:T(8,128)(2,1)}, u32[]{:S(2)}) copy-start(bf16[8192,128]{1,0:T(8,128)(2,1)} %param.14) | copy-start | bytes 6291460
  21.8 5.6 %copy-start.4 = (bf16[512,512]{1,0:T(8,128)(2,1)S(1)}, bf16[512,512]{1,0:T(8,128)(2,1)}, u32[]{:S(2)}) copy-start(bf16[512,512]{1,0:T(8,128)(2,1)} %copy-done.3) | copy-start | bytes 1572868
  21.8 5.6 %copy-start.6 = (bf16[512,512]{1,0:T(8,128)(2,1)S(1)}, bf16[512,512]{1,0:T(8,128)(2,1)}, u32[]{:S(2)}) copy-start(bf16[512,512]{1,0:T(8,128)(2,1)} %copy-done.5) | copy-start | bytes 1572868
  21.8 5.6 %copy-start.8 = (bf16[512,512]{1,0:T(8,128)(2,1)S(1)}, bf16[512,512]{1,0:T(8,128)(2,1)}, u32[]{:S(2)}) copy-start(bf16[512,512]{1,0:T(8,128)(2,1)} %r0.1) | copy-start | bytes 1572868
  21.8 29.3 %collective-permute-start.10 = (bf16[512,512]{1,0:T(8,128)(2,1)}, bf16[512,512]{1,0:T(8,128)(2,1)}, u32[]{:S(2)}, u32[]{:S(2)}) collective-permute-start(bf16[512,512]{1,0:T(8,128)(2,1)} %r0.2), channel_id=1, source_target_pairs={{0,2},{1,3},{2,4},{3,5},{4,6},{5,7},{6,0},{7,1},{8,10},{9,11},{10,... | collective-permute-start | bytes 1572872 | tf_op jit(solution)/shard_map/ppermute | solution.py:55
  26.1 25.1 %collective-permute-start.12 = (bf16[512,512]{1,0:T(8,128)(2,1)}, bf16[512,512]{1,0:T(8,128)(2,1)}, u32[]{:S(2)}, u32[]{:S(2)}) collective-permute-start(bf16[512,512]{1,0:T(8,128)(2,1)} %r0.2), channel_id=1, source_target_pairs={{0,6},{1,7},{2,0},{3,1},{4,2},{5,3},{6,4},{7,5},{8,14},{9,15},{10,... | collective-permute-start | bytes 1572872 | tf_op jit(solution)/shard_map/ppermute | solution.py:55
  27.4 2.6 %copy-start.1 = (bf16[4,512,128]{2,1,0:T(8,128)(2,1)}, bf16[4,512,128]{2,1,0:T(8,128)(2,1)S(1)}, u32[]{:S(2)}) copy-start(bf16[4,512,128]{2,1,0:T(8,128)(2,1)S(1)} %collective-permute-done.4.w1.refs_2_) | copy-start | bytes 1572868
  29.4 21.8 %collective-permute-start.11 = (bf16[512,512]{1,0:T(8,128)(2,1)}, bf16[512,512]{1,0:T(8,128)(2,1)}, u32[]{:S(2)}, u32[]{:S(2)}) collective-permute-start(bf16[512,512]{1,0:T(8,128)(2,1)} %r0.2), channel_id=1, source_target_pairs={{0,4},{1,5},{2,6},{3,7},{4,0},{5,1},{6,2},{7,3},{8,12},{9,13},{10,... | collective-permute-start | bytes 1572872 | tf_op jit(solution)/shard_map/ppermute | solution.py:55
  30.6 9.0 %copy-start.11 = (s32[8]{0:T(128)S(1)}, s32[8]{0:T(128)}, u32[]{:S(2)}) copy-start(s32[8]{0:T(128)} %owner.1) | copy-start | bytes 100
  30.6 9.0 %copy-start.12 = (s32[8]{0:T(128)S(1)}, s32[8]{0:T(128)}, u32[]{:S(2)}) copy-start(s32[8]{0:T(128)} %valid.1) | copy-start | bytes 100
  30.7 1.4 %collective-permute-start.7 = (f16[528,128]{1,0:T(8,128)(2,1)S(1)}, f16[528,128]{1,0:T(8,128)(2,1)S(1)}, u32[]{:S(2)}, u32[]{:S(2)}) collective-permute-start(f16[528,128]{1,0:T(8,128)(2,1)S(1)} %convert_element_type.59), channel_id=1, source_target_pairs={{0,1},{1,0},{2,3},{3,2},{4,5},{5,4},{6,7},{7,6},{8,9},{9,8},{10,11... | collective-permute-start | bytes 405512 | tf_op jit(solution)/shard_map/ppermute | solution.py:39
  30.9 5.0 %collective-permute-start.8 = (f16[528,128]{1,0:T(8,128)(2,1)S(1)}, f16[528,128]{1,0:T(8,128)(2,1)S(1)}, u32[]{:S(2)}, u32[]{:S(2)}) collective-permute-start(f16[528,128]{1,0:T(8,128)(2,1)S(1)} %convert_element_type.61), channel_id=1, source_target_pairs={{0,8},{1,9},{2,10},{3,11},{4,12},{5,13},{6,14},{7,15},{8,0},{9,1},... | collective-permute-start | bytes 405512 | tf_op jit(solution)/shard_map/ppermute | solution.py:39
  32.1 7.5 %collective-permute-start.9 = (f16[528,128]{1,0:T(8,128)(2,1)S(1)}, f16[528,128]{1,0:T(8,128)(2,1)S(1)}, u32[]{:S(2)}, u32[]{:S(2)}) collective-permute-start(f16[528,128]{1,0:T(8,128)(2,1)S(1)} %convert_element_type.63), channel_id=1, source_target_pairs={{0,9},{1,8},{2,11},{3,10},{4,13},{5,12},{6,15},{7,14},{8,1},{9,0},... | collective-permute-start | bytes 405512 | tf_op jit(solution)/shard_map/ppermute | solution.py:39
  41.7 20.8 %all-to-all-start = ((bf16[16,64,128]{2,1,0:T(8,128)(2,1)}), bf16[16,64,128]{2,1,0:T(8,128)(2,1)S(1)}, u32[]{:S(2)}, u32[]{:S(2)}) async-start(bf16[16,64,128]{2,1,0:T(8,128)(2,1)} %shard_map.99), calls=%async_computation | async-start | bytes 524288 | tf_op jit(solution)/shard_map/all_to_all | solution.py:371
  51.2 1.0 %copy-start.2 = (bf16[4,512,128]{2,1,0:T(8,128)(2,1)S(1)}, bf16[4,512,128]{2,1,0:T(8,128)(2,1)}, u32[]{:S(2)}) copy-start(bf16[4,512,128]{2,1,0:T(8,128)(2,1)} %copy-done.1) | copy-start | bytes 1572868
  55.4 2.1 %copy-start.9 = (f32[512,128]{1,0:T(8,128)}, f32[512,128]{1,0:T(8,128)S(1)}, u32[]{:S(2)}) copy-start(f32[512,128]{1,0:T(8,128)S(1)} %get-tuple-element.52.own) | copy-start | bytes 786436
  55.4 9.5 %copy-start.7 = (f32[512,128]{1,0:T(8,128)S(1)}, f32[512,128]{1,0:T(8,128)}, u32[]{:S(2)}) copy-start(f32[512,128]{1,0:T(8,128)} %get-tuple-element.57.turns) | copy-start | bytes 786436
  55.5 7.7 %collective-permute-start.13 = (f16[528,128]{1,0:T(8,128)(2,1)S(1)}, f16[528,128]{1,0:T(8,128)(2,1)S(1)}, u32[]{:S(2)}, u32[]{:S(2)}) collective-permute-start(f16[528,128]{1,0:T(8,128)(2,1)S(1)} %convert_element_type.65), channel_id=1, source_target_pairs={{0,8},{1,9},{2,10},{3,11},{4,12},{5,13},{6,14},{7,15},{8,0},{9,1},... | collective-permute-start | bytes 405512 | tf_op jit(solution)/shard_map/ppermute | solution.py:39
  56.4 6.9 %collective-permute-start.14 = (f16[528,128]{1,0:T(8,128)(2,1)S(1)}, f16[528,128]{1,0:T(8,128)(2,1)S(1)}, u32[]{:S(2)}, u32[]{:S(2)}) collective-permute-start(f16[528,128]{1,0:T(8,128)(2,1)S(1)} %convert_element_type.67), channel_id=1, source_target_pairs={{0,1},{1,0},{2,3},{3,2},{4,5},{5,4},{6,7},{7,6},{8,9},{9,8},{10,11... | collective-permute-start | bytes 405512 | tf_op jit(solution)/shard_map/ppermute | solution.py:39
  57.5 7.3 %collective-permute-start.15 = (f16[528,128]{1,0:T(8,128)(2,1)S(1)}, f16[528,128]{1,0:T(8,128)(2,1)S(1)}, u32[]{:S(2)}, u32[]{:S(2)}) collective-permute-start(f16[528,128]{1,0:T(8,128)(2,1)S(1)} %convert_element_type.69), channel_id=1, source_target_pairs={{0,9},{1,8},{2,11},{3,10},{4,13},{5,12},{6,15},{7,14},{8,1},{9,0},... | collective-permute-start | bytes 405512 | tf_op jit(solution)/shard_map/ppermute | solution.py:39
  64.9 1.0 %copy-start.10 = (f32[512,128]{1,0:T(8,128)S(1)}, f32[512,128]{1,0:T(8,128)}, u32[]{:S(2)}) copy-start(f32[512,128]{1,0:T(8,128)} %copy-done.9) | copy-start | bytes 786436

commit v5 on v4

--- a/solution.py
+++ b/solution.py
@@ -19,7 +19,9 @@
 STEPS = 2048.0
 LN2 = 0.6931471805599453
 LOW = 1e-36
-HIGH = 1e37
+HIGH = 3.39e38
+FULL = 3.385e38
+MOST = 6e4
 
 
 def spot(z, x, c):
@@ -181,7 +183,8 @@
     down = LIFT * lax.rsqrt(norm)
     own[...] = total[:, :HD]
     for e, f in enumerate((f1, f2, f3)):
-        f[pl.ds(0, rows), :] = total[:, (e + 1) * HD : (e + 2) * HD] * down
+        sent = total[:, (e + 1) * HD : (e + 2) * HD] * down
+        f[pl.ds(0, rows), :] = jnp.clip(sent, -MOST, MOST)
     lines = []
     for g in range(rows // HD):
         part = jnp.where(mask, norm[g * HD : (g + 1) * HD, :], 0.0)
@@ -252,7 +255,10 @@
         return jnp.exp(u * LN2)
 
     norms = [norms_of(g, own.shape[0]) for g in got]
-    total = norms_of(code, 0) + norms[0] + norms[1] + norms[2]
+    own_norm = norms_of(code, 0)
+    total = own_norm + norms[0] + norms[1] + norms[2]
+    for n in (own_norm, *norms):
+        total = jnp.where(n > FULL, jnp.inf, total)
     scale = lax.rsqrt(total / D + 1e-06)
     ups = [jnp.sqrt(n) * scale * (1.0 / LIFT) for n in norms]
     rest = jnp.zeros((HD - 4 * lines, HD), f32)

time: 67.6 us -> 67.6 us (level)
  no operation moved by 1% of the time
where the time goes in v5:
time: 67.6 us; the launch traced here: 67.3 us
  starting transfers between devices  29.3 us (43%)
  waiting for transfers between devices  17.9 us (26%)
  Pallas kernels  12.7 us (19%)
  local copies, waits for them, and re-layouts  3.19 us (5%)
  other arithmetic  3.11 us (5%)
  between operations  0.99 us (1%)
    all_to_all x1, starting transfers between devices, shards(): lax.all_to_all(outgoing, 'pool', split_axis=0, concat_axis=0, tiled=True)  9.46 us
    ppermute x8, waiting for transfers between devices, across(): lax.ppermute(v, 'mp', pairs(lambda z, x, c: (z ^ e // NC, x, c ^ e % NC)))  8.93 us
    ppermute x7, starting transfers between devices, along_x(): return lax.ppermute(v, 'mp', pairs(lambda z, x, c: (z, (x + d) % NX, c)))  8.21 us
    ppermute x1, starting transfers between devices, outward(): return lax.ppermute(v, ('pool', 'mp'), moves)  6.07 us
    pallas_call x3, Pallas kernels, multiply(): pl.pallas_call(body, out_shape=out, in_specs=[ANY] + [VMEM if stay else A...  5.85 us
    ppermute x8, starting transfers between devices, across(): lax.ppermute(v, 'mp', pairs(lambda z, x, c: (z ^ e // NC, x, c ^ e % NC)))  5.57 us
    all_to_all x1, waiting for transfers between devices, shards(): lax.all_to_all(outgoing, 'pool', split_axis=0, concat_axis=0, tiled=True)  4.83 us
    pallas_call x3, Pallas kernels, call(): pl.pallas_call(body, out_shape=out, in_specs=[SMEM] * scalars + [VMEM] *...  4.16 us
  transfers between devices with their start and end apart: 17, of which 6 were waited for; matrix products, arithmetic and copies ran while one was open for 5% of the time, Pallas kernels for 17%

profile of v5, /device:TPU:1, one launch (start us, length us, event | category | flops | bytes accessed | tf_op | source)
XLA Modules:
  0.0 67.3 jit_solution(1928895080025422313)
XLA Ops:
  0.7 2.1 %collective-permute-start = (bf16[512,512]{1,0:T(8,128)(2,1)}, bf16[512,512]{1,0:T(8,128)(2,1)S(1)}, u32[]{:S(2)}, u32[]{:S(2)}) collective-permute-start(bf16[512,512]{1,0:T(8,128)(2,1)} %r0.1), channel_id=1, source_target_pairs={{0,2},{1,3},{2,4},{3,5},{4,6},{5,7},{6,0},{7,1},{8,10},{9,11},{10,... | collective-permute-start | bytes 1572872 | tf_op jit(solution)/shard_map/ppermute | solution.py:57
  2.8 1.4 %collective-permute-start.2 = (bf16[512,512]{1,0:T(8,128)(2,1)}, bf16[512,512]{1,0:T(8,128)(2,1)S(1)}, u32[]{:S(2)}, u32[]{:S(2)}) collective-permute-start(bf16[512,512]{1,0:T(8,128)(2,1)} %r0.1), channel_id=1, source_target_pairs={{0,6},{1,7},{2,0},{3,1},{4,2},{5,3},{6,4},{7,5},{8,14},{9,15},{10,... | collective-permute-start | bytes 1572872 | tf_op jit(solution)/shard_map/ppermute | solution.py:57
  4.1 2.7 %shard_map.95 = (bf16[4,512,128]{2,1,0:T(8,128)(2,1)}, bf16[4,512,128]{2,1,0:T(8,128)(2,1)}, bf16[4,512,128]{2,1,0:T(8,128)(2,1)}) custom-call(bf16[2,4,2,512,128]{4,3,2,1,0:T(8,128)(2,1)} %bitcast.3), custom_call_target="tpu_custom_call" | custom-call | bytes 2097152 | tf_op jit(solution)/shard_map/pallas_call | solution.py:91
  6.9 1.8 %collective-permute-start.5 = (bf16[4,512,128]{2,1,0:T(8,128)(2,1)}, bf16[4,512,128]{2,1,0:T(8,128)(2,1)S(1)}, u32[]{:S(2)}, u32[]{:S(2)}) collective-permute-start(bf16[4,512,128]{2,1,0:T(8,128)(2,1)} %get-tuple-element.33), channel_id=1, source_target_pairs={{0,8},{1,9},{2,10},{3,11},{4,12},{5,13},{6,14},{7,15},{8,0},{9,1},... | collective-permute-start | bytes 1572872 | tf_op jit(solution)/shard_map/ppermute | solution.py:41
  8.7 6.1 %collective-permute-start.6 = (bf16[4,512,128]{2,1,0:T(8,128)(2,1)}, bf16[4,512,128]{2,1,0:T(8,128)(2,1)S(1)}, u32[]{:S(2)}, u32[]{:S(2)}) collective-permute-start(bf16[4,512,128]{2,1,0:T(8,128)(2,1)} %get-tuple-element.34), channel_id=1, source_target_pairs={{0,201},{1,200},{2,203},{3,202},{4,205},{5,204},{6,207},{7,206},{8... | collective-permute-start | bytes 1572872 | tf_op jit(solution)/shard_map/ppermute | solution.py:53
  14.8 0.1 add_convert_fusion
  14.8 0.1 convert_element_type.56
  15.0 0.1 pad_maximum_fusion
  15.0 2.7 %fusion.3 = (f32[512,128]{1,0:T(8,128)}, f32[512,128]{1,0:T(8,128)S(1)}) fusion(f32[512]{0:T(512)S(1)} %convert_element_type.58, f32[128]{0:T(128)S(1)} %get-tuple-element.61, f32[128]{0:T(128)S(1)} %get-tuple-element.60, pred[128]{0:T(512)(128)(4,1)S(1)} %iota_compare_fusion, pred[]{:T(512)S(6)} %lt.20, f32[512]{0:T(512)S(1)} %convert_element_type.56), kind=kLoop, calls=%fused_computation.7 | loop fusion | flops 393216 | bytes 529537 | tf_op jit(solution)/shard_map/jit(_where)/select_n | solution.py:314
  17.7 0.0 collective-permute-done.r1
  17.7 0.0 collective-permute-done.2.r3
  17.8 0.1 collective-permute-start.4
  17.9 0.8 %collective-permute-start.1 = (bf16[256,512]{1,0:T(8,128)(2,1)S(1)}, bf16[256,512]{1,0:T(8,128)(2,1)S(1)}, u32[]{:S(2)}, u32[]{:S(2)}) collective-permute-start(bf16[256,512]{1,0:T(8,128)(2,1)S(1)} %slice.6), channel_id=1, source_target_pairs={{0,2},{1,3},{2,4},{3,5},{4,6},{5,7},{6,0},{7,1},{8,10},{9,11},{10,... | collective-permute-start | bytes 786440 | tf_op jit(solution)/shard_map/ppermute | solution.py:57
  18.7 2.1 %collective-permute-start.3 = (bf16[256,512]{1,0:T(8,128)(2,1)S(1)}, bf16[256,512]{1,0:T(8,128)(2,1)S(1)}, u32[]{:S(2)}, u32[]{:S(2)}) collective-permute-start(bf16[256,512]{1,0:T(8,128)(2,1)S(1)} %slice.8), channel_id=1, source_target_pairs={{0,6},{1,7},{2,0},{3,1},{4,2},{5,3},{6,4},{7,5},{8,14},{9,15},{10,... | collective-permute-start | bytes 786440 | tf_op jit(solution)/shard_map/ppermute | solution.py:57
  20.7 1.0 %copy-done.13 = bf16[4,512,128]{2,1,0:T(8,128)(2,1)S(1)} copy-done((bf16[4,512,128]{2,1,0:T(8,128)(2,1)S(1)}, bf16[4,512,128]{2,1,0:T(8,128)(2,1)}, u32[]{:S(2)}) %copy-start.13) | copy-done | bytes 524312
  21.8 0.0 collective-permute-done.5.w2.refs_3_
  21.8 0.1 collective-permute-start.10
  21.9 4.1 %collective-permute-done.6.w3.refs_4_ = bf16[4,512,128]{2,1,0:T(8,128)(2,1)S(1)} collective-permute-done((bf16[4,512,128]{2,1,0:T(8,128)(2,1)}, bf16[4,512,128]{2,1,0:T(8,128)(2,1)S(1)}, u32[]{:S(2)}, u32[]{:S(2)}) %collective-permute-start.6) | collective-permute-done | bytes 524320 | tf_op jit(solution)/shard_map/ppermute | solution.py:53
  26.1 1.3 %collective-permute-start.12 = (bf16[512,512]{1,0:T(8,128)(2,1)}, bf16[512,512]{1,0:T(8,128)(2,1)}, u32[]{:S(2)}, u32[]{:S(2)}) collective-permute-start(bf16[512,512]{1,0:T(8,128)(2,1)} %r0.2), channel_id=1, source_target_pairs={{0,6},{1,7},{2,0},{3,1},{4,2},{5,3},{6,4},{7,5},{8,14},{9,15},{10,... | collective-permute-start | bytes 1572872 | tf_op jit(solution)/shard_map/ppermute | solution.py:57
  27.3 0.0 collective-permute-done.4.w1.refs_2_
  27.4 2.0 %shard_map.97 = (f32[512,512]{1,0:T(8,128)S(1)}, f32[512,128]{1,0:T(8,128)S(1)}) custom-call(bf16[2,4,2,512,128]{4,3,2,1,0:T(8,128)(2,1)S(1)} %bitcast.4, bf16[512,512]{1,0:T(8,128)(2,1)S(1)} %copy-done.8, bf16[512,512]{1,0:T(8,128)(2,1)S(1)} %copy-done.4, bf16[512,512]{1,0:T(8,128)(2,1)S(1)} %copy-done.6, ...), custom_call_target="tpu_custom_call" | custom-call | flops 1073741824 | bytes 4194304 | tf_op jit(solution)/shard_map/pallas_call | solution.py:205
  29.4 0.5 collective-permute-start.11
  29.9 0.0 collective-permute-done.1.refs_0_
  29.9 0.0 collective-permute-done.3.refs_1_
  29.9 0.7 %shard_map.98 = (f32[512,128]{1,0:T(8,128)S(1)}, f32[528,128]{1,0:T(8,128)S(1)}, f32[528,128]{1,0:T(8,128)S(1)}, f32[528,128]{1,0:T(8,128)S(1)}, f32[16,128]{1,0:T(8,128)S(1)}) custom-call(bf16[2,4,2,512,128]{4,3,2,1,0:T(8,128)(2,1)S(1)} %bitcast.5, bf16[256,512]{1,0:T(8,128)(2,1)S(1)} %collective-permute-done.1.refs_0_, ...), custom_call_target="tpu_custom_call" | custom-call | flops 1073741824 | bytes 4194304 | tf_op jit(solution)/shard_map/pallas_call | solution.py:205
  30.6 0.0 copy-start.11
  30.6 0.0 copy-start.12
  30.7 0.2 collective-permute-start.7
  30.9 0.1 collective-permute-start.8
  31.1 1.0 %collective-permute-done.7 = f16[528,128]{1,0:T(8,128)(2,1)S(1)} collective-permute-done((f16[528,128]{1,0:T(8,128)(2,1)S(1)}, f16[528,128]{1,0:T(8,128)(2,1)S(1)}, u32[]{:S(2)}, u32[]{:S(2)}) %collective-permute-start.7) | collective-permute-done | bytes 135200 | tf_op jit(solution)/shard_map/ppermute | solution.py:41
  32.1 1.2 %collective-permute-start.9 = (f16[528,128]{1,0:T(8,128)(2,1)S(1)}, f16[528,128]{1,0:T(8,128)(2,1)S(1)}, u32[]{:S(2)}, u32[]{:S(2)}) collective-permute-start(f16[528,128]{1,0:T(8,128)(2,1)S(1)} %convert_element_type.63), channel_id=1, source_target_pairs={{0,9},{1,8},{2,11},{3,10},{4,13},{5,12},{6,15},{7,14},{8,1},{9,0},... | collective-permute-start | bytes 405512 | tf_op jit(solution)/shard_map/ppermute | solution.py:41
  33.3 2.6 %collective-permute-done.8 = f16[528,128]{1,0:T(8,128)(2,1)S(1)} collective-permute-done((f16[528,128]{1,0:T(8,128)(2,1)S(1)}, f16[528,128]{1,0:T(8,128)(2,1)S(1)}, u32[]{:S(2)}, u32[]{:S(2)}) %collective-permute-start.8) | collective-permute-done | bytes 135200 | tf_op jit(solution)/shard_map/ppermute | solution.py:41
  36.0 3.7 %collective-permute-done.9 = f16[528,128]{1,0:T(8,128)(2,1)S(1)} collective-permute-done((f16[528,128]{1,0:T(8,128)(2,1)S(1)}, f16[528,128]{1,0:T(8,128)(2,1)S(1)}, u32[]{:S(2)}, u32[]{:S(2)}) %collective-permute-start.9) | collective-permute-done | bytes 135200 | tf_op jit(solution)/shard_map/ppermute | solution.py:41
  39.7 2.0 %shard_map.99 = bf16[16,64,128]{2,1,0:T(8,128)(2,1)} custom-call(s32[8]{0:T(128)S(1)} %copy-done.11, s32[8]{0:T(128)S(1)} %copy-done.12, f32[512,128]{1,0:T(8,128)S(1)} %get-tuple-element.40.own, f32[16,128]{1,0:T(8,128)S(1)} %get-tuple-element.41.code, f32[528,128]{1,0:T(8,128)S(1)} %convert_element_type.60.g1, f32[528,128]{1,0:T(8,128)S(1)} %convert_element_type.62.g2, ...), custom_call_target="tpu_custom_call" | custom-call | flops 1048576 | bytes 1048576 | tf_op jit(solution)/shard_map/pallas_call | solution.py:237
  41.7 9.5 %all-to-all-start = ((bf16[16,64,128]{2,1,0:T(8,128)(2,1)}), bf16[16,64,128]{2,1,0:T(8,128)(2,1)S(1)}, u32[]{:S(2)}, u32[]{:S(2)}) async-start(bf16[16,64,128]{2,1,0:T(8,128)(2,1)} %shard_map.99), calls=%async_computation | async-start | bytes 524288 | tf_op jit(solution)/shard_map/all_to_all | solution.py:377
  51.2 0.0 collective-permute-done.12.r3
  51.2 0.0 collective-permute-done.11.r2
  51.2 1.0 %copy-done.2 = bf16[4,512,128]{2,1,0:T(8,128)(2,1)S(1)} copy-done((bf16[4,512,128]{2,1,0:T(8,128)(2,1)S(1)}, bf16[4,512,128]{2,1,0:T(8,128)(2,1)}, u32[]{:S(2)}) %copy-start.2) | copy-done | bytes 524312
  52.2 3.2 %shard_map.100 = (f32[512,128]{1,0:T(8,128)S(1)}, f32[528,128]{1,0:T(8,128)S(1)}, f32[528,128]{1,0:T(8,128)S(1)}, f32[528,128]{1,0:T(8,128)S(1)}, f32[16,128]{1,0:T(8,128)S(1)}) custom-call(bf16[2,4,2,512,128]{4,3,2,1,0:T(8,128)(2,1)S(1)} %bitcast.6, bf16[512,512]{1,0:T(8,128)(2,1)} %r0.2, bf16[512,512]{1,0:T(8,128)(2,1)} %collective-permute-done.10.r1, ...), custom_call_target="tpu_custom_call" | custom-call | flops 2147483648 | bytes 4194304 | tf_op jit(solution)/shard_map/pallas_call | solution.py:205
  55.5 0.9 %collective-permute-start.13 = (f16[528,128]{1,0:T(8,128)(2,1)S(1)}, f16[528,128]{1,0:T(8,128)(2,1)S(1)}, u32[]{:S(2)}, u32[]{:S(2)}) collective-permute-start(f16[528,128]{1,0:T(8,128)(2,1)S(1)} %convert_element_type.65), channel_id=1, source_target_pairs={{0,8},{1,9},{2,10},{3,11},{4,12},{5,13},{6,14},{7,15},{8,0},{9,1},... | collective-permute-start | bytes 405512 | tf_op jit(solution)/shard_map/ppermute | solution.py:41
  56.4 1.2 %collective-permute-start.14 = (f16[528,128]{1,0:T(8,128)(2,1)S(1)}, f16[528,128]{1,0:T(8,128)(2,1)S(1)}, u32[]{:S(2)}, u32[]{:S(2)}) collective-permute-start(f16[528,128]{1,0:T(8,128)(2,1)S(1)} %convert_element_type.67), channel_id=1, source_target_pairs={{0,1},{1,0},{2,3},{3,2},{4,5},{5,4},{6,7},{7,6},{8,9},{9,8},{10,11... | collective-permute-start | bytes 405512 | tf_op jit(solution)/shard_map/ppermute | solution.py:41
  57.5 0.1 collective-permute-start.15
  57.7 4.8 %all-to-all-done.arrived = bf16[16,64,128]{2,1,0:T(8,128)(2,1)S(1)} async-done(((bf16[16,64,128]{2,1,0:T(8,128)(2,1)}), bf16[16,64,128]{2,1,0:T(8,128)(2,1)S(1)}, u32[]{:S(2)}, u32[]{:S(2)}) %all-to-all-start) | async-done | bytes 262176 | tf_op jit(solution)/shard_map/all_to_all | solution.py:377
  62.5 0.7 %shard_map.101 = bf16[16,64,128]{2,1,0:T(8,128)(2,1)} custom-call(bf16[16,64,128]{2,1,0:T(8,128)(2,1)S(1)} %all-to-all-done.arrived), custom_call_target="tpu_custom_call" | custom-call | flops 1048576 | bytes 1048576 | tf_op jit(solution)/shard_map/pallas_call | solution.py:237
  63.2 0.0 collective-permute-done.13
  63.3 1.6 %collective-permute-done.15 = f16[528,128]{1,0:T(8,128)(2,1)S(1)} collective-permute-done((f16[528,128]{1,0:T(8,128)(2,1)S(1)}, f16[528,128]{1,0:T(8,128)(2,1)S(1)}, u32[]{:S(2)}, u32[]{:S(2)}) %collective-permute-start.15) | collective-permute-done | bytes 135200 | tf_op jit(solution)/shard_map/ppermute | solution.py:41
  64.9 0.9 %copy-done.10 = f32[512,128]{1,0:T(8,128)S(1)} copy-done((f32[512,128]{1,0:T(8,128)S(1)}, f32[512,128]{1,0:T(8,128)}, u32[]{:S(2)}) %copy-start.10) | copy-done | bytes 262168
  65.9 1.4 %shard_map.102 = bf16[512,128]{1,0:T(8,128)(2,1)} custom-call(f32[512,128]{1,0:T(8,128)S(1)} %copy-done.10, f32[16,128]{1,0:T(8,128)S(1)} %get-tuple-element.53.code, f32[528,128]{1,0:T(8,128)S(1)} %convert_element_type.68.g1, f32[528,128]{1,0:T(8,128)S(1)} %convert_element_type.66.g2, f32[528,128]{1,0:T(8,128)S(1)} %convert_element_type.70.g3, ...), custom_call_target="tpu_custom_call" | custom-call | flops 1048576 | bytes 1048576 | tf_op jit(solution)/shard_map/pallas_call | solution.py:237
  (49 shorter events, 0.4 us)
Async XLA Ops:
  0.6 14.1 %copy-start.16 = (s32[8]{0:T(128)S(1)}, s32[8]{0:T(128)}, u32[]{:S(2)}) copy-start(s32[8]{0:T(128)} %param.11) | copy-start | bytes 100
  0.6 14.3 %copy-start.15 = (s32[512]{0:T(512)S(1)}, s32[512]{0:T(512)}, u32[]{:S(2)}) copy-start(s32[512]{0:T(512)} %param.13) | copy-start | bytes 6148
  0.7 20.1 %copy-start.14 = (f32[128]{0:T(128)S(1)}, f32[128]{0:T(128)}, u32[]{:S(2)}) copy-start(f32[128]{0:T(128)} %param.15) | copy-start | bytes 1540
  0.7 17.1 %collective-permute-start = (bf16[512,512]{1,0:T(8,128)(2,1)}, bf16[512,512]{1,0:T(8,128)(2,1)S(1)}, u32[]{:S(2)}, u32[]{:S(2)}) collective-permute-start(bf16[512,512]{1,0:T(8,128)(2,1)} %r0.1), channel_id=1, source_target_pairs={{0,2},{1,3},{2,4},{3,5},{4,6},{5,7},{6,0},{7,1},{8,10},{9,11},{10,... | collective-permute-start | bytes 1572872 | tf_op jit(solution)/shard_map/ppermute | solution.py:57
  2.8 15.0 %collective-permute-start.2 = (bf16[512,512]{1,0:T(8,128)(2,1)}, bf16[512,512]{1,0:T(8,128)(2,1)S(1)}, u32[]{:S(2)}, u32[]{:S(2)}) collective-permute-start(bf16[512,512]{1,0:T(8,128)(2,1)} %r0.1), channel_id=1, source_target_pairs={{0,6},{1,7},{2,0},{3,1},{4,2},{5,3},{6,4},{7,5},{8,14},{9,15},{10,... | collective-permute-start | bytes 1572872 | tf_op jit(solution)/shard_map/ppermute | solution.py:57
  6.9 14.9 %collective-permute-start.5 = (bf16[4,512,128]{2,1,0:T(8,128)(2,1)}, bf16[4,512,128]{2,1,0:T(8,128)(2,1)S(1)}, u32[]{:S(2)}, u32[]{:S(2)}) collective-permute-start(bf16[4,512,128]{2,1,0:T(8,128)(2,1)} %get-tuple-element.33), channel_id=1, source_target_pairs={{0,8},{1,9},{2,10},{3,11},{4,12},{5,13},{6,14},{7,15},{8,0},{9,1},... | collective-permute-start | bytes 1572872 | tf_op jit(solution)/shard_map/ppermute | solution.py:41
  8.7 17.4 %collective-permute-start.6 = (bf16[4,512,128]{2,1,0:T(8,128)(2,1)}, bf16[4,512,128]{2,1,0:T(8,128)(2,1)S(1)}, u32[]{:S(2)}, u32[]{:S(2)}) collective-permute-start(bf16[4,512,128]{2,1,0:T(8,128)(2,1)} %get-tuple-element.34), channel_id=1, source_target_pairs={{0,201},{1,200},{2,203},{3,202},{4,205},{5,204},{6,207},{7,206},{8... | collective-permute-start | bytes 1572872 | tf_op jit(solution)/shard_map/ppermute | solution.py:53
  17.7 3.0 %copy-start.3 = (bf16[512,512]{1,0:T(8,128)(2,1)}, bf16[512,512]{1,0:T(8,128)(2,1)S(1)}, u32[]{:S(2)}) copy-start(bf16[512,512]{1,0:T(8,128)(2,1)S(1)} %collective-permute-done.r1) | copy-start | bytes 1572868
  17.7 3.0 %copy-start.5 = (bf16[512,512]{1,0:T(8,128)(2,1)}, bf16[512,512]{1,0:T(8,128)(2,1)S(1)}, u32[]{:S(2)}) copy-start(bf16[512,512]{1,0:T(8,128)(2,1)S(1)} %collective-permute-done.2.r3) | copy-start | bytes 1572868
  17.8 9.6 %collective-permute-start.4 = (bf16[4,512,128]{2,1,0:T(8,128)(2,1)}, bf16[4,512,128]{2,1,0:T(8,128)(2,1)S(1)}, u32[]{:S(2)}, u32[]{:S(2)}) collective-permute-start(bf16[4,512,128]{2,1,0:T(8,128)(2,1)} %get-tuple-element.32.after), channel_id=1, source_target_pairs={{0,1},{1,0},{2,3},{3,2},{4,5},{5,4},{6,7},{7,6},{8,9},{9,8},{10,11... | collective-permute-start | bytes 1572872 | tf_op jit(solution)/shard_map/ppermute | solution.py:41
  17.9 12.0 %collective-permute-start.1 = (bf16[256,512]{1,0:T(8,128)(2,1)S(1)}, bf16[256,512]{1,0:T(8,128)(2,1)S(1)}, u32[]{:S(2)}, u32[]{:S(2)}) collective-permute-start(bf16[256,512]{1,0:T(8,128)(2,1)S(1)} %slice.6), channel_id=1, source_target_pairs={{0,2},{1,3},{2,4},{3,5},{4,6},{5,7},{6,0},{7,1},{8,10},{9,11},{10,... | collective-permute-start | bytes 786440 | tf_op jit(solution)/shard_map/ppermute | solution.py:57
  18.7 11.3 %collective-permute-start.3 = (bf16[256,512]{1,0:T(8,128)(2,1)S(1)}, bf16[256,512]{1,0:T(8,128)(2,1)S(1)}, u32[]{:S(2)}, u32[]{:S(2)}) collective-permute-start(bf16[256,512]{1,0:T(8,128)(2,1)S(1)} %slice.8), channel_id=1, source_target_pairs={{0,6},{1,7},{2,0},{3,1},{4,2},{5,3},{6,4},{7,5},{8,14},{9,15},{10,... | collective-permute-start | bytes 786440 | tf_op jit(solution)/shard_map/ppermute | solution.py:57
  20.7 1.0 %copy-start.13 = (bf16[4,512,128]{2,1,0:T(8,128)(2,1)S(1)}, bf16[4,512,128]{2,1,0:T(8,128)(2,1)}, u32[]{:S(2)}) copy-start(bf16[4,512,128]{2,1,0:T(8,128)(2,1)} %get-tuple-element.32.after) | copy-start | bytes 1572868
  21.8 5.6 %copy-start = (bf16[8192,128]{1,0:T(8,128)(2,1)S(1)}, bf16[8192,128]{1,0:T(8,128)(2,1)}, u32[]{:S(2)}) copy-start(bf16[8192,128]{1,0:T(8,128)(2,1)} %param.14) | copy-start | bytes 6291460
  21.8 5.6 %copy-start.4 = (bf16[512,512]{1,0:T(8,128)(2,1)S(1)}, bf16[512,512]{1,0:T(8,128)(2,1)}, u32[]{:S(2)}) copy-start(bf16[512,512]{1,0:T(8,128)(2,1)} %copy-done.3) | copy-start | bytes 1572868
  21.8 5.6 %copy-start.6 = (bf16[512,512]{1,0:T(8,128)(2,1)S(1)}, bf16[512,512]{1,0:T(8,128)(2,1)}, u32[]{:S(2)}) copy-start(bf16[512,512]{1,0:T(8,128)(2,1)} %copy-done.5) | copy-start | bytes 1572868
  21.8 5.6 %copy-start.8 = (bf16[512,512]{1,0:T(8,128)(2,1)S(1)}, bf16[512,512]{1,0:T(8,128)(2,1)}, u32[]{:S(2)}) copy-start(bf16[512,512]{1,0:T(8,128)(2,1)} %r0.1) | copy-start | bytes 1572868
  21.8 29.3 %collective-permute-start.10 = (bf16[512,512]{1,0:T(8,128)(2,1)}, bf16[512,512]{1,0:T(8,128)(2,1)}, u32[]{:S(2)}, u32[]{:S(2)}) collective-permute-start(bf16[512,512]{1,0:T(8,128)(2,1)} %r0.2), channel_id=1, source_target_pairs={{0,2},{1,3},{2,4},{3,5},{4,6},{5,7},{6,0},{7,1},{8,10},{9,11},{10,... | collective-permute-start | bytes 1572872 | tf_op jit(solution)/shard_map/ppermute | solution.py:57
  26.1 25.1 %collective-permute-start.12 = (bf16[512,512]{1,0:T(8,128)(2,1)}, bf16[512,512]{1,0:T(8,128)(2,1)}, u32[]{:S(2)}, u32[]{:S(2)}) collective-permute-start(bf16[512,512]{1,0:T(8,128)(2,1)} %r0.2), channel_id=1, source_target_pairs={{0,6},{1,7},{2,0},{3,1},{4,2},{5,3},{6,4},{7,5},{8,14},{9,15},{10,... | collective-permute-start | bytes 1572872 | tf_op jit(solution)/shard_map/ppermute | solution.py:57
  27.4 2.6 %copy-start.1 = (bf16[4,512,128]{2,1,0:T(8,128)(2,1)}, bf16[4,512,128]{2,1,0:T(8,128)(2,1)S(1)}, u32[]{:S(2)}) copy-start(bf16[4,512,128]{2,1,0:T(8,128)(2,1)S(1)} %collective-permute-done.4.w1.refs_2_) | copy-start | bytes 1572868
  29.4 21.8 %collective-permute-start.11 = (bf16[512,512]{1,0:T(8,128)(2,1)}, bf16[512,512]{1,0:T(8,128)(2,1)}, u32[]{:S(2)}, u32[]{:S(2)}) collective-permute-start(bf16[512,512]{1,0:T(8,128)(2,1)} %r0.2), channel_id=1, source_target_pairs={{0,4},{1,5},{2,6},{3,7},{4,0},{5,1},{6,2},{7,3},{8,12},{9,13},{10,... | collective-permute-start | bytes 1572872 | tf_op jit(solution)/shard_map/ppermute | solution.py:57
  30.6 9.0 %copy-start.11 = (s32[8]{0:T(128)S(1)}, s32[8]{0:T(128)}, u32[]{:S(2)}) copy-start(s32[8]{0:T(128)} %owner.1) | copy-start | bytes 100
  30.6 9.0 %copy-start.12 = (s32[8]{0:T(128)S(1)}, s32[8]{0:T(128)}, u32[]{:S(2)}) copy-start(s32[8]{0:T(128)} %valid.1) | copy-start | bytes 100
  30.7 1.4 %collective-permute-start.7 = (f16[528,128]{1,0:T(8,128)(2,1)S(1)}, f16[528,128]{1,0:T(8,128)(2,1)S(1)}, u32[]{:S(2)}, u32[]{:S(2)}) collective-permute-start(f16[528,128]{1,0:T(8,128)(2,1)S(1)} %convert_element_type.59), channel_id=1, source_target_pairs={{0,1},{1,0},{2,3},{3,2},{4,5},{5,4},{6,7},{7,6},{8,9},{9,8},{10,11... | collective-permute-start | bytes 405512 | tf_op jit(solution)/shard_map/ppermute | solution.py:41
  30.9 5.0 %collective-permute-start.8 = (f16[528,128]{1,0:T(8,128)(2,1)S(1)}, f16[528,128]{1,0:T(8,128)(2,1)S(1)}, u32[]{:S(2)}, u32[]{:S(2)}) collective-permute-start(f16[528,128]{1,0:T(8,128)(2,1)S(1)} %convert_element_type.61), channel_id=1, source_target_pairs={{0,8},{1,9},{2,10},{3,11},{4,12},{5,13},{6,14},{7,15},{8,0},{9,1},... | collective-permute-start | bytes 405512 | tf_op jit(solution)/shard_map/ppermute | solution.py:41
  32.1 7.5 %collective-permute-start.9 = (f16[528,128]{1,0:T(8,128)(2,1)S(1)}, f16[528,128]{1,0:T(8,128)(2,1)S(1)}, u32[]{:S(2)}, u32[]{:S(2)}) collective-permute-start(f16[528,128]{1,0:T(8,128)(2,1)S(1)} %convert_element_type.63), channel_id=1, source_target_pairs={{0,9},{1,8},{2,11},{3,10},{4,13},{5,12},{6,15},{7,14},{8,1},{9,0},... | collective-permute-start | bytes 405512 | tf_op jit(solution)/shard_map/ppermute | solution.py:41
  41.7 20.8 %all-to-all-start = ((bf16[16,64,128]{2,1,0:T(8,128)(2,1)}), bf16[16,64,128]{2,1,0:T(8,128)(2,1)S(1)}, u32[]{:S(2)}, u32[]{:S(2)}) async-start(bf16[16,64,128]{2,1,0:T(8,128)(2,1)} %shard_map.99), calls=%async_computation | async-start | bytes 524288 | tf_op jit(solution)/shard_map/all_to_all | solution.py:377
  51.2 1.0 %copy-start.2 = (bf16[4,512,128]{2,1,0:T(8,128)(2,1)S(1)}, bf16[4,512,128]{2,1,0:T(8,128)(2,1)}, u32[]{:S(2)}) copy-start(bf16[4,512,128]{2,1,0:T(8,128)(2,1)} %copy-done.1) | copy-start | bytes 1572868
  55.4 2.1 %copy-start.9 = (f32[512,128]{1,0:T(8,128)}, f32[512,128]{1,0:T(8,128)S(1)}, u32[]{:S(2)}) copy-start(f32[512,128]{1,0:T(8,128)S(1)} %get-tuple-element.52.own) | copy-start | bytes 786436
  55.4 9.5 %copy-start.7 = (f32[512,128]{1,0:T(8,128)S(1)}, f32[512,128]{1,0:T(8,128)}, u32[]{:S(2)}) copy-start(f32[512,128]{1,0:T(8,128)} %get-tuple-element.57.turns) | copy-start | bytes 786436
  55.5 7.7 %collective-permute-start.13 = (f16[528,128]{1,0:T(8,128)(2,1)S(1)}, f16[528,128]{1,0:T(8,128)(2,1)S(1)}, u32[]{:S(2)}, u32[]{:S(2)}) collective-permute-start(f16[528,128]{1,0:T(8,128)(2,1)S(1)} %convert_element_type.65), channel_id=1, source_target_pairs={{0,8},{1,9},{2,10},{3,11},{4,12},{5,13},{6,14},{7,15},{8,0},{9,1},... | collective-permute-start | bytes 405512 | tf_op jit(solution)/shard_map/ppermute | solution.py:41
  56.4 6.9 %collective-permute-start.14 = (f16[528,128]{1,0:T(8,128)(2,1)S(1)}, f16[528,128]{1,0:T(8,128)(2,1)S(1)}, u32[]{:S(2)}, u32[]{:S(2)}) collective-permute-start(f16[528,128]{1,0:T(8,128)(2,1)S(1)} %convert_element_type.67), channel_id=1, source_target_pairs={{0,1},{1,0},{2,3},{3,2},{4,5},{5,4},{6,7},{7,6},{8,9},{9,8},{10,11... | collective-permute-start | bytes 405512 | tf_op jit(solution)/shard_map/ppermute | solution.py:41
  57.5 7.3 %collective-permute-start.15 = (f16[528,128]{1,0:T(8,128)(2,1)S(1)}, f16[528,128]{1,0:T(8,128)(2,1)S(1)}, u32[]{:S(2)}, u32[]{:S(2)}) collective-permute-start(f16[528,128]{1,0:T(8,128)(2,1)S(1)} %convert_element_type.69), channel_id=1, source_target_pairs={{0,9},{1,8},{2,11},{3,10},{4,13},{5,12},{6,15},{7,14},{8,1},{9,0},... | collective-permute-start | bytes 405512 | tf_op jit(solution)/shard_map/ppermute | solution.py:41
  64.9 1.0 %copy-start.10 = (f32[512,128]{1,0:T(8,128)S(1)}, f32[512,128]{1,0:T(8,128)}, u32[]{:S(2)}) copy-start(f32[512,128]{1,0:T(8,128)} %copy-done.9) | copy-start | bytes 786436

commit v6 on v5

--- a/solution.py
+++ b/solution.py
@@ -73,27 +73,37 @@
     return me // (NC * NX), lax.rem(me // NC, NX), lax.rem(me, NC)
 
 
-def slice_kernel(w, w1, w2, w3, sems):
+def slice_kernel(which, w, *refs):
     z, _, c = place()
-    copies = []
-    for e, out in ((2, w2), (3, w3), (1, w1)):
+    outs, held, sems = refs[: len(which)], refs[-2], refs[-1]
+    into, away = [], []
+    for n, (e, out) in enumerate(zip(which, outs)):
         for k in range(NX):
             src = w.at[lax.bitwise_xor(z, e // NC), k, lax.bitwise_xor(c, e % NC)]
-            copies.append(pltpu.make_async_copy(src, out.at[k], sems.at[len(copies)]))
-    for copy in copies:
+            at = n * NX + k
+            into.append(pltpu.make_async_copy(src, held.at[at], sems.at[0, at]))
+            away.append(pltpu.make_async_copy(held.at[at], out.at[k], sems.at[1, at]))
+    for copy in into:
         copy.start()
-    for copy in copies:
+    for copy, leave in zip(into, away):
         copy.wait()
-
-
-def slices(w):
+        leave.start()
+    for leave in away:
+        leave.wait()
+
+
+def slices(w, which):
     part = jax.ShapeDtypeStruct((NX,) + w.shape[3:], w.dtype)
+    count = NX * len(which)
     return pl.pallas_call(
-        slice_kernel,
-        out_shape=(part,) * 3,
-        in_specs=[pl.BlockSpec(memory_space=pl.ANY)],
-        out_specs=(VMEM,) * 3,
-        scratch_shapes=[pltpu.SemaphoreType.DMA((3 * NX,))],
+        functools.partial(slice_kernel, which),
+        out_shape=(part,) * len(which),
+        in_specs=[ANY],
+        out_specs=(ANY,) * len(which),
+        scratch_shapes=[
+            pltpu.VMEM((count,) + w.shape[3:], w.dtype),
+            pltpu.SemaphoreType.DMA((2, count)),
+        ],
         cost_estimate=pl.CostEstimate(flops=0, bytes_accessed=2**21, transcendentals=0),
     )(w)
 
@@ -338,9 +348,8 @@
 
     s1 = along_x(stored_hidden, 1)
     s3 = along_x(stored_hidden, 3)
-    parts = slices(chunks)
-    held = anchor(bias, parts[0])
-    w1, w2, w3 = parts
+    w3, w2, w1 = slices(chunks, (3, 2, 1))
+    held = anchor(bias, w3)
     w2 = across(w2, 2)
     w3 = outward(w3, groups)
     w1, _ = lax.optimization_barrier((w1, s3))
@@ -363,7 +372,7 @@
     last = functools.partial(last_kernel, 2)
     parts = multiply(last, (s2a, s2b), chunks, weights, (acc, sq), outputs(count), 16,1)
     s_own, s_code, s_sent = half_width(parts)
-    s_g1, s_g2, s_g3 = [across(v, e) for e, v in zip((1, 2, 3), s_sent)]
+    s_g2, s_g3, s_g1 = [across(s_sent[e - 1], e) for e in (2, 3, 1)]
     t_rows = [turn_hidden, t1, t2, t3]
 
     args = [v.astype(f32) for v in (s_g1, s_g2, s_g3)]
@@ -380,7 +389,8 @@
     parts = multiply(whole_kernel, t_rows, chunks, weights, (), outputs(count), 16,2)
     t_own, t_code, t_sent = half_width(parts)
     t1, t2, t3 = t_sent
-    t_got = across(t1, 1), across(t2, 2), across(t3, 3)
+    t_g2, t_g3, t_g1 = across(t2, 2), across(t3, 3), across(t1, 1)
+    t_got = t_g1, t_g2, t_g3
     args = [v.astype(f32) for v in t_got]
     shape = jax.ShapeDtypeStruct(arrived.shape, arrived.dtype)
     restored = call(emit_kernel, shape, (arrived,), 2**20)

time: 67.6 us -> 67.8 us (level)
  waiting for transfers between devices: 17.9 us -> 19 us
    ppermute x8, waiting for transfers between devices: 8.93 us -> 10.4 us  [across(): lax.ppermute(v, 'mp', pairs(lambda z, x, c: (z ^ e // NC, x, c ^ e % NC)))]
    all_to_all x1, starting transfers between devices: 9.46 us -> 8.02 us  [shards(): lax.all_to_all(outgoing, 'pool', split_axis=0, concat_axis=0, tiled=True)]
    ppermute x1, starting transfers between devices: 6.07 us -> 6.89 us  [outward(): return lax.ppermute(v, ('pool', 'mp'), moves)]
  transfers between devices with their start and end apart: 17 -> 17, of which waited for: 6 -> 7; matrix products, arithmetic and copies ran while one was open for 5% -> 5% of each run, Pallas kernels for 17% -> 16%
where the time goes in v6:
time: 67.8 us; the launch traced here: 67.4 us
  starting transfers between devices  28.8 us (42%)
  waiting for transfers between devices  19 us (28%)
  Pallas kernels  12.4 us (18%)
  local copies, waits for them, and re-layouts  3.19 us (5%)
  other arithmetic  3.11 us (5%)
  between operations  0.97 us (1%)
    ppermute x8, waiting for transfers between devices, across(): lax.ppermute(v, 'mp', pairs(lambda z, x, c: (z ^ e // NC, x, c ^ e % NC)))  10.4 us
    ppermute x7, starting transfers between devices, along_x(): return lax.ppermute(v, 'mp', pairs(lambda z, x, c: (z, (x + d) % NX, c)))  8.42 us
    all_to_all x1, starting transfers between devices, shards(): lax.all_to_all(outgoing, 'pool', split_axis=0, concat_axis=0, tiled=True)  8.02 us
    ppermute x1, starting transfers between devices, outward(): return lax.ppermute(v, ('pool', 'mp'), moves)  6.89 us
    pallas_call x3, Pallas kernels, multiply(): pl.pallas_call(body, out_shape=out, in_specs=[ANY] + [VMEM if stay else A...  5.84 us
    ppermute x8, starting transfers between devices, across(): lax.ppermute(v, 'mp', pairs(lambda z, x, c: (z ^ e // NC, x, c ^ e % NC)))  5.5 us
    all_to_all x1, waiting for transfers between devices, shards(): lax.all_to_all(outgoing, 'pool', split_axis=0, concat_axis=0, tiled=True)  4.83 us
    pallas_call x3, Pallas kernels, call(): pl.pallas_call(body, out_shape=out, in_specs=[SMEM] * scalars + [VMEM] *...  4.16 us
  transfers between devices with their start and end apart: 17, of which 7 were waited for; matrix products, arithmetic and copies ran while one was open for 5% of the time, Pallas kernels for 16%

profile of v6, /device:TPU:1, one launch (start us, length us, event | category | flops | bytes accessed | tf_op | source)
XLA Modules:
  0.0 67.4 jit_solution(3409235810293682890)
XLA Ops:
  0.7 2.1 %collective-permute-start = (bf16[512,512]{1,0:T(8,128)(2,1)}, bf16[512,512]{1,0:T(8,128)(2,1)S(1)}, u32[]{:S(2)}, u32[]{:S(2)}) collective-permute-start(bf16[512,512]{1,0:T(8,128)(2,1)} %r0.1), channel_id=1, source_target_pairs={{0,2},{1,3},{2,4},{3,5},{4,6},{5,7},{6,0},{7,1},{8,10},{9,11},{10,... | collective-permute-start | bytes 1572872 | tf_op jit(solution)/shard_map/ppermute | solution.py:57
  2.8 1.4 %collective-permute-start.2 = (bf16[512,512]{1,0:T(8,128)(2,1)}, bf16[512,512]{1,0:T(8,128)(2,1)S(1)}, u32[]{:S(2)}, u32[]{:S(2)}) collective-permute-start(bf16[512,512]{1,0:T(8,128)(2,1)} %r0.1), channel_id=1, source_target_pairs={{0,6},{1,7},{2,0},{3,1},{4,2},{5,3},{6,4},{7,5},{8,14},{9,15},{10,... | collective-permute-start | bytes 1572872 | tf_op jit(solution)/shard_map/ppermute | solution.py:57
  4.1 2.4 %shard_map.95 = (bf16[4,512,128]{2,1,0:T(8,128)(2,1)}, bf16[4,512,128]{2,1,0:T(8,128)(2,1)}, bf16[4,512,128]{2,1,0:T(8,128)(2,1)}) custom-call(bf16[2,4,2,512,128]{4,3,2,1,0:T(8,128)(2,1)} %bitcast.3), custom_call_target="tpu_custom_call" | custom-call | bytes 2097152 | tf_op jit(solution)/shard_map/pallas_call | solution.py:98
  6.5 6.9 %collective-permute-start.6 = (bf16[4,512,128]{2,1,0:T(8,128)(2,1)}, bf16[4,512,128]{2,1,0:T(8,128)(2,1)S(1)}, u32[]{:S(2)}, u32[]{:S(2)}) collective-permute-start(bf16[4,512,128]{2,1,0:T(8,128)(2,1)} %get-tuple-element.34.after), channel_id=1, source_target_pairs={{0,201},{1,200},{2,203},{3,202},{4,205},{5,204},{6,207},{7,206},{8... | collective-permute-start | bytes 1572872 | tf_op jit(solution)/shard_map/ppermute | solution.py:53
  13.4 0.0 collective-permute-start.5
  13.4 0.1 add_convert_fusion
  13.5 0.1 convert_element_type.56
  13.6 0.1 pad_maximum_fusion
  13.7 2.7 %fusion.3 = (f32[512,128]{1,0:T(8,128)}, f32[512,128]{1,0:T(8,128)S(1)}) fusion(f32[512]{0:T(512)S(1)} %convert_element_type.58, f32[128]{0:T(128)S(1)} %get-tuple-element.61, f32[128]{0:T(128)S(1)} %get-tuple-element.60, pred[128]{0:T(512)(128)(4,1)S(1)} %iota_compare_fusion, pred[]{:T(512)S(6)} %lt.20, f32[512]{0:T(512)S(1)} %convert_element_type.56), kind=kLoop, calls=%fused_computation.7 | loop fusion | flops 393216 | bytes 529537 | tf_op jit(solution)/shard_map/jit(_where)/select_n | solution.py:324
  16.4 0.0 collective-permute-done.r1
  16.4 0.0 collective-permute-done.2.r3
  16.4 0.9 %collective-permute-start.4 = (bf16[4,512,128]{2,1,0:T(8,128)(2,1)}, bf16[4,512,128]{2,1,0:T(8,128)(2,1)S(1)}, u32[]{:S(2)}, u32[]{:S(2)}) collective-permute-start(bf16[4,512,128]{2,1,0:T(8,128)(2,1)} %get-tuple-element.32), channel_id=1, source_target_pairs={{0,1},{1,0},{2,3},{3,2},{4,5},{5,4},{6,7},{7,6},{8,9},{9,8},{10,11... | collective-permute-start | bytes 1572872 | tf_op jit(solution)/shard_map/ppermute | solution.py:41
  17.4 1.3 %collective-permute-start.1 = (bf16[256,512]{1,0:T(8,128)(2,1)S(1)}, bf16[256,512]{1,0:T(8,128)(2,1)S(1)}, u32[]{:S(2)}, u32[]{:S(2)}) collective-permute-start(bf16[256,512]{1,0:T(8,128)(2,1)S(1)} %slice.6), channel_id=1, source_target_pairs={{0,2},{1,3},{2,4},{3,5},{4,6},{5,7},{6,0},{7,1},{8,10},{9,11},{10,... | collective-permute-start | bytes 786440 | tf_op jit(solution)/shard_map/ppermute | solution.py:57
  18.7 1.5 %collective-permute-start.3 = (bf16[256,512]{1,0:T(8,128)(2,1)S(1)}, bf16[256,512]{1,0:T(8,128)(2,1)S(1)}, u32[]{:S(2)}, u32[]{:S(2)}) collective-permute-start(bf16[256,512]{1,0:T(8,128)(2,1)S(1)} %slice.8), channel_id=1, source_target_pairs={{0,6},{1,7},{2,0},{3,1},{4,2},{5,3},{6,4},{7,5},{8,14},{9,15},{10,... | collective-permute-start | bytes 786440 | tf_op jit(solution)/shard_map/ppermute | solution.py:57
  20.2 1.0 %copy-done.13 = bf16[4,512,128]{2,1,0:T(8,128)(2,1)S(1)} copy-done((bf16[4,512,128]{2,1,0:T(8,128)(2,1)S(1)}, bf16[4,512,128]{2,1,0:T(8,128)(2,1)}, u32[]{:S(2)}) %copy-start.13) | copy-done | bytes 524312
  21.3 3.7 %collective-permute-done.6.w3.refs_4_ = bf16[4,512,128]{2,1,0:T(8,128)(2,1)S(1)} collective-permute-done((bf16[4,512,128]{2,1,0:T(8,128)(2,1)}, bf16[4,512,128]{2,1,0:T(8,128)(2,1)S(1)}, u32[]{:S(2)}, u32[]{:S(2)}) %collective-permute-start.6) | collective-permute-done | bytes 524320 | tf_op jit(solution)/shard_map/ppermute | solution.py:53
  25.0 0.0 collective-permute-start.10
  25.0 2.1 %collective-permute-done.5.w2.refs_3_ = bf16[4,512,128]{2,1,0:T(8,128)(2,1)S(1)} collective-permute-done((bf16[4,512,128]{2,1,0:T(8,128)(2,1)}, bf16[4,512,128]{2,1,0:T(8,128)(2,1)S(1)}, u32[]{:S(2)}, u32[]{:S(2)}) %collective-permute-start.5) | collective-permute-done | bytes 524320 | tf_op jit(solution)/shard_map/ppermute | solution.py:41
  27.1 1.5 %collective-permute-start.12 = (bf16[512,512]{1,0:T(8,128)(2,1)}, bf16[512,512]{1,0:T(8,128)(2,1)}, u32[]{:S(2)}, u32[]{:S(2)}) collective-permute-start(bf16[512,512]{1,0:T(8,128)(2,1)} %r0.2), channel_id=1, source_target_pairs={{0,6},{1,7},{2,0},{3,1},{4,2},{5,3},{6,4},{7,5},{8,14},{9,15},{10,... | collective-permute-start | bytes 1572872 | tf_op jit(solution)/shard_map/ppermute | solution.py:57
  28.6 0.0 collective-permute-done.4.w1.refs_2_
  28.6 2.0 %shard_map.97 = (f32[512,512]{1,0:T(8,128)S(1)}, f32[512,128]{1,0:T(8,128)S(1)}) custom-call(bf16[2,4,2,512,128]{4,3,2,1,0:T(8,128)(2,1)S(1)} %bitcast.4, bf16[512,512]{1,0:T(8,128)(2,1)S(1)} %copy-done.8, bf16[512,512]{1,0:T(8,128)(2,1)S(1)} %copy-done.4, bf16[512,512]{1,0:T(8,128)(2,1)S(1)} %copy-done.6, ...), custom_call_target="tpu_custom_call" | custom-call | flops 1073741824 | bytes 4194304 | tf_op jit(solution)/shard_map/pallas_call | solution.py:215
  30.6 0.6 collective-permute-start.11
  31.2 0.0 collective-permute-done.1.refs_0_
  31.2 0.0 collective-permute-done.3.refs_1_
  31.2 0.7 %shard_map.98 = (f32[512,128]{1,0:T(8,128)S(1)}, f32[528,128]{1,0:T(8,128)S(1)}, f32[528,128]{1,0:T(8,128)S(1)}, f32[528,128]{1,0:T(8,128)S(1)}, f32[16,128]{1,0:T(8,128)S(1)}) custom-call(bf16[2,4,2,512,128]{4,3,2,1,0:T(8,128)(2,1)S(1)} %bitcast.5, bf16[256,512]{1,0:T(8,128)(2,1)S(1)} %collective-permute-done.1.refs_0_, ...), custom_call_target="tpu_custom_call" | custom-call | flops 1073741824 | bytes 4194304 | tf_op jit(solution)/shard_map/pallas_call | solution.py:215
  31.9 0.0 copy-start.11
  31.9 0.0 copy-start.12
  32.0 0.8 %collective-permute-start.7 = (f16[528,128]{1,0:T(8,128)(2,1)S(1)}, f16[528,128]{1,0:T(8,128)(2,1)S(1)}, u32[]{:S(2)}, u32[]{:S(2)}) collective-permute-start(f16[528,128]{1,0:T(8,128)(2,1)S(1)} %convert_element_type.59), channel_id=1, source_target_pairs={{0,1},{1,0},{2,3},{3,2},{4,5},{5,4},{6,7},{7,6},{8,9},{9,8},{10,11... | collective-permute-start | bytes 405512 | tf_op jit(solution)/shard_map/ppermute | solution.py:41
  32.8 0.1 collective-permute-start.8
  32.9 0.8 %collective-permute-done.7 = f16[528,128]{1,0:T(8,128)(2,1)S(1)} collective-permute-done((f16[528,128]{1,0:T(8,128)(2,1)S(1)}, f16[528,128]{1,0:T(8,128)(2,1)S(1)}, u32[]{:S(2)}, u32[]{:S(2)}) %collective-permute-start.7) | collective-permute-done | bytes 135200 | tf_op jit(solution)/shard_map/ppermute | solution.py:41
  33.8 1.1 %collective-permute-start.9 = (f16[528,128]{1,0:T(8,128)(2,1)S(1)}, f16[528,128]{1,0:T(8,128)(2,1)S(1)}, u32[]{:S(2)}, u32[]{:S(2)}) collective-permute-start(f16[528,128]{1,0:T(8,128)(2,1)S(1)} %convert_element_type.63), channel_id=1, source_target_pairs={{0,9},{1,8},{2,11},{3,10},{4,13},{5,12},{6,15},{7,14},{8,1},{9,0},... | collective-permute-start | bytes 405512 | tf_op jit(solution)/shard_map/ppermute | solution.py:41
  34.8 3.3 %collective-permute-done.8 = f16[528,128]{1,0:T(8,128)(2,1)S(1)} collective-permute-done((f16[528,128]{1,0:T(8,128)(2,1)S(1)}, f16[528,128]{1,0:T(8,128)(2,1)S(1)}, u32[]{:S(2)}, u32[]{:S(2)}) %collective-permute-start.8) | collective-permute-done | bytes 135200 | tf_op jit(solution)/shard_map/ppermute | solution.py:41
  38.2 3.3 %collective-permute-done.9 = f16[528,128]{1,0:T(8,128)(2,1)S(1)} collective-permute-done((f16[528,128]{1,0:T(8,128)(2,1)S(1)}, f16[528,128]{1,0:T(8,128)(2,1)S(1)}, u32[]{:S(2)}, u32[]{:S(2)}) %collective-permute-start.9) | collective-permute-done | bytes 135200 | tf_op jit(solution)/shard_map/ppermute | solution.py:41
  41.5 2.0 %shard_map.99 = bf16[16,64,128]{2,1,0:T(8,128)(2,1)} custom-call(s32[8]{0:T(128)S(1)} %copy-done.11, s32[8]{0:T(128)S(1)} %copy-done.12, f32[512,128]{1,0:T(8,128)S(1)} %get-tuple-element.40.own, f32[16,128]{1,0:T(8,128)S(1)} %get-tuple-element.41.code, f32[528,128]{1,0:T(8,128)S(1)} %convert_element_type.60.g1, f32[528,128]{1,0:T(8,128)S(1)} %convert_element_type.62.g2, ...), custom_call_target="tpu_custom_call" | custom-call | flops 1048576 | bytes 1048576 | tf_op jit(solution)/shard_map/pallas_call | solution.py:247
  43.5 8.0 %all-to-all-start = ((bf16[16,64,128]{2,1,0:T(8,128)(2,1)}), bf16[16,64,128]{2,1,0:T(8,128)(2,1)S(1)}, u32[]{:S(2)}, u32[]{:S(2)}) async-start(bf16[16,64,128]{2,1,0:T(8,128)(2,1)} %shard_map.99), calls=%async_computation | async-start | bytes 524288 | tf_op jit(solution)/shard_map/all_to_all | solution.py:386
  51.6 0.0 collective-permute-done.10.r1
  51.6 0.0 collective-permute-done.12.r3
  51.6 0.0 collective-permute-done.11.r2
  51.6 1.0 %copy-done.2 = bf16[4,512,128]{2,1,0:T(8,128)(2,1)S(1)} copy-done((bf16[4,512,128]{2,1,0:T(8,128)(2,1)S(1)}, bf16[4,512,128]{2,1,0:T(8,128)(2,1)}, u32[]{:S(2)}) %copy-start.2) | copy-done | bytes 524312
  52.6 3.2 %shard_map.100 = (f32[512,128]{1,0:T(8,128)S(1)}, f32[528,128]{1,0:T(8,128)S(1)}, f32[528,128]{1,0:T(8,128)S(1)}, f32[528,128]{1,0:T(8,128)S(1)}, f32[16,128]{1,0:T(8,128)S(1)}) custom-call(bf16[2,4,2,512,128]{4,3,2,1,0:T(8,128)(2,1)S(1)} %bitcast.6, bf16[512,512]{1,0:T(8,128)(2,1)} %r0.2, bf16[512,512]{1,0:T(8,128)(2,1)} %collective-permute-done.10.r1, ...), custom_call_target="tpu_custom_call" | custom-call | flops 2147483648 | bytes 4194304 | tf_op jit(solution)/shard_map/pallas_call | solution.py:215
  55.9 0.5 collective-permute-start.13
  56.4 1.2 %collective-permute-start.14 = (f16[528,128]{1,0:T(8,128)(2,1)S(1)}, f16[528,128]{1,0:T(8,128)(2,1)S(1)}, u32[]{:S(2)}, u32[]{:S(2)}) collective-permute-start(f16[528,128]{1,0:T(8,128)(2,1)S(1)} %convert_element_type.67), channel_id=1, source_target_pairs={{0,1},{1,0},{2,3},{3,2},{4,5},{5,4},{6,7},{7,6},{8,9},{9,8},{10,11... | collective-permute-start | bytes 405512 | tf_op jit(solution)/shard_map/ppermute | solution.py:41
  57.5 1.0 %collective-permute-start.15 = (f16[528,128]{1,0:T(8,128)(2,1)S(1)}, f16[528,128]{1,0:T(8,128)(2,1)S(1)}, u32[]{:S(2)}, u32[]{:S(2)}) collective-permute-start(f16[528,128]{1,0:T(8,128)(2,1)S(1)} %convert_element_type.69), channel_id=1, source_target_pairs={{0,9},{1,8},{2,11},{3,10},{4,13},{5,12},{6,15},{7,14},{8,1},{9,0},... | collective-permute-start | bytes 405512 | tf_op jit(solution)/shard_map/ppermute | solution.py:41
  58.5 4.8 %all-to-all-done.arrived = bf16[16,64,128]{2,1,0:T(8,128)(2,1)S(1)} async-done(((bf16[16,64,128]{2,1,0:T(8,128)(2,1)}), bf16[16,64,128]{2,1,0:T(8,128)(2,1)S(1)}, u32[]{:S(2)}, u32[]{:S(2)}) %all-to-all-start) | async-done | bytes 262176 | tf_op jit(solution)/shard_map/all_to_all | solution.py:386
  63.4 0.7 %shard_map.101 = bf16[16,64,128]{2,1,0:T(8,128)(2,1)} custom-call(bf16[16,64,128]{2,1,0:T(8,128)(2,1)S(1)} %all-to-all-done.arrived), custom_call_target="tpu_custom_call" | custom-call | flops 1048576 | bytes 1048576 | tf_op jit(solution)/shard_map/pallas_call | solution.py:247
  64.2 0.9 %collective-permute-done.15 = f16[528,128]{1,0:T(8,128)(2,1)S(1)} collective-permute-done((f16[528,128]{1,0:T(8,128)(2,1)S(1)}, f16[528,128]{1,0:T(8,128)(2,1)S(1)}, u32[]{:S(2)}, u32[]{:S(2)}) %collective-permute-start.15) | collective-permute-done | bytes 135200 | tf_op jit(solution)/shard_map/ppermute | solution.py:41
  65.1 0.9 %copy-done.10 = f32[512,128]{1,0:T(8,128)S(1)} copy-done((f32[512,128]{1,0:T(8,128)S(1)}, f32[512,128]{1,0:T(8,128)}, u32[]{:S(2)}) %copy-start.10) | copy-done | bytes 262168
  66.0 1.4 %shard_map.102 = bf16[512,128]{1,0:T(8,128)(2,1)} custom-call(f32[512,128]{1,0:T(8,128)S(1)} %copy-done.10, f32[16,128]{1,0:T(8,128)S(1)} %get-tuple-element.53.code, f32[528,128]{1,0:T(8,128)S(1)} %convert_element_type.68.g1, f32[528,128]{1,0:T(8,128)S(1)} %convert_element_type.66.g2, f32[528,128]{1,0:T(8,128)S(1)} %convert_element_type.70.g3, ...), custom_call_target="tpu_custom_call" | custom-call | flops 1048576 | bytes 1048576 | tf_op jit(solution)/shard_map/pallas_call | solution.py:247
  (49 shorter events, 0.4 us)
Async XLA Ops:
  0.6 12.8 %copy-start.16 = (s32[8]{0:T(128)S(1)}, s32[8]{0:T(128)}, u32[]{:S(2)}) copy-start(s32[8]{0:T(128)} %param.11) | copy-start | bytes 100
  0.6 12.9 %copy-start.15 = (s32[512]{0:T(512)S(1)}, s32[512]{0:T(512)}, u32[]{:S(2)}) copy-start(s32[512]{0:T(512)} %param.13) | copy-start | bytes 6148
  0.7 19.6 %copy-start.14 = (f32[128]{0:T(128)S(1)}, f32[128]{0:T(128)}, u32[]{:S(2)}) copy-start(f32[128]{0:T(128)} %param.15) | copy-start | bytes 1540
  0.7 15.7 %collective-permute-start = (bf16[512,512]{1,0:T(8,128)(2,1)}, bf16[512,512]{1,0:T(8,128)(2,1)S(1)}, u32[]{:S(2)}, u32[]{:S(2)}) collective-permute-start(bf16[512,512]{1,0:T(8,128)(2,1)} %r0.1), channel_id=1, source_target_pairs={{0,2},{1,3},{2,4},{3,5},{4,6},{5,7},{6,0},{7,1},{8,10},{9,11},{10,... | collective-permute-start | bytes 1572872 | tf_op jit(solution)/shard_map/ppermute | solution.py:57
  2.8 13.6 %collective-permute-start.2 = (bf16[512,512]{1,0:T(8,128)(2,1)}, bf16[512,512]{1,0:T(8,128)(2,1)S(1)}, u32[]{:S(2)}, u32[]{:S(2)}) collective-permute-start(bf16[512,512]{1,0:T(8,128)(2,1)} %r0.1), channel_id=1, source_target_pairs={{0,6},{1,7},{2,0},{3,1},{4,2},{5,3},{6,4},{7,5},{8,14},{9,15},{10,... | collective-permute-start | bytes 1572872 | tf_op jit(solution)/shard_map/ppermute | solution.py:57
  6.5 18.5 %collective-permute-start.6 = (bf16[4,512,128]{2,1,0:T(8,128)(2,1)}, bf16[4,512,128]{2,1,0:T(8,128)(2,1)S(1)}, u32[]{:S(2)}, u32[]{:S(2)}) collective-permute-start(bf16[4,512,128]{2,1,0:T(8,128)(2,1)} %get-tuple-element.34.after), channel_id=1, source_target_pairs={{0,201},{1,200},{2,203},{3,202},{4,205},{5,204},{6,207},{7,206},{8... | collective-permute-start | bytes 1572872 | tf_op jit(solution)/shard_map/ppermute | solution.py:53
  13.4 13.7 %collective-permute-start.5 = (bf16[4,512,128]{2,1,0:T(8,128)(2,1)}, bf16[4,512,128]{2,1,0:T(8,128)(2,1)S(1)}, u32[]{:S(2)}, u32[]{:S(2)}) collective-permute-start(bf16[4,512,128]{2,1,0:T(8,128)(2,1)} %get-tuple-element.33), channel_id=1, source_target_pairs={{0,8},{1,9},{2,10},{3,11},{4,12},{5,13},{6,14},{7,15},{8,0},{9,1},... | collective-permute-start | bytes 1572872 | tf_op jit(solution)/shard_map/ppermute | solution.py:41
  16.4 3.8 %copy-start.3 = (bf16[512,512]{1,0:T(8,128)(2,1)}, bf16[512,512]{1,0:T(8,128)(2,1)S(1)}, u32[]{:S(2)}) copy-start(bf16[512,512]{1,0:T(8,128)(2,1)S(1)} %collective-permute-done.r1) | copy-start | bytes 1572868
  16.4 3.8 %copy-start.5 = (bf16[512,512]{1,0:T(8,128)(2,1)}, bf16[512,512]{1,0:T(8,128)(2,1)S(1)}, u32[]{:S(2)}) copy-start(bf16[512,512]{1,0:T(8,128)(2,1)S(1)} %collective-permute-done.2.r3) | copy-start | bytes 1572868
  16.4 12.2 %collective-permute-start.4 = (bf16[4,512,128]{2,1,0:T(8,128)(2,1)}, bf16[4,512,128]{2,1,0:T(8,128)(2,1)S(1)}, u32[]{:S(2)}, u32[]{:S(2)}) collective-permute-start(bf16[4,512,128]{2,1,0:T(8,128)(2,1)} %get-tuple-element.32), channel_id=1, source_target_pairs={{0,1},{1,0},{2,3},{3,2},{4,5},{5,4},{6,7},{7,6},{8,9},{9,8},{10,11... | collective-permute-start | bytes 1572872 | tf_op jit(solution)/shard_map/ppermute | solution.py:41
  17.4 13.9 %collective-permute-start.1 = (bf16[256,512]{1,0:T(8,128)(2,1)S(1)}, bf16[256,512]{1,0:T(8,128)(2,1)S(1)}, u32[]{:S(2)}, u32[]{:S(2)}) collective-permute-start(bf16[256,512]{1,0:T(8,128)(2,1)S(1)} %slice.6), channel_id=1, source_target_pairs={{0,2},{1,3},{2,4},{3,5},{4,6},{5,7},{6,0},{7,1},{8,10},{9,11},{10,... | collective-permute-start | bytes 786440 | tf_op jit(solution)/shard_map/ppermute | solution.py:57
  18.7 12.6 %collective-permute-start.3 = (bf16[256,512]{1,0:T(8,128)(2,1)S(1)}, bf16[256,512]{1,0:T(8,128)(2,1)S(1)}, u32[]{:S(2)}, u32[]{:S(2)}) collective-permute-start(bf16[256,512]{1,0:T(8,128)(2,1)S(1)} %slice.8), channel_id=1, source_target_pairs={{0,6},{1,7},{2,0},{3,1},{4,2},{5,3},{6,4},{7,5},{8,14},{9,15},{10,... | collective-permute-start | bytes 786440 | tf_op jit(solution)/shard_map/ppermute | solution.py:57
  20.2 1.0 %copy-start.13 = (bf16[4,512,128]{2,1,0:T(8,128)(2,1)S(1)}, bf16[4,512,128]{2,1,0:T(8,128)(2,1)}, u32[]{:S(2)}) copy-start(bf16[4,512,128]{2,1,0:T(8,128)(2,1)} %get-tuple-element.34.after) | copy-start | bytes 1572868
  21.3 7.3 %copy-start = (bf16[8192,128]{1,0:T(8,128)(2,1)S(1)}, bf16[8192,128]{1,0:T(8,128)(2,1)}, u32[]{:S(2)}) copy-start(bf16[8192,128]{1,0:T(8,128)(2,1)} %param.14) | copy-start | bytes 6291460
  21.3 7.3 %copy-start.4 = (bf16[512,512]{1,0:T(8,128)(2,1)S(1)}, bf16[512,512]{1,0:T(8,128)(2,1)}, u32[]{:S(2)}) copy-start(bf16[512,512]{1,0:T(8,128)(2,1)} %copy-done.3) | copy-start | bytes 1572868
  21.3 7.3 %copy-start.6 = (bf16[512,512]{1,0:T(8,128)(2,1)S(1)}, bf16[512,512]{1,0:T(8,128)(2,1)}, u32[]{:S(2)}) copy-start(bf16[512,512]{1,0:T(8,128)(2,1)} %copy-done.5) | copy-start | bytes 1572868
  21.3 7.3 %copy-start.8 = (bf16[512,512]{1,0:T(8,128)(2,1)S(1)}, bf16[512,512]{1,0:T(8,128)(2,1)}, u32[]{:S(2)}) copy-start(bf16[512,512]{1,0:T(8,128)(2,1)} %r0.1) | copy-start | bytes 1572868
  25.0 26.6 %collective-permute-start.10 = (bf16[512,512]{1,0:T(8,128)(2,1)}, bf16[512,512]{1,0:T(8,128)(2,1)}, u32[]{:S(2)}, u32[]{:S(2)}) collective-permute-start(bf16[512,512]{1,0:T(8,128)(2,1)} %r0.2), channel_id=1, source_target_pairs={{0,2},{1,3},{2,4},{3,5},{4,6},{5,7},{6,0},{7,1},{8,10},{9,11},{10,... | collective-permute-start | bytes 1572872 | tf_op jit(solution)/shard_map/ppermute | solution.py:57
  27.1 24.5 %collective-permute-start.12 = (bf16[512,512]{1,0:T(8,128)(2,1)}, bf16[512,512]{1,0:T(8,128)(2,1)}, u32[]{:S(2)}, u32[]{:S(2)}) collective-permute-start(bf16[512,512]{1,0:T(8,128)(2,1)} %r0.2), channel_id=1, source_target_pairs={{0,6},{1,7},{2,0},{3,1},{4,2},{5,3},{6,4},{7,5},{8,14},{9,15},{10,... | collective-permute-start | bytes 1572872 | tf_op jit(solution)/shard_map/ppermute | solution.py:57
  28.6 2.6 %copy-start.1 = (bf16[4,512,128]{2,1,0:T(8,128)(2,1)}, bf16[4,512,128]{2,1,0:T(8,128)(2,1)S(1)}, u32[]{:S(2)}) copy-start(bf16[4,512,128]{2,1,0:T(8,128)(2,1)S(1)} %collective-permute-done.4.w1.refs_2_) | copy-start | bytes 1572868
  30.6 21.0 %collective-permute-start.11 = (bf16[512,512]{1,0:T(8,128)(2,1)}, bf16[512,512]{1,0:T(8,128)(2,1)}, u32[]{:S(2)}, u32[]{:S(2)}) collective-permute-start(bf16[512,512]{1,0:T(8,128)(2,1)} %r0.2), channel_id=1, source_target_pairs={{0,4},{1,5},{2,6},{3,7},{4,0},{5,1},{6,2},{7,3},{8,12},{9,13},{10,... | collective-permute-start | bytes 1572872 | tf_op jit(solution)/shard_map/ppermute | solution.py:57
  31.9 9.6 %copy-start.11 = (s32[8]{0:T(128)S(1)}, s32[8]{0:T(128)}, u32[]{:S(2)}) copy-start(s32[8]{0:T(128)} %owner.1) | copy-start | bytes 100
  31.9 9.6 %copy-start.12 = (s32[8]{0:T(128)S(1)}, s32[8]{0:T(128)}, u32[]{:S(2)}) copy-start(s32[8]{0:T(128)} %valid.1) | copy-start | bytes 100
  32.0 1.8 %collective-permute-start.7 = (f16[528,128]{1,0:T(8,128)(2,1)S(1)}, f16[528,128]{1,0:T(8,128)(2,1)S(1)}, u32[]{:S(2)}, u32[]{:S(2)}) collective-permute-start(f16[528,128]{1,0:T(8,128)(2,1)S(1)} %convert_element_type.59), channel_id=1, source_target_pairs={{0,1},{1,0},{2,3},{3,2},{4,5},{5,4},{6,7},{7,6},{8,9},{9,8},{10,11... | collective-permute-start | bytes 405512 | tf_op jit(solution)/shard_map/ppermute | solution.py:41
  32.8 5.4 %collective-permute-start.8 = (f16[528,128]{1,0:T(8,128)(2,1)S(1)}, f16[528,128]{1,0:T(8,128)(2,1)S(1)}, u32[]{:S(2)}, u32[]{:S(2)}) collective-permute-start(f16[528,128]{1,0:T(8,128)(2,1)S(1)} %convert_element_type.61), channel_id=1, source_target_pairs={{0,8},{1,9},{2,10},{3,11},{4,12},{5,13},{6,14},{7,15},{8,0},{9,1},... | collective-permute-start | bytes 405512 | tf_op jit(solution)/shard_map/ppermute | solution.py:41
  33.8 7.7 %collective-permute-start.9 = (f16[528,128]{1,0:T(8,128)(2,1)S(1)}, f16[528,128]{1,0:T(8,128)(2,1)S(1)}, u32[]{:S(2)}, u32[]{:S(2)}) collective-permute-start(f16[528,128]{1,0:T(8,128)(2,1)S(1)} %convert_element_type.63), channel_id=1, source_target_pairs={{0,9},{1,8},{2,11},{3,10},{4,13},{5,12},{6,15},{7,14},{8,1},{9,0},... | collective-permute-start | bytes 405512 | tf_op jit(solution)/shard_map/ppermute | solution.py:41
  43.5 19.8 %all-to-all-start = ((bf16[16,64,128]{2,1,0:T(8,128)(2,1)}), bf16[16,64,128]{2,1,0:T(8,128)(2,1)S(1)}, u32[]{:S(2)}, u32[]{:S(2)}) async-start(bf16[16,64,128]{2,1,0:T(8,128)(2,1)} %shard_map.99), calls=%async_computation | async-start | bytes 524288 | tf_op jit(solution)/shard_map/all_to_all | solution.py:386
  51.6 1.0 %copy-start.2 = (bf16[4,512,128]{2,1,0:T(8,128)(2,1)S(1)}, bf16[4,512,128]{2,1,0:T(8,128)(2,1)}, u32[]{:S(2)}) copy-start(bf16[4,512,128]{2,1,0:T(8,128)(2,1)} %copy-done.1) | copy-start | bytes 1572868
  55.8 1.7 %copy-start.9 = (f32[512,128]{1,0:T(8,128)}, f32[512,128]{1,0:T(8,128)S(1)}, u32[]{:S(2)}) copy-start(f32[512,128]{1,0:T(8,128)S(1)} %get-tuple-element.52.own) | copy-start | bytes 786436
  55.8 9.2 %copy-start.7 = (f32[512,128]{1,0:T(8,128)S(1)}, f32[512,128]{1,0:T(8,128)}, u32[]{:S(2)}) copy-start(f32[512,128]{1,0:T(8,128)} %get-tuple-element.57.turns) | copy-start | bytes 786436
  55.9 8.2 %collective-permute-start.13 = (f16[528,128]{1,0:T(8,128)(2,1)S(1)}, f16[528,128]{1,0:T(8,128)(2,1)S(1)}, u32[]{:S(2)}, u32[]{:S(2)}) collective-permute-start(f16[528,128]{1,0:T(8,128)(2,1)S(1)} %convert_element_type.65), channel_id=1, source_target_pairs={{0,8},{1,9},{2,10},{3,11},{4,12},{5,13},{6,14},{7,15},{8,0},{9,1},... | collective-permute-start | bytes 405512 | tf_op jit(solution)/shard_map/ppermute | solution.py:41
  56.4 7.8 %collective-permute-start.14 = (f16[528,128]{1,0:T(8,128)(2,1)S(1)}, f16[528,128]{1,0:T(8,128)(2,1)S(1)}, u32[]{:S(2)}, u32[]{:S(2)}) collective-permute-start(f16[528,128]{1,0:T(8,128)(2,1)S(1)} %convert_element_type.67), channel_id=1, source_target_pairs={{0,1},{1,0},{2,3},{3,2},{4,5},{5,4},{6,7},{7,6},{8,9},{9,8},{10,11... | collective-permute-start | bytes 405512 | tf_op jit(solution)/shard_map/ppermute | solution.py:41
  57.5 7.5 %collective-permute-start.15 = (f16[528,128]{1,0:T(8,128)(2,1)S(1)}, f16[528,128]{1,0:T(8,128)(2,1)S(1)}, u32[]{:S(2)}, u32[]{:S(2)}) collective-permute-start(f16[528,128]{1,0:T(8,128)(2,1)S(1)} %convert_element_type.69), channel_id=1, source_target_pairs={{0,9},{1,8},{2,11},{3,10},{4,13},{5,12},{6,15},{7,14},{8,1},{9,0},... | collective-permute-start | bytes 405512 | tf_op jit(solution)/shard_map/ppermute | solution.py:41
  65.1 1.0 %copy-start.10 = (f32[512,128]{1,0:T(8,128)S(1)}, f32[512,128]{1,0:T(8,128)}, u32[]{:S(2)}) copy-start(f32[512,128]{1,0:T(8,128)} %copy-done.9) | copy-start | bytes 786436
